TPU v7x, 128 devices: a whole 4x4x4 slice. The times are simulated.
128 devices in a mesh: pw: 32 (over z_hi, y, x), band: 4 (over z_lo, core).
Axes of the slice: x: 4, y: 4, z: 4 (z_hi: 2, z_lo: 2; z = z_hi * 2 + z_lo), core: 2. Of those that a mesh axis runs over, the one named last changes fastest.
Arguments:
- wave_coef: float32 [2, 4, 524288], P(None, 'band', 'pw'), may hold values from -6 to 6
- projector: float32 [2, 64, 524288], P(None, None, 'pw'), may hold values from -0.109375 to 0.109375
- potential: float32 [256, 256, 256], P('pw'), may hold values from -8 to 8
- grid_slot: int32 [524288], P('pw'), may hold values from 0 to 98303, as said below
- stick_column: int32 [12288], replicated, may hold values from 0 to 65535, as said below
- proj_atom: int32 [64], replicated, may hold values from 0 to 15, never falling along the last dimension, each value on 1 to 8 neighbouring positions
- coupling: float32 [64, 64], replicated, may hold values from -6 to 6
Outputs:
- applied: float32 [2, 4, 524288], P(None, 'band', 'pw')
- subspace_h: float32 [2, 4, 4], P(None, None, 'band')
- correlation: float32 [2, 4, 4], P(None, None, 'band')
Inputs may be any that keep to these rules, and one draw needn't show every extreme that they name: `grid_slot`: within each aligned block of 16384 entries (the coefficients of one pw index) the values are distinct. `stick_column`: all values are distinct. `proj_atom`: never falling; each atom has 1 to 8 projectors.
All inputs are finite; a program needn't handle non-finite values.
Results may differ from a plain program's by a relative error of at most 0.000058.
Values sent between devices are 32-bit elements; how exact they have to be, the bound alone decides.
No kernel may reach another device: no remote copies, remote signals or barrier semaphores. Data moves between devices by JAX's collectives and lax.ppermute only.
A program may use at most 192 MiB of HBM per device.

v0:
```python
import jax
import jax.numpy as jnp
from jax import lax
from jax.sharding import PartitionSpec as P

GX = 256
GY = 256
GZ = 256


KIN_MAX = 2.0
PRECISE = lax.Precision.HIGHEST


def centred(values, length):
    return jnp.where(values < length // 2, values, values - length)


def kinetic_of(x_cell, y_cell, z_cell):
    x_freq = centred(x_cell, GX).astype(jnp.float32) / (GX / 2)
    y_freq = centred(y_cell, GY).astype(jnp.float32) / (GY / 2)
    z_freq = centred(z_cell, GZ).astype(jnp.float32) / (GZ / 2)
    return KIN_MAX * (x_freq * x_freq + y_freq * y_freq + z_freq * z_freq) / 3.0


def dft_table(source, target, length, sign_of):
    phases = source[:, None] * target[None, :] % length
    angles = phases.astype(jnp.float32) * (2.0 * jnp.pi / length)
    cosine = jnp.cos(angles)
    sines = sign_of * jnp.sin(angles)
    return jnp.stack([jnp.stack([cosine, sines]), jnp.stack([-sines, cosine])])


def contract(left, right):
    return jnp.einsum("ig,bg->ib", left, right, precision=PRECISE)


def expand(coeffs, basis):
    return jnp.einsum("ib,ig->bg", coeffs, basis, precision=PRECISE)


def gram(left, right):
    real_part = jnp.einsum("ig,jg->ij", left[0], right[0], precision=PRECISE) + jnp.einsum(
        "ig,jg->ij", left[1], right[1], precision=PRECISE
    )
    imag_part = jnp.einsum("ig,jg->ij", left[0], right[1], precision=PRECISE) - jnp.einsum(
        "ig,jg->ij", left[1], right[0], precision=PRECISE
    )
    return jnp.stack([real_part, imag_part])


def place_rows(values, slots, extent):
    width = values.shape[0] * values.shape[1]
    rows = values.reshape(width, values.shape[-1]).T
    placed = jnp.zeros((extent, width), jnp.float32).at[slots].set(rows, unique_indices=True)
    return placed.T


def pick_rows(values, slots):
    picked = jnp.take(values.T, slots, axis=0)
    return picked.T


def apply_field(sticks_in, potential_part, columns):
    pairs = sticks_in.shape[0]
    bands_in = sticks_in.shape[1]
    planes_in = sticks_in.shape[2]
    count = sticks_in.shape[3]
    width = pairs * bands_in * planes_in
    flat_in = sticks_in.reshape(width, count)
    lattice = place_rows(flat_in.reshape(width, 1, count), columns, GX * GY)
    lattice = lattice.reshape(pairs, bands_in, planes_in, GX, GY)
    x_line = jnp.arange(GX, dtype=jnp.int32)
    y_line = jnp.arange(GY, dtype=jnp.int32)
    lattice = jnp.einsum(
        "pbzxy,pqyv->qbzxv", lattice, dft_table(y_line, y_line, GY, 1.0), precision=PRECISE
    )
    lattice = jnp.einsum(
        "pbzxy,pqxw->qbzwy", lattice, dft_table(x_line, x_line, GX, 1.0), precision=PRECISE
    )
    lattice = lattice * potential_part[None, None]
    lattice = jnp.einsum(
        "pbzxy,pqxw->qbzwy", lattice, dft_table(x_line, x_line, GX, -1.0), precision=PRECISE
    )
    lattice = jnp.einsum(
        "pbzxy,pqyv->qbzxv", lattice, dft_table(y_line, y_line, GY, -1.0), precision=PRECISE
    )
    picked = pick_rows(lattice.reshape(width, GX * GY), columns)
    return picked.reshape(pairs, bands_in, planes_in, count)


def local(wave_coef, projector, potential, grid_slot, stick_column, proj_atom, coupling):
    bands_here = wave_coef.shape[1]
    coef_here = wave_coef.shape[2]
    pw_count = lax.axis_size("pw")
    stick_count = stick_column.shape[0] // pw_count
    owned = lax.dynamic_slice_in_dim(stick_column, lax.axis_index("pw") * stick_count, stick_count)
    z_cell = grid_slot // stick_count
    column = jnp.take(owned, grid_slot % stick_count)
    kinetic = kinetic_of(column // GY, column % GY, z_cell)
    everyone = lax.all_gather(wave_coef, "band", axis=1, tiled=True)
    becp_real = contract(projector[0], wave_coef[0]) + contract(projector[1], wave_coef[1])
    becp_imag = contract(projector[0], wave_coef[1]) - contract(projector[1], wave_coef[0])
    becp = lax.psum(jnp.stack([becp_real, becp_imag]), "pw")
    scattered = place_rows(wave_coef, grid_slot, GZ * stick_count)
    scattered = scattered.reshape(2, bands_here, GZ, stick_count)
    z_line = jnp.arange(GZ, dtype=jnp.int32)
    spread = jnp.einsum(
        "pbzs,pqzr->qbrs", scattered, dft_table(z_line, z_line, GZ, 1.0), precision=PRECISE
    )
    worked = apply_field(
        lax.all_to_all(spread, "pw", split_axis=2, concat_axis=3, tiled=True),
        potential,
        stick_column,
    )
    returned = lax.all_to_all(worked, "pw", split_axis=3, concat_axis=2, tiled=True)
    gathered_z = jnp.einsum(
        "pbrs,pqrz->qbzs", returned, dft_table(z_line, z_line, GZ, -1.0), precision=PRECISE
    )
    picked = pick_rows(gathered_z.reshape(2 * bands_here, GZ * stick_count), grid_slot)
    local_term = picked.reshape(2, bands_here, coef_here) / (GX * GY * GZ)
    same_atom = proj_atom[:, None] == proj_atom[None, :]
    matrix = jnp.where(same_atom, 0.5 * (coupling + coupling.T), 0.0)
    coupled_real = jnp.dot(matrix, becp[0], precision=PRECISE)
    coupled_imag = jnp.dot(matrix, becp[1], precision=PRECISE)
    nonlocal_real = expand(coupled_real, projector[0]) - expand(coupled_imag, projector[1])
    nonlocal_imag = expand(coupled_imag, projector[0]) + expand(coupled_real, projector[1])
    nonlocal_term = jnp.stack([nonlocal_real, nonlocal_imag])
    applied = kinetic[None, None, :] * wave_coef + local_term + nonlocal_term
    subspace_h, correlation = lax.psum((gram(everyone, applied), gram(everyone, wave_coef)), "pw")
    return (applied, subspace_h, correlation)


def solution(mesh):
    in_specs = (
        P(None, "band", "pw"),
        P(None, None, "pw"),
        P("pw", None, None),
        P("pw"),
        P(),
        P(),
        P(),
    )
    out_specs = (P(None, "band", "pw"), P(None, None, "band"), P(None, None, "band"))
    return jax.shard_map(local, mesh=mesh, in_specs=in_specs, out_specs=out_specs, check_vma=False)
```

profile of v0, /device:TPU:0, one launch (start us, length us, event | category | flops | bytes accessed | tf_op | source)
XLA Modules:
  0.0 842.4 jit_solution(16105582156416563336)
XLA Ops:
  12.5 60.7 %scatter_custom_fusion = f32[98304,2]{1,0:T(8,128)} fusion(s32[16384]{0:T(1024)S(1)} %get-tuple-element.30, f32[16384,2]{1,0:T(8,128)} %copy.107, f32[]{:T(128)} %constant.145.clone.1), kind=kCustom, calls=%fused_computation.5 | custom fusion | bytes 786944 | tf_op jit(solution)/shard_map/scatter | solution.py:55
  73.2 27.7 %copy.108 = f32[2,256,384]{2,1,0:T(8,128)S(1)} copy(f32[2,256,384]{0,2,1:T(8,128)} %bitcast.344) | data formatting | bytes 1572864 | tf_op jit(solution)/shard_map/reshape.4
  105.6 10.7 %all-to-all-start = ((f32[2,1,256,384]{3,0,1,2:T(2,128)}), f32[2,1,256,384]{3,0,1,2:T(2,128)S(1)}, u32[]{:S(2)}, u32[]{:S(2)}) async-start(f32[2,1,256,384]{3,0,1,2:T(2,128)} %copy.109), calls=%async_computation | async-start | bytes 1572864 | tf_op jit(solution)/shard_map/all_to_all | solution.py:112
  136.8 96.9 %psum.21 = f32[2,64,1]{1,2,0:T(1,128)S(1)} all-reduce(f32[2,64,1]{1,2,0:T(1,128)S(1)} %pad_maximum_fusion.10), channel_id=1, replica_groups=mesh['pw'=32,'band'=4] {'pw'}, use_global_device_ids=true, to_apply=%region_2.3 | all-reduce | flops 128 | bytes 1024 | tf_op jit(solution)/shard_map/psum | solution.py:104
  251.3 101.9 %gather_fusion = s32[16384]{0:T(1024)S(1)} fusion(s32[384]{0:T(512)S(1)} %dynamic_slice.3, s32[16384]{0:T(1024)S(1)} %copy-done.5), kind=kCustom, calls=%fused_computation | custom fusion | bytes 196608 | tf_op jit(solution)/shard_map/jit(_take)/gather | solution.py:99
  358.1 43.9 %scatter_custom_fusion.1 = f32[65536,16]{1,0:T(8,128)} fusion(s32[12288]{0:T(1024)S(1)} %get-tuple-element.32, f32[12288,16]{1,0:T(8,128)} %copy.111, f32[]{:T(128)} %constant.145.clone.1), kind=kCustom, calls=%fused_computation.7 | custom fusion | bytes 4194816 | tf_op jit(solution)/shard_map/scatter | solution.py:55
  402.1 19.2 %copy.112 = f32[16,65536]{1,0:T(8,128)} copy(f32[16,65536]{0,1:T(8,128)} %bitcast.345) | data formatting | bytes 8388608 | tf_op jit(solution)/shard_map/transpose | solution.py:56
  421.3 10.1 %fusion.27 = f32[2,256,8,256,1]{3,1,4,2,0:T(8,128)S(1)} fusion(f32[1,2,256,256]{2,3,0,1:T(8,128)S(1)} %get-tuple-element.23, f32[1,2,256,256]{2,3,0,1:T(8,128)S(1)} %get-tuple-element.22, f32[2,8,256,256]{3,1,2,0:T(8,128)} %bitcast.348), kind=kOutput, calls=%fused_computation.35 | convolution fusion | flops 6442713088 | bytes 9437184 | tf_op jit(solution)/shard_map/pbzxy,pqyv->qbzxv/dot_general | solution.py:75
  431.5 7.6 fusion.4
  439.1 7.1 fusion.40
  446.2 8.9 %fusion.165 = f32[2,8,256,256]{2,3,1,0:T(8,128)} fusion(f32[2,8,256,256]{3,2,1,0:T(8,128)S(1)} %fusion.40, f32[1,2,256,256]{2,3,1,0:T(8,128)S(1)} %get-tuple-element.24, f32[1,2,256,256]{2,3,1,0:T(8,128)S(1)} %get-tuple-element.25), kind=kOutput, calls=%fused_computation.203 | convolution fusion | flops 6442713088 | bytes 9437184 | tf_op jit(solution)/shard_map/pbzxy,pqyv->qbzxv/dot_general | solution.py:85
  455.1 5.5 copy.156
  460.6 16.8 %copy.120 = f32[16,65536]{0,1:T(8,128)} copy(f32[16,65536]{1,0:T(8,128)} %bitcast.349) | data formatting | bytes 8388608 | tf_op jit(solution)/shard_map/reshape | solution.py:88
  477.4 51.6 %gather_fusion.1 = f32[12288,16]{1,0:T(8,128)} fusion(f32[65536,16]{1,0:T(8,128)} %bitcast.343, s32[12288]{0:T(1024)S(1)} %get-tuple-element.31), kind=kCustom, calls=%fused_computation.1 | custom fusion | bytes 1622016 | tf_op jit(solution)/shard_map/jit(_take)/gather | solution.py:60
  529.0 10.3 %select_bitcast_fusion = f32[16,12288]{0,1:T(8,128)} fusion(f32[12288,16]{1,0:T(8,128)} %gather_fusion.1, pred[12288]{0:T(1024)(128)(4,1)S(1)} %compare_and_fusion.1), kind=kLoop, calls=%fused_computation.9 | loop fusion | flops 196608 | bytes 1585152 | tf_op jit(solution)/shard_map/jit(_take)/select_n | solution.py:60
  543.7 11.2 %copy.122 = f32[2,1,8,12288]{2,0,1,3:T(2,128)} copy(f32[2,1,8,12288]{3,2,0,1:T(8,128)S(1)} %bitcast.350) | data formatting | bytes 1572864 | tf_op jit(solution)/shard_map/reshape | solution.py:89
  554.9 19.4 %reshape.367 = f32[32,1,6144]{2,1,0:T(1,128)} reshape(f32[12288,1,2,8]{3,2,1,0:T(2,128)} %bitcast.346) | data formatting | bytes 1572864
  578.7 12.4 %all-to-all-done.1 = f32[32,1,6144]{2,1,0:T(1,128)S(1)} async-done(((f32[32,1,6144]{2,1,0:T(1,128)}), f32[32,1,6144]{2,1,0:T(1,128)S(1)}, u32[]{:S(2)}, u32[]{:S(2)}) %all-to-all-start.1) | async-done | bytes 786464 | tf_op jit(solution)/shard_map/all_to_all | solution.py:116
  594.2 20.9 %reshape.368 = f32[12288,1,2,8]{3,2,1,0:T(2,128)} reshape(f32[32,6144]{1,0:T(8,128)S(1)} %reduce) | data formatting | bytes 1572864
  615.1 14.3 %copy.149 = f32[2,1,8,32,384]{4,2,3,0,1:T(8,128)S(1)} copy(f32[2,1,8,32,384]{2,0,4,3,1:T(2,128)} %bitcast.347) | data formatting | bytes 1572864 | tf_op jit(solution)/shard_map/all_to_all | solution.py:116
  631.2 24.3 %copy.150 = f32[2,256,384]{0,2,1:T(8,128)} copy(f32[2,256,384]{2,1,0:T(8,128)S(1)} %convolution_bitcast_fusion) | data formatting | bytes 1572864 | tf_op jit(solution)/shard_map/reshape;pbrs,pqrz->qbzs/transpose | solution.py:120
  655.4 69.8 %gather_fusion.2 = f32[16384,2]{1,0:T(8,128)} fusion(f32[98304,2]{1,0:T(8,128)} %bitcast.342, s32[16384]{0:T(1024)S(1)} %copy-done.4), kind=kCustom, calls=%fused_computation.2 | custom fusion | bytes 327680 | tf_op jit(solution)/shard_map/jit(_take)/gather | solution.py:60
  730.9 7.0 all_gather.3
  749.2 92.7 %all-reduce = (f32[2,4,1]{1,2,0:T(1,128)}, f32[2,4,1]{1,2,0:T(1,128)}) all-reduce(f32[2,4,1]{1,2,0:T(1,128)S(1)} %pad_maximum_fusion.11, f32[2,4,1]{1,2,0:T(1,128)S(1)} %pad_maximum_fusion.12), channel_id=1, replica_groups=mesh['pw'=32,'band'=4] {'pw'}, use_global_device_ids=true, to_apply=%region_3.4 | all-reduce | flops 16 | bytes 128 | tf_op jit(solution)/shard_map/psum | solution.py:130
  (67 shorter events, 90.1 us)
Async XLA Ops:
  100.9 15.5 %copy-start.1 = (f32[2,1,16384]{2,1,0:T(1,128)S(1)}, f32[2,1,16384]{2,1,0:T(1,128)}, u32[]{:S(2)}) copy-start(f32[2,1,16384]{2,1,0:T(1,128)} %param.7) | copy-start | bytes 393220
  104.1 22.4 %copy-start.3 = (f32[64,64]{1,0:T(8,128)S(1)}, f32[64,64]{1,0:T(8,128)}, u32[]{:S(2)}) copy-start(f32[64,64]{1,0:T(8,128)} %param.13) | copy-start | bytes 49156
  105.6 247.7 %all-to-all-start = ((f32[2,1,256,384]{3,0,1,2:T(2,128)}), f32[2,1,256,384]{3,0,1,2:T(2,128)S(1)}, u32[]{:S(2)}, u32[]{:S(2)}) async-start(f32[2,1,256,384]{3,0,1,2:T(2,128)} %copy.109), calls=%async_computation | async-start | bytes 1572864 | tf_op jit(solution)/shard_map/all_to_all | solution.py:112
  121.4 112.2 %copy-start.7 = (s32[64]{0:T(128)S(1)}, s32[64]{0:T(128)}, u32[]{:S(2)}) copy-start(s32[64]{0:T(128)} %param.12) | copy-start | bytes 772
  238.4 12.8 %copy-start.6 = (s32[12288]{0:T(1024)S(1)}, s32[12288]{0:T(1024)}, u32[]{:S(2)}) copy-start(s32[12288]{0:T(1024)} %param.11) | copy-start | bytes 147460
  238.4 12.9 %copy-start.5 = (s32[16384]{0:T(1024)S(1)}, s32[16384]{0:T(1024)}, u32[]{:S(2)}) copy-start(s32[16384]{0:T(1024)} %get-tuple-element.28) | copy-start | bytes 196612
  421.3 10.2 %copy-start = (f32[8,256,256]{2,1,0:T(8,128)S(1)}, f32[8,256,256]{2,1,0:T(8,128)}, u32[]{:S(2)}) copy-start(f32[8,256,256]{2,1,0:T(8,128)} %param.9) | copy-start | bytes 6291460
  554.9 23.5 %copy-start.2 = (s32[16384]{0:T(1024)S(1)}, s32[16384]{0:T(1024)}, u32[]{:S(2)}) copy-start(s32[16384]{0:T(1024)} %param.10) | copy-start | bytes 196612
  574.3 16.8 %all-to-all-start.1 = ((f32[32,1,6144]{2,1,0:T(1,128)}), f32[32,1,6144]{2,1,0:T(1,128)S(1)}, u32[]{:S(2)}, u32[]{:S(2)}) async-start(f32[32,1,6144]{2,1,0:T(1,128)} %reshape.367), calls=%async_computation.1 | async-start | bytes 1572864 | tf_op jit(solution)/shard_map/all_to_all | solution.py:116
  631.2 24.3 %copy-start.4 = (s32[16384]{0:T(1024)S(1)}, s32[16384]{0:T(1024)}, u32[]{:S(2)}) copy-start(s32[16384]{0:T(1024)} %get-tuple-element.29) | copy-start | bytes 196612
where the time goes:
time: 853 us; the launch traced here: 842 us
  local copies, waits for them, and re-layouts  511 us (60%)
  blocking collectives  197 us (23%)
  matrix products  85.4 us (10%)
  other arithmetic  20.9 us (2%)
  starting transfers between devices  14.8 us (2%)
  waiting for transfers between devices  12.4 us (1%)
    gather x3, local copies, waits for them, and re-layouts, pick_rows(): picked = jnp.take(values.T, slots, axis=0)  127 us
    scatter x2, local copies, waits for them, and re-layouts, place_rows(): jnp.zeros((extent, width), jnp.float32).at[slots]  105 us
    gather x1, local copies, waits for them, and re-layouts, local(): column = jnp.take(owned, grid_slot % stick_count)  102 us
    psum x1, blocking collectives, local(): becp = lax.psum(jnp.stack([becp_real, becp_imag]), 'pw')  96.9 us
    psum x1, blocking collectives, local(): lax.psum((gram(everyone, applied), gram(everyone, wave_coef)), 'pw')  92.7 us
    unnamed x23, local copies, waits for them, and re-layouts  48.2 us
    another operation x1, local copies, waits for them, and re-layouts  27.7 us
    transpose x1, local copies, waits for them, and re-layouts, local(): gathered_z.reshape(2 * bands_here, GZ * stick_count)  24.3 us
  transfers between devices with their start and end apart: 2, of which 1 were waited for; matrix products, arithmetic and copies ran while one was open for 17% of the time, Pallas kernels for 0%

commit v1 on v0

v1 whole, which is shorter than its diff:
```python
import functools

import jax
import jax.numpy as jnp
import ml_dtypes
import numpy as np
from jax import lax
from jax.experimental import pallas as pl
from jax.experimental.pallas import tpu as pltpu
from jax.sharding import PartitionSpec as P

GX = 256
GY = 256
GZ = 256
KIN_MAX = 2.0
PRECISE = lax.Precision.HIGHEST

PW = 32
STICKS = 384
COEFS = 16384
PROJ = 64
PLANES = GZ // PW
ROWS = 2 * PLANES
KC = 1024
TILES = STICKS // 128
BLOCKS = 48
XC = 16
F32 = jnp.float32
BF16 = jnp.bfloat16
NN = (((1,), (0,)), ((), ()))
NT = (((1,), (1,)), ((), ()))


def mm(left, right, dims=NN):
    return lax.dot_general(left, right, dims, preferred_element_type=F32)


def split(value):
    high = value.astype(BF16)
    low = (value - high.astype(F32)).astype(BF16)
    return high, low


def split_table(table):
    high = table.astype(np.float32).astype(ml_dtypes.bfloat16)
    low = (table - high.astype(np.float64)).astype(np.float32).astype(ml_dtypes.bfloat16)
    return high, low


def trig():
    n = np.arange(256)
    angle = 2.0 * np.pi * (np.outer(n, n) % 256) / 256.0
    return np.cos(angle), np.sin(angle)


def plane_tables():
    c, s = trig()
    high, low = split_table(np.concatenate([c, s], axis=0))
    left = np.concatenate([high, low, high], axis=1)
    return left, np.ascontiguousarray(left.T)


def spread_table():
    c, s = trig()
    rows = np.concatenate(
        [np.concatenate([np.concatenate([c[z], -s[z]])[None] if part == 0 else np.concatenate([s[z], c[z]])[None]
                         for z in range(d * PLANES, (d + 1) * PLANES)])
         for d in range(PW) for part in range(2)])
    high, low = split_table(rows)
    return np.concatenate([high, low, high], axis=1)


def collect_table():
    c, s = trig()
    full = np.zeros((512, 512))
    for d in range(PW):
        zs = np.arange(d * PLANES, (d + 1) * PLANES)
        at = d * ROWS
        full[:256, at:at + PLANES] = c[:, zs]
        full[:256, at + PLANES:at + ROWS] = s[:, zs]
        full[256:, at:at + PLANES] = -s[:, zs]
        full[256:, at + PLANES:at + ROWS] = c[:, zs]
    high, low = split_table(full)
    return np.concatenate([high, low, high], axis=1)


def iota(shape, dim):
    return lax.broadcasted_iota(jnp.int32, shape, dim).astype(F32)


def slot_parts(slot):
    slot = slot.astype(F32)
    z = jnp.floor((slot + 0.5) * (1.0 / STICKS))
    return z, slot - z * STICKS


def rank_of(owned):
    wide = jnp.broadcast_to(owned, (128, STICKS))
    down = jnp.transpose(wide)[:, :1]
    rank_row = jnp.sum(jnp.where(down < owned, 1.0, 0.0), axis=0, keepdims=True)
    order = jnp.where(iota((STICKS, STICKS), 0) == rank_row, 1.0, 0.0)
    rank_col = jnp.sum(jnp.where(owned < down, 1.0, 0.0), axis=1, keepdims=True)
    ordered = jnp.sum(jnp.where(iota((STICKS, STICKS), 1) == rank_col, down, 0.0), axis=0, keepdims=True)
    return order, ordered


def spread_kernel(slot_ref, coef_ref, proj_ref, owned_ref, table_ref, out_ref, acc, becp):
    step = pl.program_id(0)

    @pl.when(step == 0)
    def _():
        acc[...] = jnp.zeros_like(acc)
        becp[...] = jnp.zeros_like(becp)

    z, s = slot_parts(slot_ref[...])
    c_re = coef_ref[0]
    c_im = coef_ref[1]
    re_hi, re_lo = split(c_re)
    im_hi, im_lo = split(c_im)
    z_hot = iota((GZ, KC), 0).astype(BF16) == z.astype(BF16)
    none = jnp.zeros((), BF16)
    placed = jnp.concatenate(
        [jnp.where(z_hot, part, none) for part in (re_hi, im_hi, re_lo, im_lo)], axis=0)
    s_hot = jnp.where(
        (iota((STICKS, KC), 0) - 192.0).astype(BF16) == (s - 192.0).astype(BF16), jnp.ones((), BF16), none)
    acc[...] += mm(s_hot, placed, NT)

    p_re = proj_ref[0]
    p_im = proj_ref[1]
    real = p_re * c_re + p_im * c_im
    imag = p_re * c_im - p_im * c_re
    both = jnp.concatenate([real, imag], axis=0)
    total = both[:, :128]
    for at in range(128, KC, 128):
        total = total + both[:, at:at + 128]
    becp[...] += total

    @pl.when(step == pl.num_programs(0) - 1)
    def _():
        order, ordered = rank_of(owned_ref[...].astype(F32))
        sticks = mm(order.astype(BF16), acc[...].astype(BF16)).astype(BF16)
        high = sticks[:, :512]
        low = sticks[:, 512:]
        spread = mm(table_ref[...], jnp.concatenate([high, high, low], axis=1), NT)
        spread = spread.reshape(PW, ROWS, STICKS)
        for t in range(TILES):
            out_ref[:, t * ROWS:(t + 1) * ROWS, :] = spread[:, :, t * 128:(t + 1) * 128]
        line = jnp.sum(jnp.transpose(becp[...]), axis=0, keepdims=True)
        extra = jnp.concatenate(
            [line] + [ordered[:, t * 128:(t + 1) * 128] for t in range(TILES)] + [jnp.zeros((4, 128), F32)], axis=0)
        out_ref[:, TILES * ROWS:, :] = jnp.broadcast_to(extra[None], (PW, 8, 128))


def spread_sticks(slot, coef, proj, owned):
    table = jnp.asarray(spread_table())
    return pl.pallas_call(
        spread_kernel,
        grid=(COEFS // KC,),
        in_specs=[
            pl.BlockSpec((1, KC), lambda i: (0, i)),
            pl.BlockSpec((2, 1, KC), lambda i: (0, 0, i)),
            pl.BlockSpec((2, PROJ, KC), lambda i: (0, 0, i)),
            pl.BlockSpec((1, STICKS), lambda i: (0, 0)),
            pl.BlockSpec((512, 1536), lambda i: (0, 0)),
        ],
        out_specs=pl.BlockSpec((PW, 56, 128), lambda i: (0, 0, 0)),
        out_shape=jax.ShapeDtypeStruct((PW, 56, 128), F32),
        scratch_shapes=[pltpu.VMEM((STICKS, 1024), F32), pltpu.VMEM((128, 128), F32)],
        compiler_params=pltpu.CompilerParams(vmem_limit_bytes=48 << 20),
        name="spread_sticks",
    )(slot, coef, proj, owned, table)


def swap_chunks(parts):
    parts = list(parts)
    chunk = lax.broadcasted_iota(jnp.int32, parts[0].shape, 1) // 16
    for bit in (1, 2, 4):
        here = (chunk & bit) == 0
        for a in range(8):
            if a & bit:
                continue
            one, two = parts[a], parts[a | bit]
            parts[a] = jnp.where(here, one, pltpu.roll(two, 16 * bit, 1))
            parts[a | bit] = jnp.where(here, pltpu.roll(one, 128 - 16 * bit, 1), two)
    return parts


def field_kernel(range_ref, recv_ref, field_ref, left_ref, right_ref, out_ref, sticks, cells, grid, done):
    for t in range(TILES):
        for g in range(4):
            mixed = swap_chunks([recv_ref[g * 8 + i, t * ROWS:(t + 1) * ROWS, :] for i in range(8)])
            for c in range(8):
                sticks[(t * 8 + c) * 2 + g // 2, :, (g % 2) * 128:(g % 2) * 128 + 128] = mixed[c]
    for g in range(4):
        mixed = swap_chunks([recv_ref[g * 8 + i, TILES * ROWS:, :] for i in range(8)])
        for c in range(8):
            for t in range(TILES):
                cells[(t * 8 + c) * 2 + g // 2, :, (g % 2) * 128:(g % 2) * 128 + 128] = jnp.broadcast_to(
                    mixed[c][1 + t:2 + t], (8, 128))

    grid[...] = jnp.zeros_like(grid)

    def cell_of(b):
        cell = cells[b][:1]
        x = jnp.floor(cell * (1.0 / GY))
        y = cell - x * GY
        hot = jnp.where(iota((GY, 256), 0).astype(BF16) == y.astype(BF16), jnp.ones((), BF16), jnp.zeros((), BF16))
        return x, hot

    def place(b, carry):
        x, hot = cell_of(b)
        high, low = split(sticks[b])
        both = jnp.concatenate([high.astype(F32), low.astype(F32)], axis=0)
        wide = jnp.broadcast_to(both[:, None, :], (2 * ROWS, XC, 256)).astype(BF16)

        def one(at, inner):
            first = at * XC
            mine = (iota((XC, 256), 0) + first.astype(F32)).astype(BF16) == x.astype(BF16)
            masked = jnp.where(mine[None], wide, jnp.zeros((), BF16)).reshape(2 * ROWS * XC, 256)
            added = mm(masked, hot, NT).reshape(2, ROWS, XC, 256)
            here = pl.ds(pl.multiple_of(first, XC), XC)
            grid[:, here, :] += added[0] + added[1]
            return inner

        return lax.fori_loop(range_ref[b, 0], range_ref[b, 1] + 1, one, carry)

    lax.fori_loop(0, BLOCKS, place, 0)

    def plane(zz, carry):
        re = grid[zz]
        im = grid[PLANES + zz]

        def along_y(re, im):
            high, low = split(jnp.concatenate([re, im], axis=0))
            return mm(jnp.concatenate([high, high, low], axis=1), right_ref[...])

        def along_x(re, im):
            high, low = split(jnp.concatenate([re, im], axis=1))
            return mm(left_ref[...], jnp.concatenate([high, high, low], axis=0))

        got = along_y(re, im)
        re = got[:256, :256] - got[256:, 256:]
        im = got[:256, 256:] + got[256:, :256]
        got = along_x(re, im)
        re = got[:256, :256] - got[256:, 256:]
        im = got[256:, :256] + got[:256, 256:]
        field = field_ref[zz]
        re = re * field
        im = im * field
        got = along_x(re, im)
        re = got[:256, :256] + got[256:, 256:]
        im = got[:256, 256:] - got[256:, :256]
        got = along_y(re, im)
        re = got[:256, :256] + got[256:, 256:]
        im = got[256:, :256] - got[:256, 256:]
        high, low = split(re)
        done[zz, :, :256] = high
        done[zz, :, 256:] = low
        high, low = split(im)
        done[PLANES + zz, :, :256] = high
        done[PLANES + zz, :, 256:] = low
        return carry

    lax.fori_loop(0, PLANES, plane, 0)

    def pick(b, carry):
        x, hot = cell_of(b)
        hot = jnp.concatenate([hot, hot], axis=0)

        def one(at, total):
            first = at * XC
            mine = (iota((XC, 256), 0) + first.astype(F32)) == x
            here = pl.ds(pl.multiple_of(first, XC), XC)
            lines = done[:, here, :].reshape(ROWS * XC, 512)
            got = mm(lines, hot).reshape(ROWS, XC, 256)
            got = jnp.where(mine[None], got, 0.0)
            return total + got[:, :8] + got[:, 8:]

        total = lax.fori_loop(range_ref[b, 0], range_ref[b, 1] + 1, one, jnp.zeros((ROWS, 8, 256), F32))
        sticks[b] = jnp.sum(total, axis=1)
        return carry

    lax.fori_loop(0, BLOCKS, pick, 0)

    for t in range(TILES):
        for g in range(4):
            mixed = swap_chunks(
                [sticks[(t * 8 + c) * 2 + g // 2, :, (g % 2) * 128:(g % 2) * 128 + 128] for c in range(8)])
            for i in range(8):
                out_ref[g * 8 + i, t * ROWS:(t + 1) * ROWS, :] = mixed[i]


def apply_field(ranges, recv, field):
    left, right = plane_tables()
    vmem = pl.BlockSpec(memory_space=pltpu.VMEM)
    return pl.pallas_call(
        field_kernel,
        in_specs=[pl.BlockSpec(memory_space=pltpu.SMEM), vmem, vmem, vmem, vmem],
        out_specs=vmem,
        out_shape=jax.ShapeDtypeStruct((PW, 48, 128), F32),
        scratch_shapes=[
            pltpu.VMEM((BLOCKS, ROWS, 256), F32),
            pltpu.VMEM((BLOCKS, 8, 256), F32),
            pltpu.VMEM((ROWS, GX, GY), F32),
            pltpu.VMEM((ROWS, GX, 2 * GY), BF16),
        ],
        compiler_params=pltpu.CompilerParams(vmem_limit_bytes=56 << 20),
        name="apply_field",
    )(ranges, recv, field, jnp.asarray(left), jnp.asarray(right))


def centred(values, length):
    return jnp.where(values < length // 2, values, values - length)


def collect_kernel(slot_ref, coef_ref, all_ref, proj_ref, recv_ref, owned_ref, coupled_ref, table_ref,
                   out_ref, sums_ref, values, sums):
    step = pl.program_id(0)

    @pl.when(step == 0)
    def _():
        sums[...] = jnp.zeros_like(sums)
        owned = owned_ref[...].astype(F32)
        order, _ = rank_of(owned)
        order = order.astype(BF16)
        lines = jnp.concatenate(
            [recv_ref[:, t * ROWS:(t + 1) * ROWS, :].reshape(512, 128) for t in range(TILES)], axis=1)
        high, low = split(lines)
        back = mm(table_ref[...], jnp.concatenate([high, high, low], axis=0))
        high, low = split(back)
        values[:512, :STICKS] = mm(high, order).astype(BF16)
        values[:512, STICKS:] = mm(low, order).astype(BF16)
        x = jnp.floor(owned * (1.0 / GY))
        y = centred(owned - x * GY, GY)
        x = centred(x, GX)
        square = x * x + y * y
        upper = jnp.floor(square * (1.0 / 256.0))
        lower = square - upper * 256.0
        pair = jnp.concatenate([upper, lower, jnp.zeros((14, STICKS), F32)], axis=0)
        values[512:, :STICKS] = pair.astype(BF16)
        values[512:, STICKS:] = jnp.zeros((16, STICKS), BF16)

    z, s = slot_parts(slot_ref[...])
    none = jnp.zeros((), BF16)
    s_hot = jnp.where(
        (iota((STICKS, KC), 0) - 192.0).astype(BF16) == (s - 192.0).astype(BF16), jnp.ones((), BF16), none)
    found = mm(values[...], jnp.concatenate([s_hot, s_hot], axis=0))
    z_hot = iota((GZ, KC), 0) == z
    scale = 1.0 / (GX * GY * GZ)
    local_re = jnp.sum(jnp.where(z_hot, found[:256], 0.0), axis=0, keepdims=True) * scale
    local_im = jnp.sum(jnp.where(z_hot, found[256:512], 0.0), axis=0, keepdims=True) * scale
    z = centred(z, GZ)
    square = found[512:513] * 256.0 + found[513:514] + z * z
    kinetic = square * (KIN_MAX / 3.0 / 16384.0)
    c_re = coef_ref[0]
    c_im = coef_ref[1]
    p_re = proj_ref[0]
    p_im = proj_ref[1]
    w_re = coupled_ref[0]
    w_im = coupled_ref[1]
    far_re = jnp.sum(p_re * w_re - p_im * w_im, axis=0, keepdims=True)
    far_im = jnp.sum(p_re * w_im + p_im * w_re, axis=0, keepdims=True)
    h_re = kinetic * c_re + local_re + far_re
    h_im = kinetic * c_im + local_im + far_im
    out_ref[0] = h_re
    out_ref[1] = h_im
    a_re = all_ref[0]
    a_im = all_ref[1]
    sums[0] += a_re * h_re + a_im * h_im
    sums[1] += a_re * h_im - a_im * h_re
    sums[2] += a_re * c_re + a_im * c_im
    sums[3] += a_re * c_im - a_im * c_re

    @pl.when(step == pl.num_programs(0) - 1)
    def _():
        sums_ref[...] = jnp.broadcast_to(jnp.sum(sums[...], axis=2, keepdims=True), (4, 4, 128))


def collect(slot, coef, everyone, proj, recv, owned, coupled):
    table = jnp.asarray(collect_table())
    return pl.pallas_call(
        collect_kernel,
        grid=(COEFS // KC,),
        in_specs=[
            pl.BlockSpec((1, KC), lambda i: (0, i)),
            pl.BlockSpec((2, 1, KC), lambda i: (0, 0, i)),
            pl.BlockSpec((2, 4, KC), lambda i: (0, 0, i)),
            pl.BlockSpec((2, PROJ, KC), lambda i: (0, 0, i)),
            pl.BlockSpec((PW, 48, 128), lambda i: (0, 0, 0)),
            pl.BlockSpec((1, STICKS), lambda i: (0, 0)),
            pl.BlockSpec((2, PROJ, 1), lambda i: (0, 0, 0)),
            pl.BlockSpec((512, 1536), lambda i: (0, 0)),
        ],
        out_specs=[
            pl.BlockSpec((2, 1, KC), lambda i: (0, 0, i)),
            pl.BlockSpec((4, 4, 128), lambda i: (0, 0, 0)),
        ],
        out_shape=[
            jax.ShapeDtypeStruct((2, 1, COEFS), F32),
            jax.ShapeDtypeStruct((4, 4, 128), F32),
        ],
        scratch_shapes=[pltpu.VMEM((528, 2 * STICKS), BF16), pltpu.VMEM((4, 4, KC), F32)],
        compiler_params=pltpu.CompilerParams(vmem_limit_bytes=48 << 20),
        name="collect",
    )(slot, coef, everyone, proj, recv, owned, coupled, table)


def local(wave_coef, projector, potential, grid_slot, stick_column, proj_atom, coupling):
    owned = lax.dynamic_slice_in_dim(stick_column, lax.axis_index("pw") * STICKS, STICKS).reshape(1, STICKS)
    slot = grid_slot.reshape(1, COEFS)
    everyone = lax.all_gather(wave_coef, "band", axis=1, tiled=True)
    sent = spread_sticks(slot, wave_coef, projector, owned)
    recv = lax.all_to_all(sent, "pw", split_axis=0, concat_axis=0, tiled=True)

    rows = recv[:, 49:52, :].reshape(2, 16, TILES, 8, 16)
    rows = jnp.floor(rows * (1.0 / (GY * XC))).astype(jnp.int32)
    first = jnp.min(rows, axis=(1, 4)).transpose(1, 2, 0).reshape(BLOCKS)
    last = jnp.max(rows, axis=(1, 4)).transpose(1, 2, 0).reshape(BLOCKS)
    worked = apply_field(jnp.stack([first, last], axis=1), recv, potential)
    returned = lax.all_to_all(worked, "pw", split_axis=0, concat_axis=0, tiled=True)

    becp = jnp.sum(recv[:, 48, :], axis=0).reshape(2, PROJ)
    same_atom = proj_atom[:, None] == proj_atom[None, :]
    matrix = jnp.where(same_atom, 0.5 * (coupling + coupling.T), 0.0)
    coupled = jnp.sum(matrix[None] * becp[:, None, :], axis=2, keepdims=True)
    applied, sums = collect(slot, wave_coef, everyone, projector, returned, owned, coupled)
    parts = jnp.broadcast_to(sums[:, :, 0].reshape(1, 16), (PW, 16))
    parts = jnp.pad(parts, ((0, 0), (0, 112)))
    total = jnp.sum(lax.all_to_all(parts, "pw", split_axis=0, concat_axis=0, tiled=True), axis=0)[:16]
    total = total.reshape(2, 2, 4, 1)
    return applied, total[0], total[1]


def solution(mesh):
    in_specs = (
        P(None, "band", "pw"),
        P(None, None, "pw"),
        P("pw", None, None),
        P("pw"),
        P(),
        P(),
        P(),
    )
    out_specs = (P(None, "band", "pw"), P(None, None, "band"), P(None, None, "band"))
    return jax.shard_map(local, mesh=mesh, in_specs=in_specs, out_specs=out_specs, check_vma=False)
```

time: 853 us -> 220 us (0.26); the launches traced: 842 us -> 218 us
  local copies, waits for them, and re-layouts: 511 us -> 7.47 us
  Pallas kernels: 0 us -> 144 us
  blocking collectives: 197 us -> 59.6 us
  matrix products: 85.4 us -> 0 us
  other arithmetic: 20.9 us -> 1.49 us
  waiting for transfers between devices: 12.4 us -> 0.01 us
  starting transfers between devices: 14.8 us -> 4.58 us
    gather x4 -> x0, local copies, waits for them, and re-layouts: 229 us -> none  [the longest x3 127 us: pick_rows(): picked = jnp.take(values.T, slots, axis=0)]
    psum x2 -> x0, blocking collectives: 190 us -> none  [the longest x1 96.9 us: local(): becp = lax.psum(jnp.stack([becp_real, becp_imag]), 'pw')]
    pallas_call x0 -> x3, Pallas kernels: none -> 144 us  [the longest x1 103 us: apply_field(): pl.pallas_call(field_kernel, in_specs=[pl.BlockSpec(memory_space=pltpu.SM...]
    scatter x2 -> x0, local copies, waits for them, and re-layouts: 105 us -> none  [place_rows(): jnp.zeros((extent, width), jnp.float32).at[slots]]
    dot_general x24 -> x0, matrix products: 85.4 us -> none  [the longest x4 20.3 us: contract(): return jnp.einsum('ig,bg->ib', left, right, precision=PRECISE)]
    transpose x5 -> x2, local copies, waits for them, and re-layouts: 54 us -> 0.19 us  [the longest x1 0.09 us: local(): last = jnp.max(rows, axis=(1, 4)).transpose(1, 2, 0).reshape(BLOCKS)]
    all_to_all x0 -> x2, blocking collectives: none -> 45.9 us  [the longest x1 27.4 us: local(): recv = lax.all_to_all(sent, 'pw', split_axis=0, concat_axis=0, tiled=True)]
    unnamed x23 -> x20, local copies, waits for them, and re-layouts: 48.2 us -> 3.35 us
  transfers between devices with their start and end apart: 2 -> 1, of which waited for: 1 -> 0; matrix products, arithmetic and copies ran while one was open for 17% -> 1% of each run, Pallas kernels for 0% -> 0%
where the time goes in v1:
time: 220 us; the launch traced here: 218 us
  Pallas kernels  144 us (65%)
  blocking collectives  59.6 us (27%)
  local copies, waits for them, and re-layouts  7.47 us (3%)
  starting transfers between devices  4.58 us (2%)
    pallas_call x1, Pallas kernels, apply_field(): pl.pallas_call(field_kernel, in_specs=[pl.BlockSpec(memory_space=pltpu.SM...  103 us
    all_to_all x1, blocking collectives, local(): recv = lax.all_to_all(sent, 'pw', split_axis=0, concat_axis=0, tiled=True)  27.4 us
    pallas_call x1, Pallas kernels, collect(): pl.pallas_call(collect_kernel, grid=(COEFS // KC,), in_specs=[pl.BlockSpe...  21.2 us
    pallas_call x1, Pallas kernels, spread_sticks(): pl.pallas_call(spread_kernel, grid=(COEFS // KC,), in_specs=[pl.BlockSpec...  19.9 us
    all_to_all x1, blocking collectives, local(): lax.all_to_all(parts, 'pw', split_axis=0, concat_axis=0, tiled=True)  18.4 us
    all_gather x1, blocking collectives, local(): everyone = lax.all_gather(wave_coef, 'band', axis=1, tiled=True)  13.8 us
    all_to_all x1, starting transfers between devices, local(): lax.all_to_all(worked, 'pw', split_axis=0, concat_axis=0, tiled=True)  4.58 us
  transfers between devices with their start and end apart: 1, of which 0 were waited for; matrix products, arithmetic and copies ran while one was open for 1% of the time, Pallas kernels for 0%

profile of v1, /device:TPU:0, one launch (start us, length us, event | category | flops | bytes accessed | tf_op | source)
XLA Modules:
  0.0 218.1 jit_solution(5477980969060485989)
XLA Ops:
  0.6 0.8 dynamic_slice.3
  1.4 1.4 copy-done.1
  2.8 0.9 copy-done.2
  3.7 0.8 copy-done.4
  4.6 19.9 %spread_sticks.1 = f32[32,56,128]{2,1,0:T(8,128)S(1)} custom-call(s32[1,16384]{1,0:T(1,128)S(1)} %bitcast.15, f32[2,1,16384]{2,1,0:T(1,128)S(1)} %copy-done.2, f32[2,64,16384]{2,1,0:T(8,128)} %proj_ref.3, s32[1,384]{1,0:T(1,128)S(1)} %reshape.50.owned_ref, bf16[512,1536]{1,0:T(8,128)(2,1)S(1)} %copy-done.1), custom_call_target="tpu_custom_call" | custom-call | tf_op jit(solution)/shard_map/spread_sticks/pallas_call | solution.py:156
  24.4 27.4 %all_to_all.16.recv_ref = f32[32,56,128]{2,1,0:T(8,128)S(1)} all-to-all(f32[32,56,128]{2,1,0:T(8,128)S(1)} %spread_sticks.1), channel_id=1, replica_groups=mesh['pw'=32,'band'=4] {'pw'}, dimensions={0} | all-to-all | bytes 1835008 | tf_op jit(solution)/shard_map/all_to_all | solution.py:413
  51.9 0.2 convert_element_type.9
  52.1 0.3 fusion.4
  52.4 0.1 copy.62
  52.5 0.1 stack_reshape.7
  52.7 0.1 stack_reshape.6
  52.8 0.7 copy.63.range_ref
  53.5 103.1 %apply_field.1 = f32[32,48,128]{2,1,0:T(8,128)} custom-call(s32[48,2]{1,0:T(8,128)} %copy.63.range_ref, f32[32,56,128]{2,1,0:T(8,128)} %copy-done.6, f32[8,256,256]{2,1,0:T(8,128)} %field_ref.1, bf16[512,768]{1,0:T(8,128)(2,1)} %constant.32.clone.left_ref, bf16[768,512]{1,0:T(8,128)(2,1)} %constant.33.clone.right_ref), custom_call_target="tpu_custom_call" | custom-call | tf_op jit(solution)/shard_map/apply_field/pallas_call | solution.py:296
  156.7 4.6 %all-to-all-start.1 = ((f32[32,48,128]{2,1,0:T(8,128)}), f32[32,48,128]{2,1,0:T(8,128)S(1)}, u32[]{:S(2)}, u32[]{:S(2)}) async-start(f32[32,48,128]{2,1,0:T(8,128)} %apply_field.1), calls=%async_computation.1 | async-start | bytes 1572864 | tf_op jit(solution)/shard_map/all_to_all | solution.py:420
  161.3 0.1 copy.58
  161.5 13.8 %all_gather.3 = f32[2,4,16384]{2,0,1:T(2,128)S(1)} all-gather(f32[2,1,16384]{2,0,1:T(2,128)S(1)} %copy.58), channel_id=1, replica_groups=mesh['pw'=32,'band'=4] {'band'}, dimensions={1}, use_global_device_ids=true | all-gather | bytes 655360 | tf_op jit(solution)/shard_map/all_gather | solution.py:411
  175.2 0.3 copy.65.all_ref
  175.7 1.0 slice_reduce_fusion
  176.7 0.1 multiply_reduce_fusion
  176.8 0.1 copy.66.coupled_ref
  176.9 21.2 %collect.1 = (f32[2,1,16384]{2,1,0:T(1,128)}, f32[4,4,128]{2,1,0:T(4,128)S(1)}) custom-call(s32[1,16384]{1,0:T(1,128)S(1)} %bitcast.16, f32[2,1,16384]{2,1,0:T(1,128)S(1)} %copy-done.3, f32[2,4,16384]{2,1,0:T(4,128)S(1)} %copy.65.all_ref, f32[2,64,16384]{2,1,0:T(8,128)} %proj_ref.3, f32[32,48,128]{2,1,0:T(8,128)S(1)} %all-to-all-done.1.recv_ref, ...), custom_call_target="tpu_custom_call" | custom-call | tf_op jit(solution)/shard_map/collect/pallas_call | solution.py:381
  198.3 18.4 %all_to_all.17 = f32[32,1,128]{2,1,0:T(1,128)S(1)} all-to-all(f32[32,1,128]{2,1,0:T(1,128)S(1)} %pad.7), channel_id=1, replica_groups=mesh['pw'=32,'band'=4] {'pw'}, dimensions={0} | all-to-all | bytes 32768 | tf_op jit(solution)/shard_map/all_to_all | solution.py:429
  216.8 0.6 slice.48
  217.5 0.6 slice.46
  (30 shorter events, 0.7 us)
Async XLA Ops:
  1.4 1.4 copy-start.1
  2.8 0.9 copy-start.2
  3.7 0.8 copy-start.4
  51.9 1.6 copy-start.6
  53.5 107.7 %copy-start.3 = (f32[2,1,16384]{2,1,0:T(1,128)S(1)}, f32[2,1,16384]{2,1,0:T(1,128)}, u32[]{:S(2)}) copy-start(f32[2,1,16384]{2,1,0:T(1,128)} %coef_ref.3) | copy-start | bytes 393220
  53.5 107.9 %copy-start.7 = (f32[64,64]{1,0:T(8,128)S(1)}, f32[64,64]{1,0:T(8,128)}, u32[]{:S(2)}) copy-start(f32[64,64]{1,0:T(8,128)} %param.17) | copy-start | bytes 49156
  156.6 18.9 %copy-start.8 = (s32[64]{0:T(128)S(1)}, s32[64]{0:T(128)}, u32[]{:S(2)}) copy-start(s32[64]{0:T(128)} %param.16) | copy-start | bytes 772
  156.7 20.3 %copy-start = (bf16[512,1536]{1,0:T(8,128)(2,1)S(1)}, bf16[512,1536]{1,0:T(8,128)(2,1)}, u32[]{:S(2)}) copy-start(bf16[512,1536]{1,0:T(8,128)(2,1)} %constant.34.clone.table_ref) | copy-start | bytes 4718596
  156.7 20.3 %copy-start.5 = (s32[16384]{0:T(1024)S(1)}, s32[16384]{0:T(1024)}, u32[]{:S(2)}) copy-start(s32[16384]{0:T(1024)} %param.14) | copy-start | bytes 196612
  156.7 20.3 %all-to-all-start.1 = ((f32[32,48,128]{2,1,0:T(8,128)}), f32[32,48,128]{2,1,0:T(8,128)S(1)}, u32[]{:S(2)}, u32[]{:S(2)}) async-start(f32[32,48,128]{2,1,0:T(8,128)} %apply_field.1), calls=%async_computation.1 | async-start | bytes 1572864 | tf_op jit(solution)/shard_map/all_to_all | solution.py:420

commit v2 on v1

--- a/solution.py
+++ b/solution.py
@@ -23,8 +23,11 @@
 ROWS = 2 * PLANES
 KC = 1024
 TILES = STICKS // 128
-BLOCKS = 48
-XC = 16
+GROUPS = 24
+CHUNKS = 16
+NQ = 4
+NCH = 3
+PAIR = 2
 F32 = jnp.float32
 BF16 = jnp.bfloat16
 NN = (((1,), (0,)), ((), ()))
@@ -53,11 +56,25 @@
     return np.cos(angle), np.sin(angle)
 
 
+def folded_table():
+    c, s = trig()
+    return np.concatenate([c[:128], c[128:129], s[1:128]], axis=0)
+
+
 def plane_tables():
-    c, s = trig()
-    high, low = split_table(np.concatenate([c, s], axis=0))
-    left = np.concatenate([high, low, high], axis=1)
-    return left, np.ascontiguousarray(left.T)
+    table = folded_table()
+    order = [128 * part + 8 * chunk + i for chunk in range(CHUNKS) for part in range(2) for i in range(8)]
+    table_x = table[order]
+
+    def left(values):
+        high, low = split_table(values)
+        return jnp.asarray(np.concatenate([high, low, high], axis=1))
+
+    def right(values):
+        high, low = split_table(values)
+        return jnp.asarray(np.concatenate([high, low, high], axis=0))
+
+    return right(table), right(table.T), left(table_x.T), left(table_x)
 
 
 def spread_table():
@@ -94,12 +111,25 @@
     return z, slot - z * STICKS
 
 
+def fold(x):
+    key = jnp.where(x == 128.0, 0.0, jnp.minimum(x, 256.0 - x))
+    even = jnp.where(x == 128.0, -1.0, key)
+    odd = jnp.where(x == 0.0, -1.0, key)
+    return key, even, odd, jnp.where(x > 128.0, -1.0, 1.0)
+
+
 def rank_of(owned):
     wide = jnp.broadcast_to(owned, (128, STICKS))
     down = jnp.transpose(wide)[:, :1]
-    rank_row = jnp.sum(jnp.where(down < owned, 1.0, 0.0), axis=0, keepdims=True)
+
+    def sort_key(column):
+        return fold(jnp.floor(column * (1.0 / GY)))[0] * 65536.0 + column
+
+    key = sort_key(owned)
+    key_down = sort_key(down)
+    rank_row = jnp.sum(jnp.where(key_down < key, 1.0, 0.0), axis=0, keepdims=True)
     order = jnp.where(iota((STICKS, STICKS), 0) == rank_row, 1.0, 0.0)
-    rank_col = jnp.sum(jnp.where(owned < down, 1.0, 0.0), axis=1, keepdims=True)
+    rank_col = jnp.sum(jnp.where(key < key_down, 1.0, 0.0), axis=1, keepdims=True)
     ordered = jnp.sum(jnp.where(iota((STICKS, STICKS), 1) == rank_col, down, 0.0), axis=0, keepdims=True)
     return order, ordered
 
@@ -185,128 +215,170 @@
     return parts
 
 
-def field_kernel(range_ref, recv_ref, field_ref, left_ref, right_ref, out_ref, sticks, cells, grid, done):
+def field_kernel(range_ref, recv_ref, field_ref, y_in_ref, y_out_ref, x_in_ref, x_out_ref, out_ref,
+                 wide, hot, keys, signs, grid, done, sticks):
+    cells = []
+    for g in range(4):
+        mixed = swap_chunks([recv_ref[g * 8 + i, TILES * ROWS:, :] for i in range(8)])
+        cells.append(mixed)
+    one_hot = iota((128, 512), 0).astype(BF16)
+    zero = jnp.zeros((), BF16)
+    for t in range(TILES):
+        mixed = [swap_chunks([recv_ref[g * 8 + i, t * ROWS:(t + 1) * ROWS, :] for i in range(8)]) for g in range(4)]
+        for c in range(8):
+            q = t * 8 + c
+            values = jnp.concatenate([mixed[g][c] for g in range(4)], axis=1)
+            high, low = split(values)
+            both = jnp.concatenate([high.astype(F32), low.astype(F32)], axis=0)
+            wide[q] = jnp.broadcast_to(both[:, None, :], (2 * ROWS, 16, 512)).astype(BF16)
+            column = jnp.concatenate([cells[g][c][1 + t:2 + t] for g in range(4)], axis=1)
+            x = jnp.floor(column * (1.0 / GY))
+            y = column - x * GY
+            _, even, odd, sign = fold(x)
+            upper = iota((16, 512), 0) < 8.0
+            keys[q] = jnp.where(upper, even, odd).astype(BF16)
+            signs[q] = jnp.where(upper, 1.0, sign).astype(BF16)
+            _, even, odd, sign = fold(y)
+            hot[q, :128, :] = jnp.where(one_hot == even.astype(BF16), jnp.ones((), BF16), zero)
+            hot[q, 128:, :] = jnp.where(one_hot == odd.astype(BF16), sign.astype(BF16), zero)
+    for q in range(GROUPS, GROUPS + NQ - 1):
+        wide[q] = jnp.zeros((2 * ROWS, 16, 512), BF16)
+        hot[q] = jnp.zeros((256, 512), BF16)
+        keys[q] = jnp.full((16, 512), -1.0, BF16)
+        signs[q] = jnp.zeros((16, 512), BF16)
+    done[:, GX:, :] = jnp.zeros((ROWS, 16 * (NCH - 1), 512), BF16)
+
+    step_of = iota((16, 512), 0)
+    step_of = jnp.where(step_of < 8.0, step_of, step_of - 8.0)
+
+    def place(chunk, carry):
+        want = (step_of + (chunk * 8).astype(F32)).astype(BF16)
+        here = pl.ds(pl.multiple_of(chunk * 16, 16), 16)
+        start = range_ref[0, chunk]
+
+        def product(first):
+            masked = []
+            for j in range(NQ):
+                mine = jnp.where(keys[first + j] == want, signs[first + j], zero)
+                masked.append((wide[first + j] * mine[None]).reshape(2 * ROWS * 16, 512))
+            got = mm(jnp.concatenate(masked, axis=1),
+                     jnp.concatenate([hot[first + j] for j in range(NQ)], axis=1), NT)
+            got = got.reshape(2, ROWS, 16, 256)
+            return got[0] + got[1]
+
+        grid[:, here, :] = product(start)
+
+        def more(p, inner):
+            grid[:, here, :] += product(start + p * NQ)
+            return inner
+
+        return lax.fori_loop(1, range_ref[1, chunk], more, carry)
+
+    lax.fori_loop(0, CHUNKS, place, 0)
+
+    row = lax.broadcasted_iota(jnp.int32, (256, 256), 0)
+    lane = lax.broadcasted_iota(jnp.int32, (256, 256), 1)
+    even_x = ((row & 8) == 0) | (row == 8)
+    even_y = lane <= 128
+
+    def along_y(re, im, table):
+        high, low = split(jnp.concatenate([re, im], axis=0))
+        got = mm(jnp.concatenate([high, high, low], axis=1), table[...])
+        return got[:256], got[256:]
+
+    def along_x(re, im, table):
+        high, low = split(jnp.concatenate([re, im], axis=1))
+        got = mm(table[...], jnp.concatenate([high, high, low], axis=0))
+        return got[:, :256], got[:, 256:]
+
+    def plane(zz):
+        re = grid[zz]
+        im = grid[PLANES + zz]
+        re, im = along_y(jnp.where(even_y, re, -im), jnp.where(even_y, im, re), y_in_ref)
+        re, im = along_x(jnp.where(even_x, re, -im), jnp.where(even_x, im, re), x_in_ref)
+        field = field_ref[zz]
+        re, im = along_x(re * field, im * field, x_out_ref)
+        re, im = along_y(jnp.where(even_x, re, im), jnp.where(even_x, im, -re), y_out_ref)
+        high, low = split(jnp.where(even_y, re, im))
+        done[zz, :GX, :256] = high
+        done[zz, :GX, 256:] = low
+        high, low = split(jnp.where(even_y, im, -re))
+        done[PLANES + zz, :GX, :256] = high
+        done[PLANES + zz, :GX, 256:] = low
+
+    def planes(pair, carry):
+        for at in range(PAIR):
+            plane(pair * PAIR + at)
+        return carry
+
+    lax.fori_loop(0, PLANES // PAIR, planes, 0)
+
+    def pick(q, carry):
+        both = jnp.concatenate([hot[q], hot[q]], axis=0)
+        key = keys[q].astype(F32)
+        sign = signs[q].astype(F32)
+        start = range_ref[2, q]
+
+        def product(first):
+            here = pl.ds(pl.multiple_of(first * 16, 16), 16 * NCH)
+            lines = done[:, here, :].reshape(ROWS * 16 * NCH, 512)
+            got = mm(lines, both).reshape(ROWS, 2 * NCH, 8, 512)
+            total = None
+            for j in range(NCH):
+                want = step_of + ((first + j) * 8).astype(F32)
+                mine = jnp.where(key == want, sign, 0.0)
+                part = got[:, 2 * j] * mine[None, :8] + got[:, 2 * j + 1] * mine[None, 8:]
+                total = part if total is None else total + part
+            return jnp.sum(total, axis=1)
+
+        sticks[q] = product(start)
+
+        def more(p, inner):
+            sticks[q] += product(start + p * NCH)
+            return inner
+
+        return lax.fori_loop(1, range_ref[3, q], more, carry)
+
+    lax.fori_loop(0, GROUPS, pick, 0)
+
     for t in range(TILES):
         for g in range(4):
-            mixed = swap_chunks([recv_ref[g * 8 + i, t * ROWS:(t + 1) * ROWS, :] for i in range(8)])
-            for c in range(8):
-                sticks[(t * 8 + c) * 2 + g // 2, :, (g % 2) * 128:(g % 2) * 128 + 128] = mixed[c]
-    for g in range(4):
-        mixed = swap_chunks([recv_ref[g * 8 + i, TILES * ROWS:, :] for i in range(8)])
-        for c in range(8):
-            for t in range(TILES):
-                cells[(t * 8 + c) * 2 + g // 2, :, (g % 2) * 128:(g % 2) * 128 + 128] = jnp.broadcast_to(
-                    mixed[c][1 + t:2 + t], (8, 128))
-
-    grid[...] = jnp.zeros_like(grid)
-
-    def cell_of(b):
-        cell = cells[b][:1]
-        x = jnp.floor(cell * (1.0 / GY))
-        y = cell - x * GY
-        hot = jnp.where(iota((GY, 256), 0).astype(BF16) == y.astype(BF16), jnp.ones((), BF16), jnp.zeros((), BF16))
-        return x, hot
-
-    def place(b, carry):
-        x, hot = cell_of(b)
-        high, low = split(sticks[b])
-        both = jnp.concatenate([high.astype(F32), low.astype(F32)], axis=0)
-        wide = jnp.broadcast_to(both[:, None, :], (2 * ROWS, XC, 256)).astype(BF16)
-
-        def one(at, inner):
-            first = at * XC
-            mine = (iota((XC, 256), 0) + first.astype(F32)).astype(BF16) == x.astype(BF16)
-            masked = jnp.where(mine[None], wide, jnp.zeros((), BF16)).reshape(2 * ROWS * XC, 256)
-            added = mm(masked, hot, NT).reshape(2, ROWS, XC, 256)
-            here = pl.ds(pl.multiple_of(first, XC), XC)
-            grid[:, here, :] += added[0] + added[1]
-            return inner
-
-        return lax.fori_loop(range_ref[b, 0], range_ref[b, 1] + 1, one, carry)
-
-    lax.fori_loop(0, BLOCKS, place, 0)
-
-    def plane(zz, carry):
-        re = grid[zz]
-        im = grid[PLANES + zz]
-
-        def along_y(re, im):
-            high, low = split(jnp.concatenate([re, im], axis=0))
-            return mm(jnp.concatenate([high, high, low], axis=1), right_ref[...])
-
-        def along_x(re, im):
-            high, low = split(jnp.concatenate([re, im], axis=1))
-            return mm(left_ref[...], jnp.concatenate([high, high, low], axis=0))
-
-        got = along_y(re, im)
-        re = got[:256, :256] - got[256:, 256:]
-        im = got[:256, 256:] + got[256:, :256]
-        got = along_x(re, im)
-        re = got[:256, :256] - got[256:, 256:]
-        im = got[256:, :256] + got[:256, 256:]
-        field = field_ref[zz]
-        re = re * field
-        im = im * field
-        got = along_x(re, im)
-        re = got[:256, :256] + got[256:, 256:]
-        im = got[:256, 256:] - got[256:, :256]
-        got = along_y(re, im)
-        re = got[:256, :256] + got[256:, 256:]
-        im = got[256:, :256] - got[:256, 256:]
-        high, low = split(re)
-        done[zz, :, :256] = high
-        done[zz, :, 256:] = low
-        high, low = split(im)
-        done[PLANES + zz, :, :256] = high
-        done[PLANES + zz, :, 256:] = low
-        return carry
-
-    lax.fori_loop(0, PLANES, plane, 0)
-
-    def pick(b, carry):
-        x, hot = cell_of(b)
-        hot = jnp.concatenate([hot, hot], axis=0)
-
-        def one(at, total):
-            first = at * XC
-            mine = (iota((XC, 256), 0) + first.astype(F32)) == x
-            here = pl.ds(pl.multiple_of(first, XC), XC)
-            lines = done[:, here, :].reshape(ROWS * XC, 512)
-            got = mm(lines, hot).reshape(ROWS, XC, 256)
-            got = jnp.where(mine[None], got, 0.0)
-            return total + got[:, :8] + got[:, 8:]
-
-        total = lax.fori_loop(range_ref[b, 0], range_ref[b, 1] + 1, one, jnp.zeros((ROWS, 8, 256), F32))
-        sticks[b] = jnp.sum(total, axis=1)
-        return carry
-
-    lax.fori_loop(0, BLOCKS, pick, 0)
-
-    for t in range(TILES):
-        for g in range(4):
-            mixed = swap_chunks(
-                [sticks[(t * 8 + c) * 2 + g // 2, :, (g % 2) * 128:(g % 2) * 128 + 128] for c in range(8)])
+            mixed = swap_chunks([sticks[t * 8 + c, :, g * 128:(g + 1) * 128] for c in range(8)])
             for i in range(8):
                 out_ref[g * 8 + i, t * ROWS:(t + 1) * ROWS, :] = mixed[i]
 
 
 def apply_field(ranges, recv, field):
-    left, right = plane_tables()
     vmem = pl.BlockSpec(memory_space=pltpu.VMEM)
     return pl.pallas_call(
         field_kernel,
-        in_specs=[pl.BlockSpec(memory_space=pltpu.SMEM), vmem, vmem, vmem, vmem],
+        in_specs=[pl.BlockSpec(memory_space=pltpu.SMEM)] + [vmem] * 6,
         out_specs=vmem,
         out_shape=jax.ShapeDtypeStruct((PW, 48, 128), F32),
         scratch_shapes=[
-            pltpu.VMEM((BLOCKS, ROWS, 256), F32),
-            pltpu.VMEM((BLOCKS, 8, 256), F32),
+            pltpu.VMEM((GROUPS + NQ - 1, 2 * ROWS, 16, 512), BF16),
+            pltpu.VMEM((GROUPS + NQ - 1, 256, 512), BF16),
+            pltpu.VMEM((GROUPS + NQ - 1, 16, 512), BF16),
+            pltpu.VMEM((GROUPS + NQ - 1, 16, 512), BF16),
             pltpu.VMEM((ROWS, GX, GY), F32),
-            pltpu.VMEM((ROWS, GX, 2 * GY), BF16),
+            pltpu.VMEM((ROWS, GX + 16 * (NCH - 1), 512), BF16),
+            pltpu.VMEM((GROUPS, ROWS, 512), F32),
         ],
         compiler_params=pltpu.CompilerParams(vmem_limit_bytes=56 << 20),
         name="apply_field",
-    )(ranges, recv, field, jnp.asarray(left), jnp.asarray(right))
+    )(ranges, recv, field, *plane_tables())
+
+
+def ranges_of(columns):
+    chunk = jnp.floor(fold(jnp.floor(columns * (1.0 / GY)))[0] * 0.125).astype(jnp.int32)
+    chunk = chunk.reshape(PW, GROUPS, 16)
+    first = jnp.min(chunk, axis=(0, 2))
+    last = jnp.max(chunk, axis=(0, 2))
+    at = jnp.arange(GROUPS, dtype=jnp.int32)[:, None]
+    start = jnp.sum(jnp.where(last[None] < at, 1, 0), axis=1)
+    end = jnp.sum(jnp.where(first[None] <= at, 1, 0), axis=1)
+    start = jnp.minimum(start, GROUPS - 1)
+    return jnp.stack([start, (end - start + NQ - 1) // NQ, first, (last - first + NCH) // NCH])
 
 
 def centred(values, length):
@@ -412,11 +484,7 @@
     sent = spread_sticks(slot, wave_coef, projector, owned)
     recv = lax.all_to_all(sent, "pw", split_axis=0, concat_axis=0, tiled=True)
 
-    rows = recv[:, 49:52, :].reshape(2, 16, TILES, 8, 16)
-    rows = jnp.floor(rows * (1.0 / (GY * XC))).astype(jnp.int32)
-    first = jnp.min(rows, axis=(1, 4)).transpose(1, 2, 0).reshape(BLOCKS)
-    last = jnp.max(rows, axis=(1, 4)).transpose(1, 2, 0).reshape(BLOCKS)
-    worked = apply_field(jnp.stack([first, last], axis=1), recv, potential)
+    worked = apply_field(ranges_of(recv[:, 49:52, :].reshape(PW, STICKS)), recv, potential)
     returned = lax.all_to_all(worked, "pw", split_axis=0, concat_axis=0, tiled=True)
 
     becp = jnp.sum(recv[:, 48, :], axis=0).reshape(2, PROJ)

time: 220 us -> 168 us (0.76)
  Pallas kernels: 144 us -> 93.6 us
    pallas_call x1, Pallas kernels: 103 us -> 52.5 us  [apply_field(): pl.pallas_call(field_kernel, in_specs=[pl.BlockSpec(memory_space=pltpu.SM...]
where the time goes in v2:
time: 168 us; the launch traced here: 167 us
  Pallas kernels  93.6 us (56%)
  blocking collectives  59.6 us (35%)
  local copies, waits for them, and re-layouts  6.38 us (4%)
  starting transfers between devices  4.57 us (3%)
  other arithmetic  2.2 us (1%)
    pallas_call x1, Pallas kernels, apply_field(): pl.pallas_call(field_kernel, in_specs=[pl.BlockSpec(memory_space=pltpu.SM...  52.5 us
    all_to_all x1, blocking collectives, local(): recv = lax.all_to_all(sent, 'pw', split_axis=0, concat_axis=0, tiled=True)  27.4 us
    pallas_call x1, Pallas kernels, collect(): pl.pallas_call(collect_kernel, grid=(COEFS // KC,), in_specs=[pl.BlockSpe...  21.2 us
    pallas_call x1, Pallas kernels, spread_sticks(): pl.pallas_call(spread_kernel, grid=(COEFS // KC,), in_specs=[pl.BlockSpec...  19.9 us
    all_to_all x1, blocking collectives, local(): lax.all_to_all(parts, 'pw', split_axis=0, concat_axis=0, tiled=True)  18.2 us
    all_gather x1, blocking collectives, local(): everyone = lax.all_gather(wave_coef, 'band', axis=1, tiled=True)  14 us
    all_to_all x1, starting transfers between devices, local(): lax.all_to_all(worked, 'pw', split_axis=0, concat_axis=0, tiled=True)  4.57 us
  transfers between devices with their start and end apart: 1, of which 0 were waited for; matrix products, arithmetic and copies ran while one was open for 1% of the time, Pallas kernels for 0%

profile of v2, /device:TPU:0, one launch (start us, length us, event | category | flops | bytes accessed | tf_op | source)
XLA Modules:
  0.0 167.2 jit_solution(17655552190675145654)
XLA Ops:
  0.6 0.8 dynamic_slice.3
  1.4 1.4 copy-done.1
  2.8 0.9 copy-done.2
  3.7 0.8 copy-done.4
  4.6 19.9 %spread_sticks.1 = f32[32,56,128]{2,1,0:T(8,128)S(1)} custom-call(s32[1,16384]{1,0:T(1,128)S(1)} %bitcast.29, f32[2,1,16384]{2,1,0:T(1,128)S(1)} %copy-done.2, f32[2,64,16384]{2,1,0:T(8,128)} %proj_ref.3, s32[1,384]{1,0:T(1,128)S(1)} %reshape.158.owned_ref, bf16[512,1536]{1,0:T(8,128)(2,1)S(1)} %copy-done.1), custom_call_target="tpu_custom_call" | custom-call | tf_op jit(solution)/shard_map/spread_sticks/pallas_call | solution.py:186
  24.5 27.4 %all_to_all.16.recv_ref = f32[32,56,128]{2,1,0:T(8,128)S(1)} all-to-all(f32[32,56,128]{2,1,0:T(8,128)S(1)} %spread_sticks.1), channel_id=1, replica_groups=mesh['pw'=32,'band'=4] {'pw'}, dimensions={0} | all-to-all | bytes 1835008 | tf_op jit(solution)/shard_map/all_to_all | solution.py:485
  51.9 0.1 fusion.9
  52.1 0.1 reduce_min.18
  52.2 0.1 reduce_max.20
  52.4 0.1 select_reduce_fusion
  52.5 0.6 pad_add_fusion.range_ref
  53.1 52.5 %apply_field.1 = f32[32,48,128]{2,1,0:T(8,128)} custom-call(s32[4,24]{1,0:T(4,128)} %pad_add_fusion.range_ref, f32[32,56,128]{2,1,0:T(8,128)} %copy-done.6, f32[8,256,256]{2,1,0:T(8,128)} %field_ref.1, bf16[768,256]{1,0:T(8,128)(2,1)} %constant.70.clone.y_in_ref, bf16[768,256]{1,0:T(8,128)(2,1)} %constant.71.clone.y_out_ref, ...), custom_call_target="tpu_custom_call" | custom-call | tf_op jit(solution)/shard_map/apply_field/pallas_call | solution.py:353
  105.7 4.6 %all-to-all-start.1 = ((f32[32,48,128]{2,1,0:T(8,128)}), f32[32,48,128]{2,1,0:T(8,128)S(1)}, u32[]{:S(2)}, u32[]{:S(2)}) async-start(f32[32,48,128]{2,1,0:T(8,128)} %apply_field.1), calls=%async_computation.1 | async-start | bytes 1572864 | tf_op jit(solution)/shard_map/all_to_all | solution.py:488
  110.3 0.1 copy.36
  110.5 14.0 %all_gather.3 = f32[2,4,16384]{2,0,1:T(2,128)S(1)} all-gather(f32[2,1,16384]{2,0,1:T(2,128)S(1)} %copy.36), channel_id=1, replica_groups=mesh['pw'=32,'band'=4] {'band'}, dimensions={1}, use_global_device_ids=true | all-gather | bytes 655360 | tf_op jit(solution)/shard_map/all_gather | solution.py:483
  124.4 0.3 copy.38.all_ref
  124.9 1.0 slice_reduce_fusion
  125.9 0.1 multiply_reduce_fusion
  126.0 0.1 copy.39.coupled_ref
  126.1 21.2 %collect.1 = (f32[2,1,16384]{2,1,0:T(1,128)}, f32[4,4,128]{2,1,0:T(4,128)S(1)}) custom-call(s32[1,16384]{1,0:T(1,128)S(1)} %bitcast.30, f32[2,1,16384]{2,1,0:T(1,128)S(1)} %copy-done.3, f32[2,4,16384]{2,1,0:T(4,128)S(1)} %copy.38.all_ref, f32[2,64,16384]{2,1,0:T(8,128)} %proj_ref.3, f32[32,48,128]{2,1,0:T(8,128)S(1)} %all-to-all-done.1.recv_ref, ...), custom_call_target="tpu_custom_call" | custom-call | tf_op jit(solution)/shard_map/collect/pallas_call | solution.py:453
  147.3 0.1 slice_reduce_fusion.1
  147.5 18.2 %all_to_all.17 = f32[32,1,128]{2,1,0:T(1,128)S(1)} all-to-all(f32[32,1,128]{2,1,0:T(1,128)S(1)} %pad.7), channel_id=1, replica_groups=mesh['pw'=32,'band'=4] {'pw'}, dimensions={0} | all-to-all | bytes 32768 | tf_op jit(solution)/shard_map/all_to_all | solution.py:497
  165.9 0.6 slice.48
  166.5 0.6 slice.46
  (30 shorter events, 0.7 us)
Async XLA Ops:
  1.4 1.4 copy-start.1
  2.8 0.9 copy-start.2
  3.7 0.8 copy-start.4
  51.9 1.2 copy-start.6
  53.1 57.1 %copy-start.3 = (f32[2,1,16384]{2,1,0:T(1,128)S(1)}, f32[2,1,16384]{2,1,0:T(1,128)}, u32[]{:S(2)}) copy-start(f32[2,1,16384]{2,1,0:T(1,128)} %coef_ref.3) | copy-start | bytes 393220
  53.1 57.3 %copy-start.7 = (f32[64,64]{1,0:T(8,128)S(1)}, f32[64,64]{1,0:T(8,128)}, u32[]{:S(2)}) copy-start(f32[64,64]{1,0:T(8,128)} %param.19) | copy-start | bytes 49156
  105.7 19.1 %copy-start.8 = (s32[64]{0:T(128)S(1)}, s32[64]{0:T(128)}, u32[]{:S(2)}) copy-start(s32[64]{0:T(128)} %param.18) | copy-start | bytes 772
  105.7 20.5 %copy-start = (bf16[512,1536]{1,0:T(8,128)(2,1)S(1)}, bf16[512,1536]{1,0:T(8,128)(2,1)}, u32[]{:S(2)}) copy-start(bf16[512,1536]{1,0:T(8,128)(2,1)} %constant.74.clone.table_ref) | copy-start | bytes 4718596
  105.7 20.5 %copy-start.5 = (s32[16384]{0:T(1024)S(1)}, s32[16384]{0:T(1024)}, u32[]{:S(2)}) copy-start(s32[16384]{0:T(1024)} %param.16) | copy-start | bytes 196612
  105.7 20.4 %all-to-all-start.1 = ((f32[32,48,128]{2,1,0:T(8,128)}), f32[32,48,128]{2,1,0:T(8,128)S(1)}, u32[]{:S(2)}, u32[]{:S(2)}) async-start(f32[32,48,128]{2,1,0:T(8,128)} %apply_field.1), calls=%async_computation.1 | async-start | bytes 1572864 | tf_op jit(solution)/shard_map/all_to_all | solution.py:488

commit v3 on v2

--- a/solution.py
+++ b/solution.py
@@ -1,5 +1,3 @@
-import functools
-
 import jax
 import jax.numpy as jnp
 import ml_dtypes
@@ -21,13 +19,18 @@
 PROJ = 64
 PLANES = GZ // PW
 ROWS = 2 * PLANES
-KC = 1024
+KC = 2048
+WINDOW = 256
+SLOT_ROWS = 768
 TILES = STICKS // 128
 GROUPS = 24
 CHUNKS = 16
 NQ = 4
 NCH = 3
 PAIR = 2
+PLACE_UNROLL = 2
+PICK_UNROLL = 2
+GRAM_STEPS = 4
 F32 = jnp.float32
 BF16 = jnp.bfloat16
 NN = (((1,), (0,)), ((), ()))
@@ -105,10 +108,56 @@
     return lax.broadcasted_iota(jnp.int32, shape, dim).astype(F32)
 
 
-def slot_parts(slot):
-    slot = slot.astype(F32)
-    z = jnp.floor((slot + 0.5) * (1.0 / STICKS))
-    return z, slot - z * STICKS
+def sort_rows(keys, values):
+    keys = list(keys)
+    values = [list(each) for each in values]
+    sub = lax.broadcasted_iota(jnp.int32, (8, 128), 0)
+    size = 2
+    while size <= 128:
+        dist = size // 2
+        while dist >= 1:
+            if dist < 16:
+                for one in range(16):
+                    if one & dist:
+                        continue
+                    two = one | dist
+                    swap = keys[one] > keys[two]
+                    if size < 16:
+                        if one & size:
+                            swap = keys[one] < keys[two]
+                    elif size < 128:
+                        swap = jnp.where((sub & (size // 16)) == 0, keys[one] - keys[two], keys[two] - keys[one]) > 0.0
+                    for each in [keys] + values:
+                        each[one], each[two] = (jnp.where(swap, each[two], each[one]),
+                                                jnp.where(swap, each[one], each[two]))
+            else:
+                hop = dist // 16
+                low = (sub & hop) == 0
+                rising = (sub & (size // 16)) == 0 if size < 128 else jnp.full((8, 128), True)
+                least = jnp.where(low == rising, 1.0, -1.0)
+
+                def other(x):
+                    return jnp.where(low, pltpu.roll(x, 8 - hop, 0), pltpu.roll(x, hop, 0))
+
+                for one in range(16):
+                    swap = (keys[one] - other(keys[one])) * least > 0.0
+                    for each in [keys] + values:
+                        each[one] = jnp.where(swap, other(each[one]), each[one])
+            dist //= 2
+        size *= 2
+    return keys, values
+
+
+def sorted_row(ref, block):
+    at = pl.ds(block // 2, 1)
+    half = 8 * (block % 2)
+    return jnp.concatenate([ref[half + v, at, :] for v in range(8)], axis=1)
+
+
+def key_parts(key):
+    row = jnp.floor(key * (1.0 / 16384.0))
+    rest = key - row * 16384.0
+    return row, jnp.floor(rest * (1.0 / 128.0))
 
 
 def fold(x):
@@ -134,27 +183,72 @@
     return order, ordered
 
 
-def spread_kernel(slot_ref, coef_ref, proj_ref, owned_ref, table_ref, out_ref, acc, becp):
+def spread_kernel(slot_ref, tile_ref, coef_ref, proj_ref, owned_ref, table_ref, out_ref, key_ref, span_ref,
+                  part_re, part_im, acc, becp):
     step = pl.program_id(0)
 
     @pl.when(step == 0)
     def _():
+        slot = slot_ref[...].astype(F32)
+        z = jnp.floor((slot + 0.5) * (1.0 / STICKS))
+        s = slot - z * STICKS
+        tile = jnp.floor(s * (1.0 / 128.0))
+        place = (tile * 256.0 + z) * 128.0 + (s - tile * 128.0)
+        row = iota((128, 128), 0)
+        array = jnp.floor(row * 0.125)
+        key = place * 128.0 + (row - array * 8.0) * 16.0 + array
+
+        def rows(x):
+            return [x[v * 8:(v + 1) * 8] for v in range(16)]
+
+        keys, (real, imag) = sort_rows(rows(key), [rows(tile_ref[0]), rows(tile_ref[1])])
+        for v in range(16):
+            key_ref[v] = keys[v]
+            part_re[v] = real[v]
+            part_im[v] = imag[v]
+        for block in range(16):
+            half = 8 * (block % 2)
+            at = block // 2
+            first = jnp.min(key_parts(keys[half][at:at + 1])[0]).astype(jnp.int32)
+            last = jnp.max(key_parts(keys[half + 7][at:at + 1])[0]).astype(jnp.int32)
+            first = (first >> 4) << 4
+            span_ref[0, block] = first
+            span_ref[1, block] = ((last - first) >> 8) + 1
         acc[...] = jnp.zeros_like(acc)
         becp[...] = jnp.zeros_like(becp)
 
-    z, s = slot_parts(slot_ref[...])
+    none = jnp.zeros((), BF16)
+    lane_of = (iota((128, 1024), 0)).astype(BF16)
+    row_of = (iota((WINDOW, 1024), 0) - 128.0).astype(BF16)
+    for half in range(2):
+        block = step * 2 + half
+        at = pl.ds(step, 1)
+        key = jnp.concatenate([key_ref[8 * half + v, at, :] for v in range(8)], axis=1)
+        real = jnp.concatenate([part_re[8 * half + v, at, :] for v in range(8)], axis=1)
+        imag = jnp.concatenate([part_im[8 * half + v, at, :] for v in range(8)], axis=1)
+        row, lane = key_parts(key)
+        hit = lane_of == lane.astype(BF16)
+        re_hi, re_lo = split(real)
+        im_hi, im_lo = split(imag)
+        placed = jnp.concatenate([jnp.where(hit, part, none) for part in (re_hi, im_hi, re_lo, im_lo)], axis=0)
+
+        def add(first):
+            first = pl.multiple_of(first, 16)
+            want = row - (first + 128).astype(F32)
+            hot = jnp.where(row_of == want.astype(BF16), jnp.ones((), BF16), none)
+            acc[pl.ds(first, WINDOW), :] += mm(hot, placed, NT)
+
+        first = span_ref[0, block]
+        add(first)
+
+        def more(p, carry):
+            add(first + p * WINDOW)
+            return carry
+
+        lax.fori_loop(1, span_ref[1, block], more, 0)
+
     c_re = coef_ref[0]
     c_im = coef_ref[1]
-    re_hi, re_lo = split(c_re)
-    im_hi, im_lo = split(c_im)
-    z_hot = iota((GZ, KC), 0).astype(BF16) == z.astype(BF16)
-    none = jnp.zeros((), BF16)
-    placed = jnp.concatenate(
-        [jnp.where(z_hot, part, none) for part in (re_hi, im_hi, re_lo, im_lo)], axis=0)
-    s_hot = jnp.where(
-        (iota((STICKS, KC), 0) - 192.0).astype(BF16) == (s - 192.0).astype(BF16), jnp.ones((), BF16), none)
-    acc[...] += mm(s_hot, placed, NT)
-
     p_re = proj_ref[0]
     p_im = proj_ref[1]
     real = p_re * c_re + p_im * c_im
@@ -168,10 +262,13 @@
     @pl.when(step == pl.num_programs(0) - 1)
     def _():
         order, ordered = rank_of(owned_ref[...].astype(F32))
-        sticks = mm(order.astype(BF16), acc[...].astype(BF16)).astype(BF16)
-        high = sticks[:, :512]
-        low = sticks[:, 512:]
-        spread = mm(table_ref[...], jnp.concatenate([high, high, low], axis=1), NT)
+        sticks = jnp.concatenate(
+            [jnp.concatenate([acc[t * 256:(t + 1) * 256, part * 128:(part + 1) * 128] for t in range(TILES)], axis=1)
+             for part in range(4)], axis=0).astype(BF16)
+        sticks = mm(sticks, order.astype(BF16), NT).astype(BF16)
+        high = sticks[:512]
+        low = sticks[512:]
+        spread = mm(table_ref[...], jnp.concatenate([high, high, low], axis=0))
         spread = spread.reshape(PW, ROWS, STICKS)
         for t in range(TILES):
             out_ref[:, t * ROWS:(t + 1) * ROWS, :] = spread[:, :, t * 128:(t + 1) * 128]
@@ -187,18 +284,33 @@
         spread_kernel,
         grid=(COEFS // KC,),
         in_specs=[
-            pl.BlockSpec((1, KC), lambda i: (0, i)),
+            pl.BlockSpec((128, 128), lambda i: (0, 0)),
+            pl.BlockSpec((2, 128, 128), lambda i: (0, 0, 0)),
             pl.BlockSpec((2, 1, KC), lambda i: (0, 0, i)),
             pl.BlockSpec((2, PROJ, KC), lambda i: (0, 0, i)),
             pl.BlockSpec((1, STICKS), lambda i: (0, 0)),
             pl.BlockSpec((512, 1536), lambda i: (0, 0)),
         ],
-        out_specs=pl.BlockSpec((PW, 56, 128), lambda i: (0, 0, 0)),
-        out_shape=jax.ShapeDtypeStruct((PW, 56, 128), F32),
-        scratch_shapes=[pltpu.VMEM((STICKS, 1024), F32), pltpu.VMEM((128, 128), F32)],
+        out_specs=[
+            pl.BlockSpec((PW, 56, 128), lambda i: (0, 0, 0)),
+            pl.BlockSpec((16, 8, 128), lambda i: (0, 0, 0)),
+            pl.BlockSpec(memory_space=pltpu.SMEM),
+        ],
+        out_shape=[
+            jax.ShapeDtypeStruct((PW, 56, 128), F32),
+            jax.ShapeDtypeStruct((16, 8, 128), F32),
+            jax.ShapeDtypeStruct((2, 16), jnp.int32),
+        ],
+        scratch_shapes=[
+            pltpu.VMEM((16, 8, 128), F32),
+            pltpu.VMEM((16, 8, 128), F32),
+            pltpu.VMEM((SLOT_ROWS + WINDOW, 512), F32),
+            pltpu.VMEM((128, 128), F32),
+        ],
         compiler_params=pltpu.CompilerParams(vmem_limit_bytes=48 << 20),
+        cost_estimate=pl.CostEstimate(flops=6 * 10 ** 9, bytes_accessed=12 << 20, transcendentals=0),
         name="spread_sticks",
-    )(slot, coef, proj, owned, table)
+    )(slot, coef.reshape(2, 128, 128), coef, proj, owned, table)
 
 
 def swap_chunks(parts):
@@ -251,30 +363,35 @@
     step_of = iota((16, 512), 0)
     step_of = jnp.where(step_of < 8.0, step_of, step_of - 8.0)
 
-    def place(chunk, carry):
+    def place(chunk, first, groups):
         want = (step_of + (chunk * 8).astype(F32)).astype(BF16)
-        here = pl.ds(pl.multiple_of(chunk * 16, 16), 16)
-        start = range_ref[0, chunk]
-
-        def product(first):
-            masked = []
-            for j in range(NQ):
-                mine = jnp.where(keys[first + j] == want, signs[first + j], zero)
-                masked.append((wide[first + j] * mine[None]).reshape(2 * ROWS * 16, 512))
-            got = mm(jnp.concatenate(masked, axis=1),
-                     jnp.concatenate([hot[first + j] for j in range(NQ)], axis=1), NT)
-            got = got.reshape(2, ROWS, 16, 256)
-            return got[0] + got[1]
-
-        grid[:, here, :] = product(start)
-
+        masked = []
+        for j in range(groups):
+            mine = jnp.where(keys[first + j] == want, signs[first + j], zero)
+            masked.append((wide[first + j] * mine[None]).reshape(2 * ROWS * 16, 512))
+        got = mm(jnp.concatenate(masked, axis=1),
+                 jnp.concatenate([hot[first + j] for j in range(groups)], axis=1), NT)
+        got = got.reshape(2, ROWS, 16, 256)
+        return got[0] + got[1]
+
+    def rows_of(chunk):
+        return pl.ds(pl.multiple_of(chunk * 16, 16), 16)
+
+    def place_first(step, carry):
+        for at in range(PLACE_UNROLL):
+            chunk = step * PLACE_UNROLL + at
+            grid[:, rows_of(chunk), :] = place(chunk, range_ref[0, chunk], NQ)
+        return carry
+
+    def place_rest(chunk, carry):
         def more(p, inner):
-            grid[:, here, :] += product(start + p * NQ)
+            grid[:, rows_of(chunk), :] += place(chunk, range_ref[0, chunk] + p, 1)
             return inner
 
-        return lax.fori_loop(1, range_ref[1, chunk], more, carry)
-
-    lax.fori_loop(0, CHUNKS, place, 0)
+        return lax.fori_loop(NQ, range_ref[1, chunk], more, carry)
+
+    lax.fori_loop(0, CHUNKS // PLACE_UNROLL, place_first, 0)
+    lax.fori_loop(0, CHUNKS, place_rest, 0)
 
     row = lax.broadcasted_iota(jnp.int32, (256, 256), 0)
     lane = lax.broadcasted_iota(jnp.int32, (256, 256), 1)
@@ -313,33 +430,36 @@
 
     lax.fori_loop(0, PLANES // PAIR, planes, 0)
 
-    def pick(q, carry):
+    def pick(q, first, chunks):
         both = jnp.concatenate([hot[q], hot[q]], axis=0)
         key = keys[q].astype(F32)
         sign = signs[q].astype(F32)
-        start = range_ref[2, q]
-
-        def product(first):
-            here = pl.ds(pl.multiple_of(first * 16, 16), 16 * NCH)
-            lines = done[:, here, :].reshape(ROWS * 16 * NCH, 512)
-            got = mm(lines, both).reshape(ROWS, 2 * NCH, 8, 512)
-            total = None
-            for j in range(NCH):
-                want = step_of + ((first + j) * 8).astype(F32)
-                mine = jnp.where(key == want, sign, 0.0)
-                part = got[:, 2 * j] * mine[None, :8] + got[:, 2 * j + 1] * mine[None, 8:]
-                total = part if total is None else total + part
-            return jnp.sum(total, axis=1)
-
-        sticks[q] = product(start)
-
+        here = pl.ds(pl.multiple_of(first * 16, 16), 16 * chunks)
+        lines = done[:, here, :].reshape(ROWS * 16 * chunks, 512)
+        got = mm(lines, both).reshape(ROWS, 2 * chunks, 8, 512)
+        total = None
+        for j in range(chunks):
+            want = step_of + ((first + j) * 8).astype(F32)
+            mine = jnp.where(key == want, sign, 0.0)
+            part = got[:, 2 * j] * mine[None, :8] + got[:, 2 * j + 1] * mine[None, 8:]
+            total = part if total is None else total + part
+        return jnp.sum(total, axis=1)
+
+    def pick_first(step, carry):
+        for at in range(PICK_UNROLL):
+            q = step * PICK_UNROLL + at
+            sticks[q] = pick(q, range_ref[2, q], NCH)
+        return carry
+
+    def pick_rest(q, carry):
         def more(p, inner):
-            sticks[q] += product(start + p * NCH)
+            sticks[q] += pick(q, range_ref[2, q] + p, 1)
             return inner
 
-        return lax.fori_loop(1, range_ref[3, q], more, carry)
-
-    lax.fori_loop(0, GROUPS, pick, 0)
+        return lax.fori_loop(NCH, range_ref[3, q], more, carry)
+
+    lax.fori_loop(0, GROUPS // PICK_UNROLL, pick_first, 0)
+    lax.fori_loop(0, GROUPS, pick_rest, 0)
 
     for t in range(TILES):
         for g in range(4):
@@ -365,6 +485,7 @@
             pltpu.VMEM((GROUPS, ROWS, 512), F32),
         ],
         compiler_params=pltpu.CompilerParams(vmem_limit_bytes=56 << 20),
+        cost_estimate=pl.CostEstimate(flops=35 * 10 ** 9, bytes_accessed=8 << 20, transcendentals=0),
         name="apply_field",
     )(ranges, recv, field, *plane_tables())
 
@@ -378,125 +499,244 @@
     start = jnp.sum(jnp.where(last[None] < at, 1, 0), axis=1)
     end = jnp.sum(jnp.where(first[None] <= at, 1, 0), axis=1)
     start = jnp.minimum(start, GROUPS - 1)
-    return jnp.stack([start, (end - start + NQ - 1) // NQ, first, (last - first + NCH) // NCH])
+    return jnp.stack([start, end - start, first, last - first + 1])
 
 
 def centred(values, length):
     return jnp.where(values < length // 2, values, values - length)
 
 
-def collect_kernel(slot_ref, coef_ref, all_ref, proj_ref, recv_ref, owned_ref, coupled_ref, table_ref,
-                   out_ref, sums_ref, values, sums):
+def kinetic_kernel(slot_ref, coef_ref, all_ref, owned_ref, kinetic_ref, sums_ref):
+    slot = slot_ref[...].astype(F32)
+    z = jnp.floor((slot + 0.5) * (1.0 / STICKS))
+    s = slot - z * STICKS
+    tile = jnp.floor(s * (1.0 / 128.0))
+    lane = (s - tile * 128.0).astype(jnp.int32)
+    owned = owned_ref[...].astype(F32)
+    x = jnp.floor(owned * (1.0 / GY))
+    y = centred(owned - x * GY, GY)
+    x = centred(x, GX)
+    flat = x * x + y * y
+    square = jnp.zeros((128, 128), F32)
+    for t in range(TILES):
+        line = jnp.broadcast_to(flat[:, t * 128:(t + 1) * 128], (128, 128))
+        square = jnp.where(tile == t, jnp.take_along_axis(line, lane, axis=1), square)
+    z = centred(z, GZ)
+    kinetic = (square + z * z) * (KIN_MAX / 3.0 / 16384.0)
+    kinetic_ref[...] = kinetic
+    c_re = coef_ref[0]
+    c_im = coef_ref[1]
+    for a in range(4):
+        real = all_ref[a, 0] * c_re + all_ref[a, 1] * c_im
+        imag = all_ref[a, 0] * c_im - all_ref[a, 1] * c_re
+        for at, value in ((a, real * kinetic), (4 + a, imag * kinetic), (8 + a, real), (12 + a, imag)):
+            sums_ref[at:at + 1, :] = jnp.sum(value, axis=0, keepdims=True)
+
+
+def kinetic_part(slot, coef, everyone, owned):
+    vmem = pl.BlockSpec(memory_space=pltpu.VMEM)
+    return pl.pallas_call(
+        kinetic_kernel,
+        in_specs=[vmem] * 4,
+        out_specs=[vmem, vmem],
+        out_shape=[jax.ShapeDtypeStruct((128, 128), F32), jax.ShapeDtypeStruct((16, 128), F32)],
+        cost_estimate=pl.CostEstimate(flops=10 ** 6, bytes_accessed=1 << 20, transcendentals=0),
+        name="kinetic_part",
+    )(slot, coef, everyone, owned)
+
+
+def gram_kernel(sums_ref, all_ref, worked_ref, out_ref, total):
     step = pl.program_id(0)
 
     @pl.when(step == 0)
     def _():
-        sums[...] = jnp.zeros_like(sums)
-        owned = owned_ref[...].astype(F32)
-        order, _ = rank_of(owned)
-        order = order.astype(BF16)
-        lines = jnp.concatenate(
-            [recv_ref[:, t * ROWS:(t + 1) * ROWS, :].reshape(512, 128) for t in range(TILES)], axis=1)
-        high, low = split(lines)
-        back = mm(table_ref[...], jnp.concatenate([high, high, low], axis=0))
-        high, low = split(back)
-        values[:512, :STICKS] = mm(high, order).astype(BF16)
-        values[:512, STICKS:] = mm(low, order).astype(BF16)
-        x = jnp.floor(owned * (1.0 / GY))
-        y = centred(owned - x * GY, GY)
-        x = centred(x, GX)
-        square = x * x + y * y
-        upper = jnp.floor(square * (1.0 / 256.0))
-        lower = square - upper * 256.0
-        pair = jnp.concatenate([upper, lower, jnp.zeros((14, STICKS), F32)], axis=0)
-        values[512:, :STICKS] = pair.astype(BF16)
-        values[512:, STICKS:] = jnp.zeros((16, STICKS), BF16)
-
-    z, s = slot_parts(slot_ref[...])
-    none = jnp.zeros((), BF16)
-    s_hot = jnp.where(
-        (iota((STICKS, KC), 0) - 192.0).astype(BF16) == (s - 192.0).astype(BF16), jnp.ones((), BF16), none)
-    found = mm(values[...], jnp.concatenate([s_hot, s_hot], axis=0))
-    z_hot = iota((GZ, KC), 0) == z
-    scale = 1.0 / (GX * GY * GZ)
-    local_re = jnp.sum(jnp.where(z_hot, found[:256], 0.0), axis=0, keepdims=True) * scale
-    local_im = jnp.sum(jnp.where(z_hot, found[256:512], 0.0), axis=0, keepdims=True) * scale
-    z = centred(z, GZ)
-    square = found[512:513] * 256.0 + found[513:514] + z * z
-    kinetic = square * (KIN_MAX / 3.0 / 16384.0)
-    c_re = coef_ref[0]
-    c_im = coef_ref[1]
+        total[...] = jnp.zeros_like(total)
+
+    span = PW // GRAM_STEPS
+    here = pl.ds(pl.multiple_of(step * span, span), span)
+    worked = worked_ref[here].reshape(span * TILES, 2, PLANES, 128)
+    out_ref[here, :TILES * ROWS, :] = worked_ref[here]
+    w_re = worked[:, 0]
+    w_im = worked[:, 1]
+    for a in range(4):
+        lines = all_ref[a, :, :TILES * ROWS, :].reshape(span * TILES, 2, PLANES, 128)
+        a_re = lines[:, 0]
+        a_im = lines[:, 1]
+        total[a] += jnp.sum(a_re * w_re + a_im * w_im, axis=0)
+        total[4 + a] += jnp.sum(a_re * w_im - a_im * w_re, axis=0)
+
+    @pl.when(step == pl.num_programs(0) - 1)
+    def _():
+        scale = 1.0 / (GX * GY * GZ)
+        local_sums = jnp.concatenate(
+            [jnp.sum(total[a], axis=0, keepdims=True) for a in range(8)] + [jnp.zeros((8, 128), F32)], axis=0) * scale
+        lines = jnp.concatenate([local_sums + sums_ref[...], jnp.zeros((112, 128), F32)], axis=0)
+        line = jnp.sum(jnp.transpose(lines), axis=0, keepdims=True)
+        out_ref[:, TILES * ROWS:, :] = jnp.broadcast_to(line[None], (PW, 8, 128))
+
+
+def gram_part(sums, everyone, worked):
+    span = PW // GRAM_STEPS
+    return pl.pallas_call(
+        gram_kernel,
+        grid=(GRAM_STEPS,),
+        in_specs=[
+            pl.BlockSpec((16, 128), lambda i: (0, 0)),
+            pl.BlockSpec((4, span, 56, 128), lambda i: (0, i, 0, 0)),
+            pl.BlockSpec((PW, 48, 128), lambda i: (0, 0, 0)),
+        ],
+        out_specs=pl.BlockSpec((PW, 56, 128), lambda i: (0, 0, 0)),
+        out_shape=jax.ShapeDtypeStruct((PW, 56, 128), F32),
+        scratch_shapes=[pltpu.VMEM((8, PLANES, 128), F32)],
+        compiler_params=pltpu.CompilerParams(vmem_limit_bytes=32 << 20),
+        cost_estimate=pl.CostEstimate(flops=10 ** 7, bytes_accessed=6 << 20, transcendentals=0),
+        name="gram_part",
+    )(sums, everyone, worked)
+
+
+def base_kernel(kinetic_ref, coef_ref, proj_ref, coupled_ref, out_ref):
+    kinetic = kinetic_ref[...]
     p_re = proj_ref[0]
     p_im = proj_ref[1]
     w_re = coupled_ref[0]
     w_im = coupled_ref[1]
     far_re = jnp.sum(p_re * w_re - p_im * w_im, axis=0, keepdims=True)
     far_im = jnp.sum(p_re * w_im + p_im * w_re, axis=0, keepdims=True)
-    h_re = kinetic * c_re + local_re + far_re
-    h_im = kinetic * c_im + local_im + far_im
-    out_ref[0] = h_re
-    out_ref[1] = h_im
-    a_re = all_ref[0]
-    a_im = all_ref[1]
-    sums[0] += a_re * h_re + a_im * h_im
-    sums[1] += a_re * h_im - a_im * h_re
-    sums[2] += a_re * c_re + a_im * c_im
-    sums[3] += a_re * c_im - a_im * c_re
-
-    @pl.when(step == pl.num_programs(0) - 1)
-    def _():
-        sums_ref[...] = jnp.broadcast_to(jnp.sum(sums[...], axis=2, keepdims=True), (4, 4, 128))
-
-
-def collect(slot, coef, everyone, proj, recv, owned, coupled):
-    table = jnp.asarray(collect_table())
+    out_ref[0] = kinetic * coef_ref[0] + far_re
+    out_ref[1] = kinetic * coef_ref[1] + far_im
+
+
+def base_part(kinetic, coef, proj, coupled):
     return pl.pallas_call(
-        collect_kernel,
+        base_kernel,
         grid=(COEFS // KC,),
         in_specs=[
             pl.BlockSpec((1, KC), lambda i: (0, i)),
             pl.BlockSpec((2, 1, KC), lambda i: (0, 0, i)),
-            pl.BlockSpec((2, 4, KC), lambda i: (0, 0, i)),
             pl.BlockSpec((2, PROJ, KC), lambda i: (0, 0, i)),
-            pl.BlockSpec((PW, 48, 128), lambda i: (0, 0, 0)),
-            pl.BlockSpec((1, STICKS), lambda i: (0, 0)),
             pl.BlockSpec((2, PROJ, 1), lambda i: (0, 0, 0)),
-            pl.BlockSpec((512, 1536), lambda i: (0, 0)),
         ],
-        out_specs=[
-            pl.BlockSpec((2, 1, KC), lambda i: (0, 0, i)),
-            pl.BlockSpec((4, 4, 128), lambda i: (0, 0, 0)),
+        out_specs=pl.BlockSpec((2, 1, KC), lambda i: (0, 0, i)),
+        out_shape=jax.ShapeDtypeStruct((2, 1, COEFS), F32),
+        compiler_params=pltpu.CompilerParams(vmem_limit_bytes=32 << 20),
+        cost_estimate=pl.CostEstimate(flops=10 ** 7, bytes_accessed=10 << 20, transcendentals=0),
+        name="base_part",
+    )(kinetic, coef, proj, coupled)
+
+
+def collect_kernel(span_ref, key_ref, recv_ref, owned_ref, table_ref, base_ref, far_ref, out_ref, sums_ref,
+                   values, found_re, found_im):
+    sums_ref[...] = jnp.sum(recv_ref[:, TILES * ROWS:, :], axis=0) + far_ref[...]
+    order, _ = rank_of(owned_ref[...].astype(F32))
+    order = order.astype(BF16)
+    lines = jnp.concatenate(
+        [recv_ref[:, t * ROWS:(t + 1) * ROWS, :].reshape(512, 128) for t in range(TILES)], axis=1)
+    high, low = split(lines)
+    back = mm(table_ref[...], jnp.concatenate([high, high, low], axis=0))
+    for at, part in enumerate(split(back)):
+        part = mm(part, order).astype(BF16)
+        for ri in range(2):
+            for t in range(TILES):
+                values[ri, t * 256:(t + 1) * 256, at * 128:(at + 1) * 128] = part[
+                    ri * 256:(ri + 1) * 256, t * 128:(t + 1) * 128]
+    values[:, SLOT_ROWS:, :] = jnp.zeros((2, WINDOW, 256), BF16)
+
+    lane_of = iota((128, 1024), 0).astype(BF16)
+    row_of = iota((WINDOW, 1024), 0)
+
+    def one(step, carry):
+        at = pl.ds(step, 1)
+        for half in range(2):
+            block = step * 2 + half
+            key = jnp.concatenate([key_ref[8 * half + v, at, :] for v in range(8)], axis=1)
+            row, lane = key_parts(key)
+            hit = jnp.where(lane_of == lane.astype(BF16), jnp.ones((), BF16), jnp.zeros((), BF16))
+            hit = jnp.concatenate([hit, hit], axis=0)
+
+            def fetch(first):
+                first = pl.multiple_of(first, 16)
+                here = pl.ds(first, WINDOW)
+                got = mm(jnp.concatenate([values[0, here, :], values[1, here, :]], axis=0), hit)
+                mine = row_of == row - first.astype(F32)
+                return (jnp.sum(jnp.where(mine, got[:WINDOW], 0.0), axis=0, keepdims=True),
+                        jnp.sum(jnp.where(mine, got[WINDOW:], 0.0), axis=0, keepdims=True))
+
+            first = span_ref[0, block]
+
+            def put(pair):
+                for v in range(8):
+                    found_re[8 * half + v, at, :] = pair[0][:, v * 128:(v + 1) * 128]
+                    found_im[8 * half + v, at, :] = pair[1][:, v * 128:(v + 1) * 128]
+
+            def more(p, inner):
+                pair = fetch(first + p * WINDOW)
+                for v in range(8):
+                    found_re[8 * half + v, at, :] += pair[0][:, v * 128:(v + 1) * 128]
+                    found_im[8 * half + v, at, :] += pair[1][:, v * 128:(v + 1) * 128]
+                return inner
+
+            put(fetch(first))
+            lax.fori_loop(1, span_ref[1, block], more, 0)
+        return carry
+
+    lax.fori_loop(0, 8, one, 0)
+    scale = 1.0 / (GX * GY * GZ)
+    home = []
+    for v in range(16):
+        key = key_ref[v]
+        home.append(key - jnp.floor(key * (1.0 / 128.0)) * 128.0)
+    _, (real, imag) = sort_rows(home, [[found_re[v] for v in range(16)], [found_im[v] for v in range(16)]])
+    for v in range(16):
+        here = slice(v * 8, (v + 1) * 8)
+        out_ref[0, here, :] = base_ref[0, here, :] + real[v] * scale
+        out_ref[1, here, :] = base_ref[1, here, :] + imag[v] * scale
+
+
+def collect(span, key, recv, owned, base, far):
+    vmem = pl.BlockSpec(memory_space=pltpu.VMEM)
+    return pl.pallas_call(
+        collect_kernel,
+        in_specs=[pl.BlockSpec(memory_space=pltpu.SMEM)] + [vmem] * 6,
+        out_specs=[vmem, vmem],
+        out_shape=[jax.ShapeDtypeStruct((2, 128, 128), F32), jax.ShapeDtypeStruct((8, 128), F32)],
+        scratch_shapes=[
+            pltpu.VMEM((2, SLOT_ROWS + WINDOW, 256), BF16),
+            pltpu.VMEM((16, 8, 128), F32),
+            pltpu.VMEM((16, 8, 128), F32),
         ],
-        out_shape=[
-            jax.ShapeDtypeStruct((2, 1, COEFS), F32),
-            jax.ShapeDtypeStruct((4, 4, 128), F32),
-        ],
-        scratch_shapes=[pltpu.VMEM((528, 2 * STICKS), BF16), pltpu.VMEM((4, 4, KC), F32)],
         compiler_params=pltpu.CompilerParams(vmem_limit_bytes=48 << 20),
+        cost_estimate=pl.CostEstimate(flops=6 * 10 ** 9, bytes_accessed=4 << 20, transcendentals=0),
         name="collect",
-    )(slot, coef, everyone, proj, recv, owned, coupled, table)
+    )(span, key, recv, owned, jnp.asarray(collect_table()), base, far)
 
 
 def local(wave_coef, projector, potential, grid_slot, stick_column, proj_atom, coupling):
     owned = lax.dynamic_slice_in_dim(stick_column, lax.axis_index("pw") * STICKS, STICKS).reshape(1, STICKS)
-    slot = grid_slot.reshape(1, COEFS)
-    everyone = lax.all_gather(wave_coef, "band", axis=1, tiled=True)
-    sent = spread_sticks(slot, wave_coef, projector, owned)
+    slot = grid_slot.reshape(128, 128)
+    coef = wave_coef.reshape(2, 128, 128)
+    everyone = lax.all_gather(wave_coef.reshape(1, 2 * COEFS), "band", axis=0, tiled=True)
+    sent, key, span = spread_sticks(slot, wave_coef, projector, owned)
     recv = lax.all_to_all(sent, "pw", split_axis=0, concat_axis=0, tiled=True)
-
+    kinetic, sums = kinetic_part(slot, coef, everyone.reshape(4, 2, 128, 128), owned)
+
+    every_stick = lax.all_gather(recv, "band", axis=0)
     worked = apply_field(ranges_of(recv[:, 49:52, :].reshape(PW, STICKS)), recv, potential)
-    returned = lax.all_to_all(worked, "pw", split_axis=0, concat_axis=0, tiled=True)
+    payload = gram_part(sums, every_stick, worked)
+    returned = lax.all_to_all(payload, "pw", split_axis=0, concat_axis=0, tiled=True)
 
     becp = jnp.sum(recv[:, 48, :], axis=0).reshape(2, PROJ)
     same_atom = proj_atom[:, None] == proj_atom[None, :]
     matrix = jnp.where(same_atom, 0.5 * (coupling + coupling.T), 0.0)
     coupled = jnp.sum(matrix[None] * becp[:, None, :], axis=2, keepdims=True)
-    applied, sums = collect(slot, wave_coef, everyone, projector, returned, owned, coupled)
-    parts = jnp.broadcast_to(sums[:, :, 0].reshape(1, 16), (PW, 16))
-    parts = jnp.pad(parts, ((0, 0), (0, 112)))
-    total = jnp.sum(lax.all_to_all(parts, "pw", split_axis=0, concat_axis=0, tiled=True), axis=0)[:16]
-    total = total.reshape(2, 2, 4, 1)
-    return applied, total[0], total[1]
+    base = base_part(kinetic.reshape(1, COEFS), wave_coef, projector, coupled)
+    every_becp = jnp.sum(every_stick[:, :, 48, :], axis=1).reshape(4, 2, PROJ)
+    line = coupled.reshape(1, 2, PROJ)
+    far_re = jnp.sum(every_becp * line, axis=(1, 2))
+    far_im = jnp.sum(every_becp[:, 0] * line[:, 1] - every_becp[:, 1] * line[:, 0], axis=1)
+    far = jnp.concatenate([far_re, far_im, jnp.zeros((120,), F32)]).reshape(1, 128)
+    applied, total = collect(span, key, returned, owned, base.reshape(2, 128, 128), far)
+    total = total[0, :16].reshape(2, 2, 4, 1)
+    return applied.reshape(2, 1, COEFS), total[0], total[1]
 
 
 def solution(mesh):

time: 168 us -> 167 us (level)
  blocking collectives: 59.6 us -> 34.5 us
  waiting for transfers between devices: 0.01 us -> 15.9 us
  Pallas kernels: 93.6 us -> 78.1 us
  between operations: 0.76 us -> 14.2 us
  local copies, waits for them, and re-layouts: 6.38 us -> 13.4 us
  other arithmetic: 2.2 us -> 4.48 us
    all_to_all x1 -> x0, blocking collectives: 18.2 us -> none  [local(): lax.all_to_all(parts, 'pw', split_axis=0, concat_axis=0, tiled=True)]
    all_to_all x1, waiting for transfers between devices: 0.01 us -> 15.9 us  [local(): lax.all_to_all(payload, 'pw', split_axis=0, concat_axis=0, tiled=True)]
    unnamed x20 -> x31, local copies, waits for them, and re-layouts: 3.35 us -> 10.7 us
    pallas_call x1, Pallas kernels: 52.5 us -> 45.4 us  [apply_field(): pl.pallas_call(field_kernel, in_specs=[pl.BlockSpec(memory_space=pltpu.SM...]
    all_gather x1, blocking collectives: 14 us -> 7.37 us  [local(): lax.all_gather(wave_coef.reshape(1, 2 * COEFS), 'band', axis=0, tiled=True)]
    pallas_call x1, Pallas kernels: 19.9 us -> 14.3 us  [spread_sticks(): pl.pallas_call(spread_kernel, grid=(COEFS // KC,), in_specs=[pl.BlockSpec...]
    pallas_call x1 -> x4, Pallas kernels: 21.2 us -> 18.4 us  [the longest x1 10.9 us: collect(): pl.pallas_call(collect_kernel, in_specs=[pl.BlockSpec(memory_space=pltpu....]
  transfers between devices with their start and end apart: 1 -> 2, of which waited for: 0 -> 1; matrix products, arithmetic and copies ran while one was open for 1% -> 3% of each run, Pallas kernels for 0% -> 31%
where the time goes in v3:
time: 167 us; the launch traced here: 166 us
  Pallas kernels  78.1 us (47%)
  blocking collectives  34.5 us (21%)
  waiting for transfers between devices  15.9 us (10%)
  between operations  14.2 us (9%)
  local copies, waits for them, and re-layouts  13.4 us (8%)
  starting transfers between devices  5.12 us (3%)
  other arithmetic  4.48 us (3%)
    pallas_call x1, Pallas kernels, apply_field(): pl.pallas_call(field_kernel, in_specs=[pl.BlockSpec(memory_space=pltpu.SM...  45.4 us
    all_to_all x1, blocking collectives, local(): recv = lax.all_to_all(sent, 'pw', split_axis=0, concat_axis=0, tiled=True)  27.2 us
    all_to_all x1, waiting for transfers between devices, local(): lax.all_to_all(payload, 'pw', split_axis=0, concat_axis=0, tiled=True)  15.9 us
    pallas_call x1, Pallas kernels, spread_sticks(): pl.pallas_call(spread_kernel, grid=(COEFS // KC,), in_specs=[pl.BlockSpec...  14.3 us
    pallas_call x1, Pallas kernels, collect(): pl.pallas_call(collect_kernel, in_specs=[pl.BlockSpec(memory_space=pltpu....  10.9 us
    unnamed x31, local copies, waits for them, and re-layouts  10.7 us
    all_gather x1, blocking collectives, local(): lax.all_gather(wave_coef.reshape(1, 2 * COEFS), 'band', axis=0, tiled=True)  7.37 us
    all_to_all x1, starting transfers between devices, local(): lax.all_to_all(payload, 'pw', split_axis=0, concat_axis=0, tiled=True)  5.09 us
  transfers between devices with their start and end apart: 2, of which 1 were waited for; matrix products, arithmetic and copies ran while one was open for 3% of the time, Pallas kernels for 31%

profile of v3, /device:TPU:0, one launch (start us, length us, event | category | flops | bytes accessed | tf_op | source)
XLA Modules:
  0.0 165.7 jit_solution(13614868761532587944)
XLA Ops:
  7.2 0.8 dynamic_slice.3
  8.0 0.9 copy-done.2
  8.9 0.8 copy-done.7
  9.7 1.4 copy-done.12
  11.2 14.3 %spread_sticks.1 = (f32[32,56,128]{2,1,0:T(8,128)S(1)}, f32[16,8,128]{2,1,0:T(8,128)S(1)}, s32[2,16]{1,0:T(2,128)S(1)}) custom-call(s32[128,128]{1,0:T(8,128)S(1)} %bitcast.48, f32[2,128,128]{2,1,0:T(8,128)S(1)} %bitcast.43, f32[2,1,16384]{2,1,0:T(1,128)S(1)} %copy-done.2, f32[2,64,16384]{2,1,0:T(8,128)} %proj_ref.3, s32[1,384]{1,0:T(1,128)S(1)} %reshape.93.owned_ref, ...), custom_call_target="tpu_custom_call" | custom-call | flops 6000000000 | bytes 12582912 | tf_op jit(solution)/shard_map/spread_sticks/pallas_call | solution.py:283
  25.5 27.2 %all_to_all.10.recv_ref = f32[32,56,128]{2,1,0:T(8,128)} all-to-all(f32[32,56,128]{2,1,0:T(8,128)S(1)} %get-tuple-element.13), channel_id=1, replica_groups=mesh['pw'=32,'band'=4] {'pw'}, dimensions={0} | all-to-all | bytes 1835008 | tf_op jit(solution)/shard_map/all_to_all | solution.py:719
  52.8 7.4 %all-gather.1 = f32[4,1,32768]{2,1,0:T(1,128)} all-gather(f32[1,1,32768]{2,1,0:T(1,128)S(1)} %bitcast.44), channel_id=1, replica_groups=mesh['pw'=32,'band'=4] {'band'}, dimensions={0}, use_global_device_ids=true | all-gather | bytes 655360 | tf_op jit(solution)/shard_map/all_gather | solution.py:717
  60.2 2.1 %kinetic_part.1 = (f32[128,128]{1,0:T(8,128)}, f32[16,128]{1,0:T(8,128)}) custom-call(s32[128,128]{1,0:T(8,128)} %bitcast.47, f32[2,128,128]{2,1,0:T(8,128)} %bitcast.42, f32[4,2,128,128]{3,2,1,0:T(8,128)} %bitcast.49, s32[1,384]{1,0:T(1,128)} %copy-done.9), custom_call_target="tpu_custom_call" | custom-call | flops 1000000 | bytes 1048576 | tf_op jit(solution)/shard_map/kinetic_part/pallas_call | solution.py:538
  62.3 1.0 slice_reduce_fusion.1
  63.6 1.0 fusion.8
  65.1 3.5 %copy-done = f32[2,64,16384]{2,1,0:T(8,128)S(1)} copy-done((f32[2,64,16384]{2,1,0:T(8,128)S(1)}, f32[2,64,16384]{2,1,0:T(8,128)}, u32[]{:S(2)}) %copy-start) | copy-done | bytes 8388632
  68.5 0.8 copy-done.6
  69.4 3.4 %base_part.1 = f32[2,1,16384]{2,1,0:T(1,128)S(1)} custom-call(f32[1,16384]{1,0:T(1,128)S(1)} %bitcast.46, f32[2,1,16384]{2,1,0:T(1,128)S(1)} %copy-done.4, f32[2,64,16384]{2,1,0:T(8,128)S(1)} %copy-done, f32[2,64,1]{2,1,0:T(8,128)S(1)} %copy.42.coupled_ref), custom_call_target="tpu_custom_call" | custom-call | flops 10000000 | bytes 10485760 | tf_op jit(solution)/shard_map/base_part/pallas_call | solution.py:610
  73.0 0.6 pad_add_fusion.range_ref
  73.6 45.4 %apply_field.1.worked_ref = f32[32,48,128]{2,1,0:T(8,128)} custom-call(s32[4,24]{1,0:T(4,128)} %pad_add_fusion.range_ref, f32[32,56,128]{2,1,0:T(8,128)} %all_to_all.10.recv_ref, f32[8,256,256]{2,1,0:T(8,128)} %field_ref.1, bf16[768,256]{1,0:T(8,128)(2,1)} %constant.47.clone.y_in_ref, bf16[768,256]{1,0:T(8,128)(2,1)} %constant.48.clone.y_out_ref, ...), custom_call_target="tpu_custom_call" | custom-call | flops 35000000512 | bytes 8388608 | tf_op jit(solution)/shard_map/apply_field/pallas_call | solution.py:473
  119.0 2.0 %copy-done.1 = f32[128,56,128]{2,1,0:T(8,128)S(1)} copy-done((f32[128,56,128]{2,1,0:T(8,128)S(1)}, f32[128,56,128]{2,1,0:T(8,128)}, u32[]{:S(2)}) %copy-start.1) | copy-done | bytes 3670040
  121.0 1.1 copy-done.5
  122.2 1.9 %gram_part.1 = f32[32,56,128]{2,1,0:T(8,128)} custom-call(f32[16,128]{1,0:T(8,128)S(1)} %copy-done.8, f32[4,32,56,128]{3,2,1,0:T(8,128)S(1)} %bitcast.41, f32[32,48,128]{2,1,0:T(8,128)S(1)} %copy-done.5), custom_call_target="tpu_custom_call" | custom-call | flops 10000000 | bytes 6291456 | tf_op jit(solution)/shard_map/gram_part/pallas_call | solution.py:580
  124.1 5.1 %all-to-all-start.1 = ((f32[32,56,128]{2,1,0:T(8,128)}), f32[32,56,128]{2,1,0:T(8,128)S(1)}, u32[]{:S(2)}, u32[]{:S(2)}) async-start(f32[32,56,128]{2,1,0:T(8,128)} %gram_part.1), calls=%async_computation.1 | async-start | bytes 1835008 | tf_op jit(solution)/shard_map/all_to_all | solution.py:725
  129.2 1.1 slice_reduce_fusion
  130.7 15.9 %all-to-all-done.1.recv_ref = f32[32,56,128]{2,1,0:T(8,128)S(1)} async-done(((f32[32,56,128]{2,1,0:T(8,128)}), f32[32,56,128]{2,1,0:T(8,128)S(1)}, u32[]{:S(2)}, u32[]{:S(2)}) %all-to-all-start.1) | async-done | bytes 917536 | tf_op jit(solution)/shard_map/all_to_all | solution.py:725
  146.6 10.9 %collect.1 = (f32[2,128,128]{2,1,0:T(8,128)}, f32[8,128]{1,0:T(8,128)S(1)}) custom-call(s32[2,16]{1,0:T(2,128)S(1)} %get-tuple-element.10.span_ref, f32[16,8,128]{2,1,0:T(8,128)S(1)} %get-tuple-element.11.key_ref, f32[32,56,128]{2,1,0:T(8,128)S(1)} %all-to-all-done.1.recv_ref, s32[1,384]{1,0:T(1,128)S(1)} %copy-done.10, bf16[512,1536]{1,0:T(8,128)(2,1)S(1)} %copy-done.11, ...), custom_call_target="tpu_custom_call" | custom-call | flops 6000000000 | bytes 4194304 | tf_op jit(solution)/shard_map/collect/pallas_call | solution.py:697
  157.6 0.6 squeeze.18
  158.2 0.6 squeeze.19
  (49 shorter events, 1.6 us)
Async XLA Ops:
  7.2 111.8 %all-gather.4.cloned.1.call-start = ((), (), s32[]{:S(2)}) async-start(), calls=%async_computation.2 | async-start | bytes 4587520 | tf_op jit(solution)/shard_map/all_gather | solution.py:722
  8.0 17.5 %copy-start.9 = (s32[1,384]{1,0:T(1,128)}, s32[1,384]{1,0:T(1,128)S(1)}, u32[]{:S(2)}) copy-start(s32[1,384]{1,0:T(1,128)S(1)} %reshape.93.owned_ref) | copy-start | bytes 4612
  8.0 0.9 copy-start.2
  8.9 0.8 copy-start.7
  9.7 1.4 copy-start.12
  11.2 41.6 %copy-start.13 = (f32[64,64]{1,0:T(8,128)S(1)}, f32[64,64]{1,0:T(8,128)}, u32[]{:S(2)}) copy-start(f32[64,64]{1,0:T(8,128)} %param.19) | copy-start | bytes 49156
  11.2 41.6 %copy-start.3 = (f32[2,1,16384]{2,1,0:T(1,128)S(1)}, f32[2,1,16384]{2,1,0:T(1,128)}, u32[]{:S(2)}) copy-start(f32[2,1,16384]{2,1,0:T(1,128)} %coef_ref.3) | copy-start | bytes 393220
  25.5 36.8 %copy-start.14 = (s32[64]{0:T(128)S(1)}, s32[64]{0:T(128)}, u32[]{:S(2)}) copy-start(s32[64]{0:T(128)} %param.18) | copy-start | bytes 772
  25.5 39.6 %copy-start.4 = (f32[2,1,16384]{2,1,0:T(1,128)S(1)}, f32[2,1,16384]{2,1,0:T(1,128)}, u32[]{:S(2)}) copy-start(f32[2,1,16384]{2,1,0:T(1,128)} %coef_ref.3) | copy-start | bytes 393220
  65.1 3.5 %copy-start = (f32[2,64,16384]{2,1,0:T(8,128)S(1)}, f32[2,64,16384]{2,1,0:T(8,128)}, u32[]{:S(2)}) copy-start(f32[2,64,16384]{2,1,0:T(8,128)} %proj_ref.3) | copy-start | bytes 25165828
  68.5 0.8 copy-start.6
  73.6 45.4 %copy-start.8 = (f32[16,128]{1,0:T(8,128)S(1)}, f32[16,128]{1,0:T(8,128)}, u32[]{:S(2)}) copy-start(f32[16,128]{1,0:T(8,128)} %get-tuple-element.12.sums_ref) | copy-start | bytes 24580
  73.6 73.0 %copy-start.11 = (bf16[512,1536]{1,0:T(8,128)(2,1)S(1)}, bf16[512,1536]{1,0:T(8,128)(2,1)}, u32[]{:S(2)}) copy-start(bf16[512,1536]{1,0:T(8,128)(2,1)} %constant.51.clone.table_ref) | copy-start | bytes 4718596
  119.0 27.6 %copy-start.10 = (s32[1,384]{1,0:T(1,128)S(1)}, s32[1,384]{1,0:T(1,128)}, u32[]{:S(2)}) copy-start(s32[1,384]{1,0:T(1,128)} %copy-done.9) | copy-start | bytes 4612
  119.0 2.0 %copy-start.1 = (f32[128,56,128]{2,1,0:T(8,128)S(1)}, f32[128,56,128]{2,1,0:T(8,128)}, u32[]{:S(2)}) copy-start(f32[128,56,128]{2,1,0:T(8,128)} %all-gather.4.cloned.1.call-done) | copy-start | bytes 11010052
  121.0 1.1 copy-start.5
  124.1 22.5 %all-to-all-start.1 = ((f32[32,56,128]{2,1,0:T(8,128)}), f32[32,56,128]{2,1,0:T(8,128)S(1)}, u32[]{:S(2)}, u32[]{:S(2)}) async-start(f32[32,56,128]{2,1,0:T(8,128)} %gram_part.1), calls=%async_computation.1 | async-start | bytes 1835008 | tf_op jit(solution)/shard_map/all_to_all | solution.py:725
Sparse Core Ops, SparseCore 0:
  52.8 38.2 all-gather.3

commit v4 on v3

--- a/solution.py
+++ b/solution.py
@@ -28,8 +28,8 @@
 NQ = 4
 NCH = 3
 PAIR = 2
-PLACE_UNROLL = 2
-PICK_UNROLL = 2
+PLACE_UNROLL = 4
+PICK_UNROLL = 4
 GRAM_STEPS = 4
 F32 = jnp.float32
 BF16 = jnp.bfloat16
@@ -183,8 +183,30 @@
     return order, ordered
 
 
-def spread_kernel(slot_ref, tile_ref, coef_ref, proj_ref, owned_ref, table_ref, out_ref, key_ref, span_ref,
-                  part_re, part_im, acc, becp):
+def centred(values, length):
+    return jnp.where(values < length // 2, values, values - length)
+
+
+def owned_row(stick_ref):
+    first = lax.axis_index("pw") * TILES
+    return jnp.concatenate([stick_ref[pl.ds(first + t, 1), :] for t in range(TILES)], axis=1).astype(F32)
+
+
+def kinetic_of(z, tile, lane, owned):
+    x = jnp.floor(owned * (1.0 / GY))
+    y = centred(owned - x * GY, GY)
+    x = centred(x, GX)
+    flat = x * x + y * y
+    square = jnp.zeros((128, 128), F32)
+    for t in range(TILES):
+        line = jnp.broadcast_to(flat[:, t * 128:(t + 1) * 128], (128, 128))
+        square = jnp.where(tile == t, jnp.take_along_axis(line, lane.astype(jnp.int32), axis=1), square)
+    z = centred(z, GZ)
+    return (square + z * z) * (KIN_MAX / 3.0 / 16384.0)
+
+
+def spread_kernel(slot_ref, tile_ref, coef_ref, proj_ref, stick_ref, table_ref, out_ref, key_ref, kinetic_ref,
+                  span_ref, part_re, part_im, acc, becp):
     step = pl.program_id(0)
 
     @pl.when(step == 0)
@@ -193,7 +215,15 @@
         z = jnp.floor((slot + 0.5) * (1.0 / STICKS))
         s = slot - z * STICKS
         tile = jnp.floor(s * (1.0 / 128.0))
-        place = (tile * 256.0 + z) * 128.0 + (s - tile * 128.0)
+        lane = s - tile * 128.0
+        place = (tile * 256.0 + z) * 128.0 + lane
+        kinetic = kinetic_of(z, tile, lane, owned_row(stick_ref))
+        kinetic_ref[...] = kinetic
+        for d in range(PW):
+            here = slice(d * 4, d * 4 + 4)
+            out_ref[d, 52:56, :] = kinetic[here]
+            out_ref[d, 56:60, :] = tile_ref[0, here, :]
+            out_ref[d, 60:64, :] = tile_ref[1, here, :]
         row = iota((128, 128), 0)
         array = jnp.floor(row * 0.125)
         key = place * 128.0 + (row - array * 8.0) * 16.0 + array
@@ -261,7 +291,7 @@
 
     @pl.when(step == pl.num_programs(0) - 1)
     def _():
-        order, ordered = rank_of(owned_ref[...].astype(F32))
+        order, ordered = rank_of(owned_row(stick_ref))
         sticks = jnp.concatenate(
             [jnp.concatenate([acc[t * 256:(t + 1) * 256, part * 128:(part + 1) * 128] for t in range(TILES)], axis=1)
              for part in range(4)], axis=0).astype(BF16)
@@ -274,11 +304,11 @@
             out_ref[:, t * ROWS:(t + 1) * ROWS, :] = spread[:, :, t * 128:(t + 1) * 128]
         line = jnp.sum(jnp.transpose(becp[...]), axis=0, keepdims=True)
         extra = jnp.concatenate(
-            [line] + [ordered[:, t * 128:(t + 1) * 128] for t in range(TILES)] + [jnp.zeros((4, 128), F32)], axis=0)
-        out_ref[:, TILES * ROWS:, :] = jnp.broadcast_to(extra[None], (PW, 8, 128))
-
-
-def spread_sticks(slot, coef, proj, owned):
+            [line] + [ordered[:, t * 128:(t + 1) * 128] for t in range(TILES)], axis=0)
+        out_ref[:, TILES * ROWS:TILES * ROWS + 4, :] = jnp.broadcast_to(extra[None], (PW, 4, 128))
+
+
+def spread_sticks(slot, coef, proj, stick):
     table = jnp.asarray(spread_table())
     return pl.pallas_call(
         spread_kernel,
@@ -288,17 +318,19 @@
             pl.BlockSpec((2, 128, 128), lambda i: (0, 0, 0)),
             pl.BlockSpec((2, 1, KC), lambda i: (0, 0, i)),
             pl.BlockSpec((2, PROJ, KC), lambda i: (0, 0, i)),
-            pl.BlockSpec((1, STICKS), lambda i: (0, 0)),
+            pl.BlockSpec((PW * TILES, 128), lambda i: (0, 0)),
             pl.BlockSpec((512, 1536), lambda i: (0, 0)),
         ],
         out_specs=[
-            pl.BlockSpec((PW, 56, 128), lambda i: (0, 0, 0)),
+            pl.BlockSpec((PW, 64, 128), lambda i: (0, 0, 0)),
             pl.BlockSpec((16, 8, 128), lambda i: (0, 0, 0)),
+            pl.BlockSpec((128, 128), lambda i: (0, 0)),
             pl.BlockSpec(memory_space=pltpu.SMEM),
         ],
         out_shape=[
-            jax.ShapeDtypeStruct((PW, 56, 128), F32),
+            jax.ShapeDtypeStruct((PW, 64, 128), F32),
             jax.ShapeDtypeStruct((16, 8, 128), F32),
+            jax.ShapeDtypeStruct((128, 128), F32),
             jax.ShapeDtypeStruct((2, 16), jnp.int32),
         ],
         scratch_shapes=[
@@ -307,10 +339,10 @@
             pltpu.VMEM((SLOT_ROWS + WINDOW, 512), F32),
             pltpu.VMEM((128, 128), F32),
         ],
-        compiler_params=pltpu.CompilerParams(vmem_limit_bytes=48 << 20),
+        compiler_params=pltpu.CompilerParams(vmem_limit_bytes=60 << 20),
         cost_estimate=pl.CostEstimate(flops=6 * 10 ** 9, bytes_accessed=12 << 20, transcendentals=0),
         name="spread_sticks",
-    )(slot, coef.reshape(2, 128, 128), coef, proj, owned, table)
+    )(slot, coef.reshape(2, 128, 128), coef, proj, stick, table)
 
 
 def swap_chunks(parts):
@@ -327,12 +359,37 @@
     return parts
 
 
-def field_kernel(range_ref, recv_ref, field_ref, y_in_ref, y_out_ref, x_in_ref, x_out_ref, out_ref,
-                 wide, hot, keys, signs, grid, done, sticks):
+def write_bounds(columns, bounds):
+    firsts, lasts = [], []
+    for column in columns:
+        chunk = jnp.floor(fold(jnp.floor(column * (1.0 / GY)))[0] * 0.125)
+        firsts.append(jnp.min(chunk, axis=1, keepdims=True))
+        lasts.append(jnp.max(chunk, axis=1, keepdims=True))
+    first = jnp.broadcast_to(jnp.concatenate(firsts, axis=0), (GROUPS, 128))
+    last = jnp.broadcast_to(jnp.concatenate(lasts, axis=0), (GROUPS, 128))
+    lane = iota((GROUPS, 128), 1)
+    start = jnp.sum(jnp.where(last < lane, 1.0, 0.0), axis=0, keepdims=True)
+    end = jnp.sum(jnp.where(first <= lane, 1.0, 0.0), axis=0, keepdims=True)
+    more = jnp.zeros((128 - GROUPS, 128), F32)
+    first = jnp.transpose(jnp.concatenate([first, more], axis=0))[:1]
+    last = jnp.transpose(jnp.concatenate([last, more], axis=0))[:1]
+    lines = [jnp.minimum(start, GROUPS - 1.0), end - start, first, last - first + 1.0, jnp.zeros((4, 128), F32)]
+    bounds[...] = jnp.concatenate(lines, axis=0).astype(jnp.int32)
+
+
+def field_kernel(recv_ref, field_hbm, y_in_ref, y_out_ref, x_in_ref, x_out_ref, out_ref,
+                 wide, hot, keys, signs, grid, done, sticks, field_ref, bounds, range_ref, field_sem, range_sem):
+    field_copy = pltpu.make_async_copy(field_hbm, field_ref, field_sem)
+    field_copy.start()
     cells = []
     for g in range(4):
-        mixed = swap_chunks([recv_ref[g * 8 + i, TILES * ROWS:, :] for i in range(8)])
+        mixed = swap_chunks([recv_ref[g * 8 + i, TILES * ROWS:TILES * ROWS + 8, :] for i in range(8)])
         cells.append(mixed)
+    columns = [jnp.concatenate([cells[g][q % 8][1 + q // 8:2 + q // 8] for g in range(4)], axis=1)
+               for q in range(GROUPS)]
+    write_bounds(columns, bounds)
+    range_copy = pltpu.make_async_copy(bounds, range_ref, range_sem)
+    range_copy.start()
     one_hot = iota((128, 512), 0).astype(BF16)
     zero = jnp.zeros((), BF16)
     for t in range(TILES):
@@ -343,7 +400,7 @@
             high, low = split(values)
             both = jnp.concatenate([high.astype(F32), low.astype(F32)], axis=0)
             wide[q] = jnp.broadcast_to(both[:, None, :], (2 * ROWS, 16, 512)).astype(BF16)
-            column = jnp.concatenate([cells[g][c][1 + t:2 + t] for g in range(4)], axis=1)
+            column = columns[q]
             x = jnp.floor(column * (1.0 / GY))
             y = column - x * GY
             _, even, odd, sign = fold(x)
@@ -390,6 +447,7 @@
 
         return lax.fori_loop(NQ, range_ref[1, chunk], more, carry)
 
+    range_copy.wait()
     lax.fori_loop(0, CHUNKS // PLACE_UNROLL, place_first, 0)
     lax.fori_loop(0, CHUNKS, place_rest, 0)
 
@@ -428,6 +486,7 @@
             plane(pair * PAIR + at)
         return carry
 
+    field_copy.wait()
     lax.fori_loop(0, PLANES // PAIR, planes, 0)
 
     def pick(q, first, chunks):
@@ -468,11 +527,11 @@
                 out_ref[g * 8 + i, t * ROWS:(t + 1) * ROWS, :] = mixed[i]
 
 
-def apply_field(ranges, recv, field):
+def apply_field(recv, field):
     vmem = pl.BlockSpec(memory_space=pltpu.VMEM)
     return pl.pallas_call(
         field_kernel,
-        in_specs=[pl.BlockSpec(memory_space=pltpu.SMEM)] + [vmem] * 6,
+        in_specs=[vmem, pl.BlockSpec(memory_space=pl.ANY)] + [vmem] * 4,
         out_specs=vmem,
         out_shape=jax.ShapeDtypeStruct((PW, 48, 128), F32),
         scratch_shapes=[
@@ -483,115 +542,80 @@
             pltpu.VMEM((ROWS, GX, GY), F32),
             pltpu.VMEM((ROWS, GX + 16 * (NCH - 1), 512), BF16),
             pltpu.VMEM((GROUPS, ROWS, 512), F32),
+            pltpu.VMEM((PLANES, GX, GY), F32),
+            pltpu.VMEM((8, 128), jnp.int32),
+            pltpu.SMEM((8, 128), jnp.int32),
+            pltpu.SemaphoreType.DMA,
+            pltpu.SemaphoreType.DMA,
         ],
-        compiler_params=pltpu.CompilerParams(vmem_limit_bytes=56 << 20),
+        compiler_params=pltpu.CompilerParams(vmem_limit_bytes=60 << 20),
         cost_estimate=pl.CostEstimate(flops=35 * 10 ** 9, bytes_accessed=8 << 20, transcendentals=0),
         name="apply_field",
-    )(ranges, recv, field, *plane_tables())
-
-
-def ranges_of(columns):
-    chunk = jnp.floor(fold(jnp.floor(columns * (1.0 / GY)))[0] * 0.125).astype(jnp.int32)
-    chunk = chunk.reshape(PW, GROUPS, 16)
-    first = jnp.min(chunk, axis=(0, 2))
-    last = jnp.max(chunk, axis=(0, 2))
-    at = jnp.arange(GROUPS, dtype=jnp.int32)[:, None]
-    start = jnp.sum(jnp.where(last[None] < at, 1, 0), axis=1)
-    end = jnp.sum(jnp.where(first[None] <= at, 1, 0), axis=1)
-    start = jnp.minimum(start, GROUPS - 1)
-    return jnp.stack([start, end - start, first, last - first + 1])
-
-
-def centred(values, length):
-    return jnp.where(values < length // 2, values, values - length)
-
-
-def kinetic_kernel(slot_ref, coef_ref, all_ref, owned_ref, kinetic_ref, sums_ref):
-    slot = slot_ref[...].astype(F32)
-    z = jnp.floor((slot + 0.5) * (1.0 / STICKS))
-    s = slot - z * STICKS
-    tile = jnp.floor(s * (1.0 / 128.0))
-    lane = (s - tile * 128.0).astype(jnp.int32)
-    owned = owned_ref[...].astype(F32)
-    x = jnp.floor(owned * (1.0 / GY))
-    y = centred(owned - x * GY, GY)
-    x = centred(x, GX)
-    flat = x * x + y * y
-    square = jnp.zeros((128, 128), F32)
-    for t in range(TILES):
-        line = jnp.broadcast_to(flat[:, t * 128:(t + 1) * 128], (128, 128))
-        square = jnp.where(tile == t, jnp.take_along_axis(line, lane, axis=1), square)
-    z = centred(z, GZ)
-    kinetic = (square + z * z) * (KIN_MAX / 3.0 / 16384.0)
-    kinetic_ref[...] = kinetic
-    c_re = coef_ref[0]
-    c_im = coef_ref[1]
-    for a in range(4):
-        real = all_ref[a, 0] * c_re + all_ref[a, 1] * c_im
-        imag = all_ref[a, 0] * c_im - all_ref[a, 1] * c_re
-        for at, value in ((a, real * kinetic), (4 + a, imag * kinetic), (8 + a, real), (12 + a, imag)):
-            sums_ref[at:at + 1, :] = jnp.sum(value, axis=0, keepdims=True)
-
-
-def kinetic_part(slot, coef, everyone, owned):
-    vmem = pl.BlockSpec(memory_space=pltpu.VMEM)
-    return pl.pallas_call(
-        kinetic_kernel,
-        in_specs=[vmem] * 4,
-        out_specs=[vmem, vmem],
-        out_shape=[jax.ShapeDtypeStruct((128, 128), F32), jax.ShapeDtypeStruct((16, 128), F32)],
-        cost_estimate=pl.CostEstimate(flops=10 ** 6, bytes_accessed=1 << 20, transcendentals=0),
-        name="kinetic_part",
-    )(slot, coef, everyone, owned)
-
-
-def gram_kernel(sums_ref, all_ref, worked_ref, out_ref, total):
+    )(recv, field, *plane_tables())
+
+
+def gram_kernel(own_ref, one_ref, two_ref, three_ref, worked_ref, out_ref, becp_ref, total, small):
     step = pl.program_id(0)
 
     @pl.when(step == 0)
     def _():
         total[...] = jnp.zeros_like(total)
+        small[...] = jnp.zeros_like(small)
+        becp_ref[...] = jnp.zeros_like(becp_ref)
 
     span = PW // GRAM_STEPS
     here = pl.ds(pl.multiple_of(step * span, span), span)
-    worked = worked_ref[here].reshape(span * TILES, 2, PLANES, 128)
-    out_ref[here, :TILES * ROWS, :] = worked_ref[here]
+    worked = worked_ref[...].reshape(span * TILES, 2, PLANES, 128)
+    out_ref[here, :TILES * ROWS, :] = worked_ref[...]
     w_re = worked[:, 0]
     w_im = worked[:, 1]
-    for a in range(4):
-        lines = all_ref[a, :, :TILES * ROWS, :].reshape(span * TILES, 2, PLANES, 128)
+    upper = lax.broadcasted_iota(jnp.int32, (span * 8, 128), 0) % 8 < 4
+    mine = own_ref[:, 56:, :].reshape(span * 8, 128)
+    weight = own_ref[:, 48:56, :].reshape(span * 8, 128)
+
+    def halves(x):
+        return pltpu.roll(x.reshape(span, 8, 128), 4, 1).reshape(span * 8, 128)
+
+    turned = jnp.where(upper, halves(mine), -halves(mine))
+    weight = jnp.where(upper, halves(weight), weight)
+    for a, ref in enumerate((own_ref, one_ref, two_ref, three_ref)):
+        lines = ref[:, :TILES * ROWS, :].reshape(span * TILES, 2, PLANES, 128)
         a_re = lines[:, 0]
         a_im = lines[:, 1]
         total[a] += jnp.sum(a_re * w_re + a_im * w_im, axis=0)
         total[4 + a] += jnp.sum(a_re * w_im - a_im * w_re, axis=0)
+        becp_ref[a] += jnp.sum(ref[:, 48:56, :], axis=0)
+        coef = ref[:, 56:, :].reshape(span * 8, 128)
+        real = coef * mine
+        imag = coef * turned
+        for at, value in ((a, real * weight), (4 + a, imag * weight), (8 + a, real), (12 + a, imag)):
+            small[at] += jnp.sum(value.reshape(span, 8, 128), axis=0)
 
     @pl.when(step == pl.num_programs(0) - 1)
     def _():
         scale = 1.0 / (GX * GY * GZ)
-        local_sums = jnp.concatenate(
-            [jnp.sum(total[a], axis=0, keepdims=True) for a in range(8)] + [jnp.zeros((8, 128), F32)], axis=0) * scale
-        lines = jnp.concatenate([local_sums + sums_ref[...], jnp.zeros((112, 128), F32)], axis=0)
+        lines = [jnp.sum(small[at] + total[at] * scale, axis=0, keepdims=True) for at in range(8)]
+        lines += [jnp.sum(small[at], axis=0, keepdims=True) for at in range(8, 16)]
+        lines = jnp.concatenate(lines + [jnp.zeros((112, 128), F32)], axis=0)
         line = jnp.sum(jnp.transpose(lines), axis=0, keepdims=True)
         out_ref[:, TILES * ROWS:, :] = jnp.broadcast_to(line[None], (PW, 8, 128))
 
 
-def gram_part(sums, everyone, worked):
+def gram_part(recv, others, worked):
     span = PW // GRAM_STEPS
     return pl.pallas_call(
         gram_kernel,
         grid=(GRAM_STEPS,),
-        in_specs=[
-            pl.BlockSpec((16, 128), lambda i: (0, 0)),
-            pl.BlockSpec((4, span, 56, 128), lambda i: (0, i, 0, 0)),
-            pl.BlockSpec((PW, 48, 128), lambda i: (0, 0, 0)),
+        in_specs=[pl.BlockSpec((span, 64, 128), lambda i: (i, 0, 0))] * 4 + [
+            pl.BlockSpec((span, 48, 128), lambda i: (i, 0, 0)),
         ],
-        out_specs=pl.BlockSpec((PW, 56, 128), lambda i: (0, 0, 0)),
-        out_shape=jax.ShapeDtypeStruct((PW, 56, 128), F32),
-        scratch_shapes=[pltpu.VMEM((8, PLANES, 128), F32)],
-        compiler_params=pltpu.CompilerParams(vmem_limit_bytes=32 << 20),
+        out_specs=[pl.BlockSpec((PW, 56, 128), lambda i: (0, 0, 0)), pl.BlockSpec((4, 8, 128), lambda i: (0, 0, 0))],
+        out_shape=[jax.ShapeDtypeStruct((PW, 56, 128), F32), jax.ShapeDtypeStruct((4, 8, 128), F32)],
+        scratch_shapes=[pltpu.VMEM((8, PLANES, 128), F32), pltpu.VMEM((16, 8, 128), F32)],
+        compiler_params=pltpu.CompilerParams(vmem_limit_bytes=60 << 20),
         cost_estimate=pl.CostEstimate(flops=10 ** 7, bytes_accessed=6 << 20, transcendentals=0),
         name="gram_part",
-    )(sums, everyone, worked)
+    )(recv, *others, worked)
 
 
 def base_kernel(kinetic_ref, coef_ref, proj_ref, coupled_ref, out_ref):
@@ -618,16 +642,16 @@
         ],
         out_specs=pl.BlockSpec((2, 1, KC), lambda i: (0, 0, i)),
         out_shape=jax.ShapeDtypeStruct((2, 1, COEFS), F32),
-        compiler_params=pltpu.CompilerParams(vmem_limit_bytes=32 << 20),
+        compiler_params=pltpu.CompilerParams(vmem_limit_bytes=60 << 20),
         cost_estimate=pl.CostEstimate(flops=10 ** 7, bytes_accessed=10 << 20, transcendentals=0),
         name="base_part",
     )(kinetic, coef, proj, coupled)
 
 
-def collect_kernel(span_ref, key_ref, recv_ref, owned_ref, table_ref, base_ref, far_ref, out_ref, sums_ref,
+def collect_kernel(span_ref, key_ref, recv_ref, stick_ref, table_ref, base_ref, far_ref, out_ref, sums_ref,
                    values, found_re, found_im):
     sums_ref[...] = jnp.sum(recv_ref[:, TILES * ROWS:, :], axis=0) + far_ref[...]
-    order, _ = rank_of(owned_ref[...].astype(F32))
+    order, _ = rank_of(owned_row(stick_ref))
     order = order.astype(BF16)
     lines = jnp.concatenate(
         [recv_ref[:, t * ROWS:(t + 1) * ROWS, :].reshape(512, 128) for t in range(TILES)], axis=1)
@@ -692,7 +716,7 @@
         out_ref[1, here, :] = base_ref[1, here, :] + imag[v] * scale
 
 
-def collect(span, key, recv, owned, base, far):
+def collect(span, key, recv, stick, base, far):
     vmem = pl.BlockSpec(memory_space=pltpu.VMEM)
     return pl.pallas_call(
         collect_kernel,
@@ -704,38 +728,35 @@
             pltpu.VMEM((16, 8, 128), F32),
             pltpu.VMEM((16, 8, 128), F32),
         ],
-        compiler_params=pltpu.CompilerParams(vmem_limit_bytes=48 << 20),
+        compiler_params=pltpu.CompilerParams(vmem_limit_bytes=60 << 20),
         cost_estimate=pl.CostEstimate(flops=6 * 10 ** 9, bytes_accessed=4 << 20, transcendentals=0),
         name="collect",
-    )(span, key, recv, owned, jnp.asarray(collect_table()), base, far)
+    )(span, key, recv, stick, jnp.asarray(collect_table()), base, far)
 
 
 def local(wave_coef, projector, potential, grid_slot, stick_column, proj_atom, coupling):
-    owned = lax.dynamic_slice_in_dim(stick_column, lax.axis_index("pw") * STICKS, STICKS).reshape(1, STICKS)
-    slot = grid_slot.reshape(128, 128)
-    coef = wave_coef.reshape(2, 128, 128)
-    everyone = lax.all_gather(wave_coef.reshape(1, 2 * COEFS), "band", axis=0, tiled=True)
-    sent, key, span = spread_sticks(slot, wave_coef, projector, owned)
+    stick = stick_column.reshape(PW * TILES, 128)
+    sent, key, kinetic, span = spread_sticks(grid_slot.reshape(128, 128), wave_coef, projector, stick)
     recv = lax.all_to_all(sent, "pw", split_axis=0, concat_axis=0, tiled=True)
-    kinetic, sums = kinetic_part(slot, coef, everyone.reshape(4, 2, 128, 128), owned)
-
-    every_stick = lax.all_gather(recv, "band", axis=0)
-    worked = apply_field(ranges_of(recv[:, 49:52, :].reshape(PW, STICKS)), recv, potential)
-    payload = gram_part(sums, every_stick, worked)
+    others = [lax.ppermute(recv, "band", [(b, b ^ m) for b in range(4)]) for m in (1, 2, 3)]
+    worked = apply_field(recv, potential)
+    payload, becp = gram_part(recv, others, worked)
     returned = lax.all_to_all(payload, "pw", split_axis=0, concat_axis=0, tiled=True)
 
-    becp = jnp.sum(recv[:, 48, :], axis=0).reshape(2, PROJ)
+    becp = becp[:, 0, :].reshape(4, 2, PROJ)
     same_atom = proj_atom[:, None] == proj_atom[None, :]
     matrix = jnp.where(same_atom, 0.5 * (coupling + coupling.T), 0.0)
-    coupled = jnp.sum(matrix[None] * becp[:, None, :], axis=2, keepdims=True)
+    coupled = jnp.sum(matrix[None] * becp[0][:, None, :], axis=2, keepdims=True)
     base = base_part(kinetic.reshape(1, COEFS), wave_coef, projector, coupled)
-    every_becp = jnp.sum(every_stick[:, :, 48, :], axis=1).reshape(4, 2, PROJ)
     line = coupled.reshape(1, 2, PROJ)
-    far_re = jnp.sum(every_becp * line, axis=(1, 2))
-    far_im = jnp.sum(every_becp[:, 0] * line[:, 1] - every_becp[:, 1] * line[:, 0], axis=1)
+    far_re = jnp.sum(becp * line, axis=(1, 2))
+    far_im = jnp.sum(becp[:, 0] * line[:, 1] - becp[:, 1] * line[:, 0], axis=1)
     far = jnp.concatenate([far_re, far_im, jnp.zeros((120,), F32)]).reshape(1, 128)
-    applied, total = collect(span, key, returned, owned, base.reshape(2, 128, 128), far)
-    total = total[0, :16].reshape(2, 2, 4, 1)
+    applied, total = collect(span, key, returned, stick, base.reshape(2, 128, 128), far)
+    total = total[0, :16].reshape(2, 2, 1, 4)
+    band = jnp.arange(4, dtype=jnp.int32)
+    here = (band[:, None] ^ band[None, :]) == lax.axis_index("band")
+    total = jnp.sum(jnp.where(here, total, 0.0), axis=3, keepdims=True)
     return applied.reshape(2, 1, COEFS), total[0], total[1]
 
 

time: 167 us -> 136 us (0.81)
  blocking collectives: 34.5 us -> 0 us
  between operations: 14.2 us -> 0.76 us
  starting transfers between devices: 5.12 us -> 17.2 us
  waiting for transfers between devices: 15.9 us -> 26.4 us
  local copies, waits for them, and re-layouts: 13.4 us -> 4.06 us
  Pallas kernels: 78.1 us -> 83.2 us
  other arithmetic: 4.48 us -> 1.82 us
    all_to_all x1 -> x0, blocking collectives: 27.2 us -> none  [local(): recv = lax.all_to_all(sent, 'pw', split_axis=0, concat_axis=0, tiled=True)]
    all_to_all x0 -> x1, waiting for transfers between devices: none -> 18.1 us  [local(): recv = lax.all_to_all(sent, 'pw', split_axis=0, concat_axis=0, tiled=True)]
    all_to_all x0 -> x1, starting transfers between devices: none -> 10.7 us  [local(): recv = lax.all_to_all(sent, 'pw', split_axis=0, concat_axis=0, tiled=True)]
    unnamed x31 -> x13, local copies, waits for them, and re-layouts: 10.7 us -> 1.03 us
    all_to_all x1, waiting for transfers between devices: 15.9 us -> 6.76 us  [local(): lax.all_to_all(payload, 'pw', split_axis=0, concat_axis=0, tiled=True)]
    all_gather x1 -> x0, blocking collectives: 7.37 us -> none  [local(): lax.all_gather(wave_coef.reshape(1, 2 * COEFS), 'band', axis=0, tiled=True)]
    pallas_call x1, Pallas kernels: 3.44 us -> 7.81 us  [base_part(): pl.pallas_call(base_kernel, grid=(COEFS // KC,), in_specs=[pl.BlockSpec((...]
    ppermute x0 -> x3, starting transfers between devices: none -> 1.86 us  [local(): lax.ppermute(recv, 'band', [(b, b ^ m) for b in range(4)])]
  transfers between devices with their start and end apart: 2 -> 5, of which waited for: 1 -> 3; matrix products, arithmetic and copies ran while one was open for 3% -> 2% of each run, Pallas kernels for 31% -> 39%
where the time goes in v4:
time: 136 us; the launch traced here: 133 us
  Pallas kernels  83.2 us (61%)
  waiting for transfers between devices  26.4 us (19%)
  starting transfers between devices  17.2 us (13%)
  local copies, waits for them, and re-layouts  4.06 us (3%)
  other arithmetic  1.82 us (1%)
    pallas_call x1, Pallas kernels, apply_field(): pl.pallas_call(field_kernel, in_specs=[vmem, pl.BlockSpec(memory_space=pl...  44.3 us
    all_to_all x1, waiting for transfers between devices, local(): recv = lax.all_to_all(sent, 'pw', split_axis=0, concat_axis=0, tiled=True)  18.1 us
    pallas_call x1, Pallas kernels, spread_sticks(): pl.pallas_call(spread_kernel, grid=(COEFS // KC,), in_specs=[pl.BlockSpec...  15 us
    pallas_call x1, Pallas kernels, collect(): pl.pallas_call(collect_kernel, in_specs=[pl.BlockSpec(memory_space=pltpu....  11.6 us
    all_to_all x1, starting transfers between devices, local(): recv = lax.all_to_all(sent, 'pw', split_axis=0, concat_axis=0, tiled=True)  10.7 us
    pallas_call x1, Pallas kernels, base_part(): pl.pallas_call(base_kernel, grid=(COEFS // KC,), in_specs=[pl.BlockSpec((...  7.81 us
    all_to_all x1, waiting for transfers between devices, local(): lax.all_to_all(payload, 'pw', split_axis=0, concat_axis=0, tiled=True)  6.76 us
    all_to_all x1, starting transfers between devices, local(): lax.all_to_all(payload, 'pw', split_axis=0, concat_axis=0, tiled=True)  4.62 us
  transfers between devices with their start and end apart: 5, of which 3 were waited for; matrix products, arithmetic and copies ran while one was open for 2% of the time, Pallas kernels for 39%

profile of v4, /device:TPU:0, one launch (start us, length us, event | category | flops | bytes accessed | tf_op | source)
XLA Modules:
  0.0 133.5 jit_solution(3648994708179841507)
XLA Ops:
  0.6 15.0 %spread_sticks.1 = (f32[32,64,128]{2,1,0:T(8,128)}, f32[16,8,128]{2,1,0:T(8,128)}, f32[128,128]{1,0:T(8,128)}, s32[2,16]{1,0:T(2,128)}) custom-call(s32[128,128]{1,0:T(8,128)} %bitcast.39, f32[2,128,128]{2,1,0:T(8,128)} %bitcast.30, f32[2,1,16384]{2,1,0:T(1,128)} %coef_ref.3, f32[2,64,16384]{2,1,0:T(8,128)} %proj_ref.3, s32[96,128]{1,0:T(8,128)} %bitcast.40, ...), custom_call_target="tpu_custom_call" | custom-call | flops 6000000000 | bytes 12582912 | tf_op jit(solution)/shard_map/spread_sticks/pallas_call | solution.py:313
  15.7 10.7 %all-to-all-start = ((f32[32,64,128]{2,1,0:T(8,128)}), f32[32,64,128]{2,1,0:T(8,128)S(1)}, u32[]{:S(2)}, u32[]{:S(2)}) async-start(f32[32,64,128]{2,1,0:T(8,128)} %get-tuple-element.13), calls=%async_computation | async-start | bytes 2097152 | tf_op jit(solution)/shard_map/all_to_all | solution.py:740
  26.6 18.1 %all-to-all-done.recv_ref.own_ref = f32[32,64,128]{2,1,0:T(8,128)S(1)} async-done(((f32[32,64,128]{2,1,0:T(8,128)}), f32[32,64,128]{2,1,0:T(8,128)S(1)}, u32[]{:S(2)}, u32[]{:S(2)}) %all-to-all-start) | async-done | bytes 1048608 | tf_op jit(solution)/shard_map/all_to_all | solution.py:740
  44.7 1.0 collective-permute-start.1
  45.7 0.9 collective-permute-start.2
  46.5 44.3 %apply_field.1.worked_ref = f32[32,48,128]{2,1,0:T(8,128)} custom-call(f32[32,64,128]{2,1,0:T(8,128)} %copy-done, f32[8,256,256]{2,1,0:T(8,128)} %field_hbm.1, bf16[768,256]{1,0:T(8,128)(2,1)} %constant.22.clone.y_in_ref, bf16[768,256]{1,0:T(8,128)(2,1)} %constant.23.clone.y_out_ref, bf16[256,768]{1,0:T(8,128)(2,1)} %constant.24.clone.x_in_ref, ...), custom_call_target="tpu_custom_call" | custom-call | flops 35000000512 | bytes 8388608 | tf_op jit(solution)/shard_map/apply_field/pallas_call | solution.py:532
  90.9 1.5 %collective-permute-done.2.three_ref = f32[32,64,128]{2,1,0:T(8,128)} collective-permute-done((f32[32,64,128]{2,1,0:T(8,128)S(1)}, f32[32,64,128]{2,1,0:T(8,128)}, u32[]{:S(2)}, u32[]{:S(2)}) %collective-permute-start.2) | collective-permute-done | bytes 1048608 | tf_op jit(solution)/shard_map/ppermute | solution.py:741
  92.4 4.5 %gram_part.1 = (f32[32,56,128]{2,1,0:T(8,128)}, f32[4,8,128]{2,1,0:T(8,128)}) custom-call(f32[32,64,128]{2,1,0:T(8,128)} %copy-done, f32[32,64,128]{2,1,0:T(8,128)} %copy-done.1, f32[32,64,128]{2,1,0:T(8,128)} %copy-done.2, f32[32,64,128]{2,1,0:T(8,128)} %collective-permute-done.2.three_ref, f32[32,48,128]{2,1,0:T(8,128)} %apply_field.1.worked_ref), custom_call_target="tpu_custom_call" | custom-call | flops 10000000 | bytes 6291456 | tf_op jit(solution)/shard_map/gram_part/pallas_call | solution.py:606
  96.9 0.7 slice_reduce_fusion.2
  97.7 4.6 %all-to-all-start.1 = ((f32[32,56,128]{2,1,0:T(8,128)}), f32[32,56,128]{2,1,0:T(8,128)S(1)}, u32[]{:S(2)}, u32[]{:S(2)}) async-start(f32[32,56,128]{2,1,0:T(8,128)} %get-tuple-element.14), calls=%async_computation.1 | async-start | bytes 1835008 | tf_op jit(solution)/shard_map/all_to_all | solution.py:744
  102.3 0.1 multiply_reduce_fusion
  102.4 0.1 mul.58
  102.5 0.8 multiply_reduce_fusion.1
  103.4 0.7 copy.23.coupled_ref
  104.2 7.8 %base_part.1 = f32[2,1,16384]{2,1,0:T(1,128)} custom-call(f32[1,16384]{1,0:T(1,128)} %bitcast.32, f32[2,1,16384]{2,1,0:T(1,128)} %coef_ref.3, f32[2,64,16384]{2,1,0:T(8,128)} %proj_ref.3, f32[2,64,1]{2,1,0:T(8,128)} %copy.23.coupled_ref), custom_call_target="tpu_custom_call" | custom-call | flops 10000000 | bytes 10485760 | tf_op jit(solution)/shard_map/base_part/pallas_call | solution.py:634
  112.0 0.1 subtract_reduce_fusion
  112.1 0.6 maximum_bitcast_fusion.far_ref
  112.7 6.8 %all-to-all-done.1.recv_ref = f32[32,56,128]{2,1,0:T(8,128)S(1)} async-done(((f32[32,56,128]{2,1,0:T(8,128)}), f32[32,56,128]{2,1,0:T(8,128)S(1)}, u32[]{:S(2)}, u32[]{:S(2)}) %all-to-all-start.1) | async-done | bytes 917536 | tf_op jit(solution)/shard_map/all_to_all | solution.py:744
  119.5 0.9 copy-done.3
  120.4 11.6 %collect.1 = (f32[2,128,128]{2,1,0:T(8,128)}, f32[8,128]{1,0:T(8,128)}) custom-call(s32[2,16]{1,0:T(2,128)} %get-tuple-element.11.span_ref, f32[16,8,128]{2,1,0:T(8,128)} %get-tuple-element.12.key_ref, f32[32,56,128]{2,1,0:T(8,128)} %copy-done.3, s32[96,128]{1,0:T(8,128)} %bitcast.41, bf16[512,1536]{1,0:T(8,128)(2,1)} %constant.26.clone.table_ref, ...), custom_call_target="tpu_custom_call" | custom-call | flops 6000000000 | bytes 4194304 | tf_op jit(solution)/shard_map/collect/pallas_call | solution.py:721
  132.0 0.7 slice_reduce_fusion.1
  132.7 0.1 broadcast_in_dim.38
  132.8 0.1 select_reduce_fusion
  132.9 0.6 fusion.3
  (22 shorter events, 0.4 us)
Async XLA Ops:
  15.6 10.8 %copy-start.4 = (f32[64,64]{1,0:T(8,128)S(1)}, f32[64,64]{1,0:T(8,128)}, u32[]{:S(2)}) copy-start(f32[64,64]{1,0:T(8,128)} %param.19) | copy-start | bytes 49156
  15.6 10.9 %copy-start.5 = (s32[64]{0:T(128)S(1)}, s32[64]{0:T(128)}, u32[]{:S(2)}) copy-start(s32[64]{0:T(128)} %param.18) | copy-start | bytes 772
  15.7 29.0 %all-to-all-start = ((f32[32,64,128]{2,1,0:T(8,128)}), f32[32,64,128]{2,1,0:T(8,128)S(1)}, u32[]{:S(2)}, u32[]{:S(2)}) async-start(f32[32,64,128]{2,1,0:T(8,128)} %get-tuple-element.13), calls=%async_computation | async-start | bytes 2097152 | tf_op jit(solution)/shard_map/all_to_all | solution.py:740
  44.7 1.9 %copy-start = (f32[32,64,128]{2,1,0:T(8,128)}, f32[32,64,128]{2,1,0:T(8,128)S(1)}, u32[]{:S(2)}) copy-start(f32[32,64,128]{2,1,0:T(8,128)S(1)} %all-to-all-done.recv_ref.own_ref) | copy-start | bytes 3145732
  44.7 46.2 %collective-permute-start = (f32[32,64,128]{2,1,0:T(8,128)S(1)}, f32[32,64,128]{2,1,0:T(8,128)S(1)}, u32[]{:S(2)}, u32[]{:S(2)}) collective-permute-start(f32[32,64,128]{2,1,0:T(8,128)S(1)} %all-to-all-done.recv_ref.own_ref), channel_id=1, source_target_pairs={{0,1},{1,0},{2,3},{3,2},{4,5},{5,4},{6,7},{7,6},{8,9},{9,8},{10,11... | collective-permute-start | bytes 3145736 | tf_op jit(solution)/shard_map/ppermute | solution.py:741
  44.7 46.2 %collective-permute-start.1 = (f32[32,64,128]{2,1,0:T(8,128)S(1)}, f32[32,64,128]{2,1,0:T(8,128)S(1)}, u32[]{:S(2)}, u32[]{:S(2)}) collective-permute-start(f32[32,64,128]{2,1,0:T(8,128)S(1)} %all-to-all-done.recv_ref.own_ref), channel_id=1, source_target_pairs={{0,2},{1,3},{2,0},{3,1},{4,6},{5,7},{6,4},{7,5},{8,10},{9,11},{10,... | collective-permute-start | bytes 3145736 | tf_op jit(solution)/shard_map/ppermute | solution.py:741
  45.7 46.8 %collective-permute-start.2 = (f32[32,64,128]{2,1,0:T(8,128)S(1)}, f32[32,64,128]{2,1,0:T(8,128)}, u32[]{:S(2)}, u32[]{:S(2)}) collective-permute-start(f32[32,64,128]{2,1,0:T(8,128)S(1)} %all-to-all-done.recv_ref.own_ref), channel_id=1, source_target_pairs={{0,3},{1,2},{2,1},{3,0},{4,7},{5,6},{6,5},{7,4},{8,11},{9,10},{10,... | collective-permute-start | bytes 3145736 | tf_op jit(solution)/shard_map/ppermute | solution.py:741
  90.9 1.6 %copy-start.1 = (f32[32,64,128]{2,1,0:T(8,128)}, f32[32,64,128]{2,1,0:T(8,128)S(1)}, u32[]{:S(2)}) copy-start(f32[32,64,128]{2,1,0:T(8,128)S(1)} %collective-permute-done.one_ref) | copy-start | bytes 3145732
  90.9 1.6 %copy-start.2 = (f32[32,64,128]{2,1,0:T(8,128)}, f32[32,64,128]{2,1,0:T(8,128)S(1)}, u32[]{:S(2)}) copy-start(f32[32,64,128]{2,1,0:T(8,128)S(1)} %collective-permute-done.1.two_ref) | copy-start | bytes 3145732
  97.7 21.8 %all-to-all-start.1 = ((f32[32,56,128]{2,1,0:T(8,128)}), f32[32,56,128]{2,1,0:T(8,128)S(1)}, u32[]{:S(2)}, u32[]{:S(2)}) async-start(f32[32,56,128]{2,1,0:T(8,128)} %get-tuple-element.14), calls=%async_computation.1 | async-start | bytes 1835008 | tf_op jit(solution)/shard_map/all_to_all | solution.py:744
  119.5 0.9 copy-start.3

commit v5 on v4

--- a/solution.py
+++ b/solution.py
@@ -1,3 +1,5 @@
+import functools
+
 import jax
 import jax.numpy as jnp
 import ml_dtypes
@@ -19,7 +21,8 @@
 PROJ = 64
 PLANES = GZ // PW
 ROWS = 2 * PLANES
-KC = 2048
+KC = 4096
+STEP_BLOCKS = KC // 1024
 WINDOW = 256
 SLOT_ROWS = 768
 TILES = STICKS // 128
@@ -27,10 +30,11 @@
 CHUNKS = 16
 NQ = 4
 NCH = 3
-PAIR = 2
+PAIR = 4
 PLACE_UNROLL = 4
-PICK_UNROLL = 4
-GRAM_STEPS = 4
+PICK_UNROLL = 6
+GRAM_STEPS = 2
+FETCH_UNROLL = 4
 F32 = jnp.float32
 BF16 = jnp.bfloat16
 NN = (((1,), (0,)), ((), ()))
@@ -148,7 +152,7 @@
     return keys, values
 
 
-def sorted_row(ref, block):
+def block_row(ref, block):
     at = pl.ds(block // 2, 1)
     half = 8 * (block % 2)
     return jnp.concatenate([ref[half + v, at, :] for v in range(8)], axis=1)
@@ -205,12 +209,14 @@
     return (square + z * z) * (KIN_MAX / 3.0 / 16384.0)
 
 
-def spread_kernel(slot_ref, tile_ref, coef_ref, proj_ref, stick_ref, table_ref, out_ref, key_ref, kinetic_ref,
-                  span_ref, part_re, part_im, acc, becp):
+def spread_kernel(slot_ref, tile_ref, coef_ref, proj_ref, stick_ref, table_hbm, out_ref, key_ref, kinetic_ref,
+                  span_ref, parts, acc, becp, table_ref, table_sem):
     step = pl.program_id(0)
+    table_copy = pltpu.make_async_copy(table_hbm, table_ref, table_sem)
 
     @pl.when(step == 0)
     def _():
+        table_copy.start()
         slot = slot_ref[...].astype(F32)
         z = jnp.floor((slot + 0.5) * (1.0 / STICKS))
         s = slot - z * STICKS
@@ -234,8 +240,8 @@
         keys, (real, imag) = sort_rows(rows(key), [rows(tile_ref[0]), rows(tile_ref[1])])
         for v in range(16):
             key_ref[v] = keys[v]
-            part_re[v] = real[v]
-            part_im[v] = imag[v]
+            for at, part in enumerate(key_parts(keys[v]) + split(real[v]) + split(imag[v])):
+                parts[at, v] = part.astype(F32)
         for block in range(16):
             half = 8 * (block % 2)
             at = block // 2
@@ -250,32 +256,37 @@
     none = jnp.zeros((), BF16)
     lane_of = (iota((128, 1024), 0)).astype(BF16)
     row_of = (iota((WINDOW, 1024), 0) - 128.0).astype(BF16)
-    for half in range(2):
-        block = step * 2 + half
-        at = pl.ds(step, 1)
-        key = jnp.concatenate([key_ref[8 * half + v, at, :] for v in range(8)], axis=1)
-        real = jnp.concatenate([part_re[8 * half + v, at, :] for v in range(8)], axis=1)
-        imag = jnp.concatenate([part_im[8 * half + v, at, :] for v in range(8)], axis=1)
-        row, lane = key_parts(key)
+
+    def product(block, first):
+        row, lane, re_hi, re_lo, im_hi, im_lo = [block_row(parts.at[at], block) for at in range(6)]
         hit = lane_of == lane.astype(BF16)
-        re_hi, re_lo = split(real)
-        im_hi, im_lo = split(imag)
-        placed = jnp.concatenate([jnp.where(hit, part, none) for part in (re_hi, im_hi, re_lo, im_lo)], axis=0)
-
-        def add(first):
-            first = pl.multiple_of(first, 16)
-            want = row - (first + 128).astype(F32)
-            hot = jnp.where(row_of == want.astype(BF16), jnp.ones((), BF16), none)
-            acc[pl.ds(first, WINDOW), :] += mm(hot, placed, NT)
-
+        placed = jnp.concatenate(
+            [jnp.where(hit, part.astype(BF16), none) for part in (re_hi, im_hi, re_lo, im_lo)], axis=0)
+        want = row - (first + 128).astype(F32)
+        hot = jnp.where(row_of == want.astype(BF16), jnp.ones((), BF16), none)
+        return mm(hot, placed, NT)
+
+    def window(first):
+        return pl.ds(pl.multiple_of(first, 16), WINDOW)
+
+    blocks = [step * STEP_BLOCKS + at for at in range(STEP_BLOCKS)]
+    for block in blocks:
         first = span_ref[0, block]
-        add(first)
-
-        def more(p, carry):
-            add(first + p * WINDOW)
-            return carry
-
-        lax.fori_loop(1, span_ref[1, block], more, 0)
+        acc[window(first), :] += product(block, first)
+
+    @pl.when(sum(span_ref[1, block] for block in blocks) > STEP_BLOCKS)
+    def _():
+        def rest(at, carry):
+            block = step * STEP_BLOCKS + at
+
+            def more(p, inner):
+                first = span_ref[0, block] + p * WINDOW
+                acc[window(first), :] += product(block, first)
+                return inner
+
+            return lax.fori_loop(1, span_ref[1, block], more, carry)
+
+        lax.fori_loop(0, STEP_BLOCKS, rest, 0)
 
     c_re = coef_ref[0]
     c_im = coef_ref[1]
@@ -298,6 +309,7 @@
         sticks = mm(sticks, order.astype(BF16), NT).astype(BF16)
         high = sticks[:512]
         low = sticks[512:]
+        table_copy.wait()
         spread = mm(table_ref[...], jnp.concatenate([high, high, low], axis=0))
         spread = spread.reshape(PW, ROWS, STICKS)
         for t in range(TILES):
@@ -319,7 +331,7 @@
             pl.BlockSpec((2, 1, KC), lambda i: (0, 0, i)),
             pl.BlockSpec((2, PROJ, KC), lambda i: (0, 0, i)),
             pl.BlockSpec((PW * TILES, 128), lambda i: (0, 0)),
-            pl.BlockSpec((512, 1536), lambda i: (0, 0)),
+            pl.BlockSpec(memory_space=pl.ANY),
         ],
         out_specs=[
             pl.BlockSpec((PW, 64, 128), lambda i: (0, 0, 0)),
@@ -334,10 +346,11 @@
             jax.ShapeDtypeStruct((2, 16), jnp.int32),
         ],
         scratch_shapes=[
-            pltpu.VMEM((16, 8, 128), F32),
-            pltpu.VMEM((16, 8, 128), F32),
+            pltpu.VMEM((6, 16, 8, 128), F32),
             pltpu.VMEM((SLOT_ROWS + WINDOW, 512), F32),
             pltpu.VMEM((128, 128), F32),
+            pltpu.VMEM((512, 1536), BF16),
+            pltpu.SemaphoreType.DMA,
         ],
         compiler_params=pltpu.CompilerParams(vmem_limit_bytes=60 << 20),
         cost_estimate=pl.CostEstimate(flops=6 * 10 ** 9, bytes_accessed=12 << 20, transcendentals=0),
@@ -373,7 +386,10 @@
     more = jnp.zeros((128 - GROUPS, 128), F32)
     first = jnp.transpose(jnp.concatenate([first, more], axis=0))[:1]
     last = jnp.transpose(jnp.concatenate([last, more], axis=0))[:1]
-    lines = [jnp.minimum(start, GROUPS - 1.0), end - start, first, last - first + 1.0, jnp.zeros((4, 128), F32)]
+    count = jnp.where(lane[:1] < CHUNKS, end - start, 0.0)
+    lines = [jnp.minimum(start, GROUPS - 1.0), end - start, first, last - first + 1.0,
+             jnp.broadcast_to(jnp.max(count, axis=1, keepdims=True), (1, 128)),
+             jnp.broadcast_to(jnp.max(last - first + 1.0, axis=1, keepdims=True), (1, 128)), jnp.zeros((2, 128), F32)]
     bounds[...] = jnp.concatenate(lines, axis=0).astype(jnp.int32)
 
 
@@ -410,7 +426,7 @@
             _, even, odd, sign = fold(y)
             hot[q, :128, :] = jnp.where(one_hot == even.astype(BF16), jnp.ones((), BF16), zero)
             hot[q, 128:, :] = jnp.where(one_hot == odd.astype(BF16), sign.astype(BF16), zero)
-    for q in range(GROUPS, GROUPS + NQ - 1):
+    for q in range(GROUPS, GROUPS + NQ):
         wide[q] = jnp.zeros((2 * ROWS, 16, 512), BF16)
         hot[q] = jnp.zeros((256, 512), BF16)
         keys[q] = jnp.full((16, 512), -1.0, BF16)
@@ -435,9 +451,15 @@
         return pl.ds(pl.multiple_of(chunk * 16, 16), 16)
 
     def place_first(step, carry):
-        for at in range(PLACE_UNROLL):
-            chunk = step * PLACE_UNROLL + at
-            grid[:, rows_of(chunk), :] = place(chunk, range_ref[0, chunk], NQ)
+        chunks = [step * PLACE_UNROLL + at for at in range(PLACE_UNROLL)]
+        most = functools.reduce(jnp.maximum, [range_ref[1, chunk] for chunk in chunks])
+
+        def run(groups):
+            for chunk in chunks:
+                grid[:, rows_of(chunk), :] = place(chunk, range_ref[0, chunk], groups)
+
+        pl.when(most <= NQ)(lambda: run(NQ))
+        pl.when(most > NQ)(lambda: run(NQ + 1))
         return carry
 
     def place_rest(chunk, carry):
@@ -445,11 +467,14 @@
             grid[:, rows_of(chunk), :] += place(chunk, range_ref[0, chunk] + p, 1)
             return inner
 
-        return lax.fori_loop(NQ, range_ref[1, chunk], more, carry)
+        return lax.fori_loop(NQ + 1, range_ref[1, chunk], more, carry)
 
     range_copy.wait()
     lax.fori_loop(0, CHUNKS // PLACE_UNROLL, place_first, 0)
-    lax.fori_loop(0, CHUNKS, place_rest, 0)
+
+    @pl.when(range_ref[4, 0] > NQ + 1)
+    def _():
+        lax.fori_loop(0, CHUNKS, place_rest, 0)
 
     row = lax.broadcasted_iota(jnp.int32, (256, 256), 0)
     lane = lax.broadcasted_iota(jnp.int32, (256, 256), 1)
@@ -518,7 +543,10 @@
         return lax.fori_loop(NCH, range_ref[3, q], more, carry)
 
     lax.fori_loop(0, GROUPS // PICK_UNROLL, pick_first, 0)
-    lax.fori_loop(0, GROUPS, pick_rest, 0)
+
+    @pl.when(range_ref[5, 0] > NCH)
+    def _():
+        lax.fori_loop(0, GROUPS, pick_rest, 0)
 
     for t in range(TILES):
         for g in range(4):
@@ -535,10 +563,10 @@
         out_specs=vmem,
         out_shape=jax.ShapeDtypeStruct((PW, 48, 128), F32),
         scratch_shapes=[
-            pltpu.VMEM((GROUPS + NQ - 1, 2 * ROWS, 16, 512), BF16),
-            pltpu.VMEM((GROUPS + NQ - 1, 256, 512), BF16),
-            pltpu.VMEM((GROUPS + NQ - 1, 16, 512), BF16),
-            pltpu.VMEM((GROUPS + NQ - 1, 16, 512), BF16),
+            pltpu.VMEM((GROUPS + NQ, 2 * ROWS, 16, 512), BF16),
+            pltpu.VMEM((GROUPS + NQ, 256, 512), BF16),
+            pltpu.VMEM((GROUPS + NQ, 16, 512), BF16),
+            pltpu.VMEM((GROUPS + NQ, 16, 512), BF16),
             pltpu.VMEM((ROWS, GX, GY), F32),
             pltpu.VMEM((ROWS, GX + 16 * (NCH - 1), 512), BF16),
             pltpu.VMEM((GROUPS, ROWS, 512), F32),
@@ -618,19 +646,33 @@
     )(recv, *others, worked)
 
 
-def base_kernel(kinetic_ref, coef_ref, proj_ref, coupled_ref, out_ref):
+def base_kernel(kinetic_ref, coef_ref, proj_ref, matrix_ref, becp_ref, out_ref, far_ref, weight):
+    @pl.when(pl.program_id(0) == 0)
+    def _():
+        matrix = matrix_ref[...]
+        lines = jnp.concatenate([becp_ref[a, :1, :] for a in range(4)], axis=0)
+        w_re = jnp.sum(matrix * lines[:1, :PROJ], axis=1, keepdims=True)
+        w_im = jnp.sum(matrix * lines[:1, PROJ:], axis=1, keepdims=True)
+        weight[0] = jnp.broadcast_to(w_re, (PROJ, 128))
+        weight[1] = jnp.broadcast_to(w_im, (PROJ, 128))
+        down = jnp.transpose(jnp.concatenate([lines, jnp.zeros((124, 128), F32)], axis=0))
+        far_re = jnp.sum(down[:PROJ] * w_re + down[PROJ:] * w_im, axis=0, keepdims=True)
+        far_im = jnp.sum(down[:PROJ] * w_im - down[PROJ:] * w_re, axis=0, keepdims=True)
+        far = jnp.broadcast_to(far_re, (8, 128)) + pltpu.roll(jnp.broadcast_to(far_im, (8, 128)), 4, 1)
+        far_ref[...] = far
+
     kinetic = kinetic_ref[...]
     p_re = proj_ref[0]
     p_im = proj_ref[1]
-    w_re = coupled_ref[0]
-    w_im = coupled_ref[1]
+    w_re = weight[0][:, :1]
+    w_im = weight[1][:, :1]
     far_re = jnp.sum(p_re * w_re - p_im * w_im, axis=0, keepdims=True)
     far_im = jnp.sum(p_re * w_im + p_im * w_re, axis=0, keepdims=True)
     out_ref[0] = kinetic * coef_ref[0] + far_re
     out_ref[1] = kinetic * coef_ref[1] + far_im
 
 
-def base_part(kinetic, coef, proj, coupled):
+def base_part(kinetic, coef, proj, matrix, becp):
     return pl.pallas_call(
         base_kernel,
         grid=(COEFS // KC,),
@@ -638,19 +680,30 @@
             pl.BlockSpec((1, KC), lambda i: (0, i)),
             pl.BlockSpec((2, 1, KC), lambda i: (0, 0, i)),
             pl.BlockSpec((2, PROJ, KC), lambda i: (0, 0, i)),
-            pl.BlockSpec((2, PROJ, 1), lambda i: (0, 0, 0)),
+            pl.BlockSpec((PROJ, PROJ), lambda i: (0, 0)),
+            pl.BlockSpec((4, 8, 128), lambda i: (0, 0, 0)),
         ],
-        out_specs=pl.BlockSpec((2, 1, KC), lambda i: (0, 0, i)),
-        out_shape=jax.ShapeDtypeStruct((2, 1, COEFS), F32),
+        out_specs=[pl.BlockSpec((2, 1, KC), lambda i: (0, 0, i)), pl.BlockSpec((8, 128), lambda i: (0, 0))],
+        out_shape=[jax.ShapeDtypeStruct((2, 1, COEFS), F32), jax.ShapeDtypeStruct((8, 128), F32)],
+        scratch_shapes=[pltpu.VMEM((2, PROJ, 128), F32)],
         compiler_params=pltpu.CompilerParams(vmem_limit_bytes=60 << 20),
         cost_estimate=pl.CostEstimate(flops=10 ** 7, bytes_accessed=10 << 20, transcendentals=0),
         name="base_part",
-    )(kinetic, coef, proj, coupled)
-
-
-def collect_kernel(span_ref, key_ref, recv_ref, stick_ref, table_ref, base_ref, far_ref, out_ref, sums_ref,
-                   values, found_re, found_im):
-    sums_ref[...] = jnp.sum(recv_ref[:, TILES * ROWS:, :], axis=0) + far_ref[...]
+    )(kinetic, coef, proj, matrix, becp)
+
+
+def collect_kernel(span_ref, key_ref, recv_ref, stick_ref, table_ref, base_ref, far_ref, out_ref,
+                   energy_ref, overlap_ref, values, found_re, found_im):
+    total = jnp.sum(recv_ref[:, TILES * ROWS:, :], axis=0) + far_ref[...]
+    band = lax.axis_index("band")
+    lane = lax.broadcasted_iota(jnp.int32, (8, 128), 1)
+    for bit in (1, 2):
+        swapped = jnp.where((lane & bit) == 0, pltpu.roll(total, 128 - bit, 1), pltpu.roll(total, bit, 1))
+        total = jnp.where((band & bit) != 0, swapped, total)
+    for ri in range(2):
+        energy_ref[ri] = total[:1, ri * 4:ri * 4 + 4]
+        overlap_ref[ri] = total[:1, 8 + ri * 4:12 + ri * 4]
+
     order, _ = rank_of(owned_row(stick_ref))
     order = order.astype(BF16)
     lines = jnp.concatenate(
@@ -668,42 +721,42 @@
     lane_of = iota((128, 1024), 0).astype(BF16)
     row_of = iota((WINDOW, 1024), 0)
 
+    def fetch(block, first):
+        row, lane = key_parts(block_row(key_ref, block))
+        hit = jnp.where(lane_of == lane.astype(BF16), jnp.ones((), BF16), jnp.zeros((), BF16))
+        here = pl.ds(pl.multiple_of(first, 16), WINDOW)
+        got = mm(jnp.concatenate([values[0, here, :], values[1, here, :]], axis=0), jnp.concatenate([hit, hit], axis=0))
+        mine = row_of == row - first.astype(F32)
+        return (jnp.sum(jnp.where(mine, got[:WINDOW], 0.0), axis=0, keepdims=True),
+                jnp.sum(jnp.where(mine, got[WINDOW:], 0.0), axis=0, keepdims=True))
+
+    def put(block, pair, old):
+        at = pl.ds(block // 2, 1)
+        half = 8 * (block % 2)
+        for ref, line in zip((found_re, found_im), pair):
+            for v in range(8):
+                piece = line[:, v * 128:(v + 1) * 128]
+                ref[half + v, at, :] = ref[half + v, at, :] + piece if old else piece
+
     def one(step, carry):
-        at = pl.ds(step, 1)
-        for half in range(2):
-            block = step * 2 + half
-            key = jnp.concatenate([key_ref[8 * half + v, at, :] for v in range(8)], axis=1)
-            row, lane = key_parts(key)
-            hit = jnp.where(lane_of == lane.astype(BF16), jnp.ones((), BF16), jnp.zeros((), BF16))
-            hit = jnp.concatenate([hit, hit], axis=0)
-
-            def fetch(first):
-                first = pl.multiple_of(first, 16)
-                here = pl.ds(first, WINDOW)
-                got = mm(jnp.concatenate([values[0, here, :], values[1, here, :]], axis=0), hit)
-                mine = row_of == row - first.astype(F32)
-                return (jnp.sum(jnp.where(mine, got[:WINDOW], 0.0), axis=0, keepdims=True),
-                        jnp.sum(jnp.where(mine, got[WINDOW:], 0.0), axis=0, keepdims=True))
-
-            first = span_ref[0, block]
-
-            def put(pair):
-                for v in range(8):
-                    found_re[8 * half + v, at, :] = pair[0][:, v * 128:(v + 1) * 128]
-                    found_im[8 * half + v, at, :] = pair[1][:, v * 128:(v + 1) * 128]
-
+        for at in range(FETCH_UNROLL):
+            block = step * FETCH_UNROLL + at
+            put(block, fetch(block, span_ref[0, block]), False)
+        return carry
+
+    lax.fori_loop(0, 16 // FETCH_UNROLL, one, 0)
+
+    @pl.when(sum(span_ref[1, block] for block in range(16)) > 16)
+    def _():
+        def rest(block, carry):
             def more(p, inner):
-                pair = fetch(first + p * WINDOW)
-                for v in range(8):
-                    found_re[8 * half + v, at, :] += pair[0][:, v * 128:(v + 1) * 128]
-                    found_im[8 * half + v, at, :] += pair[1][:, v * 128:(v + 1) * 128]
+                put(block, fetch(block, span_ref[0, block] + p * WINDOW), True)
                 return inner
 
-            put(fetch(first))
-            lax.fori_loop(1, span_ref[1, block], more, 0)
-        return carry
-
-    lax.fori_loop(0, 8, one, 0)
+            return lax.fori_loop(1, span_ref[1, block], more, carry)
+
+        lax.fori_loop(0, 16, rest, 0)
+
     scale = 1.0 / (GX * GY * GZ)
     home = []
     for v in range(16):
@@ -721,14 +774,18 @@
     return pl.pallas_call(
         collect_kernel,
         in_specs=[pl.BlockSpec(memory_space=pltpu.SMEM)] + [vmem] * 6,
-        out_specs=[vmem, vmem],
-        out_shape=[jax.ShapeDtypeStruct((2, 128, 128), F32), jax.ShapeDtypeStruct((8, 128), F32)],
+        out_specs=[vmem, vmem, vmem],
+        out_shape=[
+            jax.ShapeDtypeStruct((2, 128, 128), F32),
+            jax.ShapeDtypeStruct((2, 1, 4), F32),
+            jax.ShapeDtypeStruct((2, 1, 4), F32),
+        ],
         scratch_shapes=[
             pltpu.VMEM((2, SLOT_ROWS + WINDOW, 256), BF16),
             pltpu.VMEM((16, 8, 128), F32),
             pltpu.VMEM((16, 8, 128), F32),
         ],
-        compiler_params=pltpu.CompilerParams(vmem_limit_bytes=60 << 20),
+        compiler_params=pltpu.CompilerParams(vmem_limit_bytes=32 << 20),
         cost_estimate=pl.CostEstimate(flops=6 * 10 ** 9, bytes_accessed=4 << 20, transcendentals=0),
         name="collect",
     )(span, key, recv, stick, jnp.asarray(collect_table()), base, far)
@@ -743,21 +800,11 @@
     payload, becp = gram_part(recv, others, worked)
     returned = lax.all_to_all(payload, "pw", split_axis=0, concat_axis=0, tiled=True)
 
-    becp = becp[:, 0, :].reshape(4, 2, PROJ)
     same_atom = proj_atom[:, None] == proj_atom[None, :]
     matrix = jnp.where(same_atom, 0.5 * (coupling + coupling.T), 0.0)
-    coupled = jnp.sum(matrix[None] * becp[0][:, None, :], axis=2, keepdims=True)
-    base = base_part(kinetic.reshape(1, COEFS), wave_coef, projector, coupled)
-    line = coupled.reshape(1, 2, PROJ)
-    far_re = jnp.sum(becp * line, axis=(1, 2))
-    far_im = jnp.sum(becp[:, 0] * line[:, 1] - becp[:, 1] * line[:, 0], axis=1)
-    far = jnp.concatenate([far_re, far_im, jnp.zeros((120,), F32)]).reshape(1, 128)
-    applied, total = collect(span, key, returned, stick, base.reshape(2, 128, 128), far)
-    total = total[0, :16].reshape(2, 2, 1, 4)
-    band = jnp.arange(4, dtype=jnp.int32)
-    here = (band[:, None] ^ band[None, :]) == lax.axis_index("band")
-    total = jnp.sum(jnp.where(here, total, 0.0), axis=3, keepdims=True)
-    return applied.reshape(2, 1, COEFS), total[0], total[1]
+    base, far = base_part(kinetic.reshape(1, COEFS), wave_coef, projector, matrix, becp)
+    applied, energy, overlap = collect(span, key, returned, stick, base.reshape(2, 128, 128), far)
+    return applied.reshape(2, 1, COEFS), energy.transpose(0, 2, 1), overlap.transpose(0, 2, 1)
 
 
 def solution(mesh):

time: 136 us -> 126 us (0.926); the launches traced: 133 us -> 126 us
  blocking collectives: 0 us -> 29.5 us
  waiting for transfers between devices: 26.4 us -> 14 us
  starting transfers between devices: 17.2 us -> 6.26 us
  Pallas kernels: 83.2 us -> 72.5 us
  local copies, waits for them, and re-layouts: 4.06 us -> 1.69 us
    all_to_all x0 -> x1, blocking collectives: none -> 29.5 us  [local(): recv = lax.all_to_all(sent, 'pw', split_axis=0, concat_axis=0, tiled=True)]
    all_to_all x1 -> x0, waiting for transfers between devices: 18.1 us -> none  [local(): recv = lax.all_to_all(sent, 'pw', split_axis=0, concat_axis=0, tiled=True)]
    all_to_all x1 -> x0, starting transfers between devices: 10.7 us -> none  [local(): recv = lax.all_to_all(sent, 'pw', split_axis=0, concat_axis=0, tiled=True)]
    all_to_all x1, waiting for transfers between devices: 6.76 us -> 10.2 us  [local(): lax.all_to_all(payload, 'pw', split_axis=0, concat_axis=0, tiled=True)]
    pallas_call x1, Pallas kernels: 11.6 us -> 8.29 us  [collect(): pl.pallas_call(collect_kernel, in_specs=[pl.BlockSpec(memory_space=pltpu....]
    pallas_call x1, Pallas kernels: 15 us -> 12.1 us  [spread_sticks(): pl.pallas_call(spread_kernel, grid=(COEFS // KC,), in_specs=[pl.BlockSpec...]
    pallas_call x1, Pallas kernels: 44.3 us -> 42 us  [apply_field(): pl.pallas_call(field_kernel, in_specs=[vmem, pl.BlockSpec(memory_space=pl...]
    ppermute x3, waiting for transfers between devices: 1.55 us -> 3.86 us  [local(): lax.ppermute(recv, 'band', [(b, b ^ m) for b in range(4)])]
  transfers between devices with their start and end apart: 5 -> 4, of which waited for: 3 -> 2; matrix products, arithmetic and copies ran while one was open for 2% -> 1% of each run, Pallas kernels for 39% -> 39%
where the time goes in v5:
time: 126 us
  Pallas kernels  72.5 us (58%)
  blocking collectives  29.5 us (23%)
  waiting for transfers between devices  14 us (11%)
  starting transfers between devices  6.26 us (5%)
  local copies, waits for them, and re-layouts  1.69 us (1%)
    pallas_call x1, Pallas kernels, apply_field(): pl.pallas_call(field_kernel, in_specs=[vmem, pl.BlockSpec(memory_space=pl...  42 us
    all_to_all x1, blocking collectives, local(): recv = lax.all_to_all(sent, 'pw', split_axis=0, concat_axis=0, tiled=True)  29.5 us
    pallas_call x1, Pallas kernels, spread_sticks(): pl.pallas_call(spread_kernel, grid=(COEFS // KC,), in_specs=[pl.BlockSpec...  12.1 us
    all_to_all x1, waiting for transfers between devices, local(): lax.all_to_all(payload, 'pw', split_axis=0, concat_axis=0, tiled=True)  10.2 us
    pallas_call x1, Pallas kernels, collect(): pl.pallas_call(collect_kernel, in_specs=[pl.BlockSpec(memory_space=pltpu....  8.29 us
    pallas_call x1, Pallas kernels, base_part(): pl.pallas_call(base_kernel, grid=(COEFS // KC,), in_specs=[pl.BlockSpec((...  6.37 us
    all_to_all x1, starting transfers between devices, local(): lax.all_to_all(payload, 'pw', split_axis=0, concat_axis=0, tiled=True)  4.4 us
    ppermute x3, waiting for transfers between devices, local(): lax.ppermute(recv, 'band', [(b, b ^ m) for b in range(4)])  3.86 us
  transfers between devices with their start and end apart: 4, of which 2 were waited for; matrix products, arithmetic and copies ran while one was open for 1% of the time, Pallas kernels for 39%

profile of v5, /device:TPU:0, one launch (start us, length us, event | category | flops | bytes accessed | tf_op | source)
XLA Modules:
  0.0 125.5 jit_solution(15307232680806830781)
XLA Ops:
  0.6 12.1 %spread_sticks.1 = (f32[32,64,128]{2,1,0:T(8,128)}, f32[16,8,128]{2,1,0:T(8,128)}, f32[128,128]{1,0:T(8,128)}, s32[2,16]{1,0:T(2,128)}) custom-call(s32[128,128]{1,0:T(8,128)} %bitcast.23, f32[2,128,128]{2,1,0:T(8,128)} %bitcast.21, f32[2,1,16384]{2,1,0:T(1,128)} %coef_ref.3, f32[2,64,16384]{2,1,0:T(8,128)} %proj_ref.3, s32[96,128]{1,0:T(8,128)} %bitcast.19, ...), custom_call_target="tpu_custom_call" | custom-call | flops 6000000000 | bytes 12582912 | tf_op jit(solution)/shard_map/spread_sticks/pallas_call | solution.py:325
  12.7 29.5 %all_to_all.10.recv_ref.own_ref = f32[32,64,128]{2,1,0:T(8,128)S(1)} all-to-all(f32[32,64,128]{2,1,0:T(8,128)} %get-tuple-element.16), channel_id=1, replica_groups=mesh['pw'=32,'band'=4] {'pw'}, dimensions={0} | all-to-all | bytes 2097152 | tf_op jit(solution)/shard_map/all_to_all | solution.py:797
  42.3 0.0 collective-permute-start
  42.3 1.0 collective-permute-start.1
  43.3 0.8 collective-permute-start.2
  44.1 0.0 copy-done.6
  44.1 42.0 %apply_field.1.worked_ref = f32[32,48,128]{2,1,0:T(8,128)} custom-call(f32[32,64,128]{2,1,0:T(8,128)} %copy-done.6, f32[8,256,256]{2,1,0:T(8,128)} %field_hbm.1, bf16[768,256]{1,0:T(8,128)(2,1)} %constant.17.clone.y_in_ref, bf16[768,256]{1,0:T(8,128)(2,1)} %constant.18.clone.y_out_ref, bf16[256,768]{1,0:T(8,128)(2,1)} %constant.19.clone.x_in_ref, ...), custom_call_target="tpu_custom_call" | custom-call | flops 35000000512 | bytes 8388608 | tf_op jit(solution)/shard_map/apply_field/pallas_call | solution.py:560
  86.1 0.0 copy-start.9
  86.1 0.0 copy-start.10
  86.1 0.0 collective-permute-done.one_ref
  86.1 0.0 copy-start.7
  86.1 0.0 collective-permute-done.1.two_ref
  86.2 0.0 copy-start.8
  86.2 3.9 %collective-permute-done.2.three_ref = f32[32,64,128]{2,1,0:T(8,128)} collective-permute-done((f32[32,64,128]{2,1,0:T(8,128)S(1)}, f32[32,64,128]{2,1,0:T(8,128)}, u32[]{:S(2)}, u32[]{:S(2)}) %collective-permute-start.2) | collective-permute-done | bytes 1048608 | tf_op jit(solution)/shard_map/ppermute | solution.py:798
  90.0 3.8 %gram_part.1 = (f32[32,56,128]{2,1,0:T(8,128)}, f32[4,8,128]{2,1,0:T(8,128)}) custom-call(f32[32,64,128]{2,1,0:T(8,128)} %copy-done.6, f32[32,64,128]{2,1,0:T(8,128)} %copy-done.7, f32[32,64,128]{2,1,0:T(8,128)} %copy-done.8, f32[32,64,128]{2,1,0:T(8,128)} %collective-permute-done.2.three_ref, f32[32,48,128]{2,1,0:T(8,128)} %apply_field.1.worked_ref), custom_call_target="tpu_custom_call" | custom-call | flops 10000000 | bytes 6291456 | tf_op jit(solution)/shard_map/gram_part/pallas_call | solution.py:634
  93.9 4.4 %all-to-all-start.1 = ((f32[32,56,128]{2,1,0:T(8,128)}), f32[32,56,128]{2,1,0:T(8,128)S(1)}, u32[]{:S(2)}, u32[]{:S(2)}) async-start(f32[32,56,128]{2,1,0:T(8,128)} %get-tuple-element.17), calls=%async_computation.1 | async-start | bytes 1835008 | tf_op jit(solution)/shard_map/all_to_all | solution.py:801
  98.3 0.1 copy.16
  98.4 0.7 fusion.1.matrix_ref
  99.0 6.4 %base_part.1 = (f32[2,1,16384]{2,1,0:T(1,128)}, f32[8,128]{1,0:T(8,128)}) custom-call(f32[1,16384]{1,0:T(1,128)} %bitcast.22, f32[2,1,16384]{2,1,0:T(1,128)} %coef_ref.3, f32[2,64,16384]{2,1,0:T(8,128)} %proj_ref.3, f32[64,64]{1,0:T(8,128)} %fusion.1.matrix_ref, f32[4,8,128]{2,1,0:T(8,128)} %get-tuple-element.19.becp_ref), custom_call_target="tpu_custom_call" | custom-call | flops 10000000 | bytes 10485760 | tf_op jit(solution)/shard_map/base_part/pallas_call | solution.py:676
  105.4 10.2 %all-to-all-done.1.recv_ref = f32[32,56,128]{2,1,0:T(8,128)S(1)} async-done(((f32[32,56,128]{2,1,0:T(8,128)}), f32[32,56,128]{2,1,0:T(8,128)S(1)}, u32[]{:S(2)}, u32[]{:S(2)}) %all-to-all-start.1) | async-done | bytes 917536 | tf_op jit(solution)/shard_map/all_to_all | solution.py:801
  115.6 0.0 copy-start
  115.6 0.9 copy-done
  116.5 0.7 copy-done.2
  117.2 8.3 %collect.1 = (f32[2,128,128]{2,1,0:T(8,128)}, f32[2,1,4]{2,1,0:T(1,128)}, f32[2,1,4]{2,1,0:T(1,128)}) custom-call(s32[2,16]{1,0:T(2,128)S(1)} %copy-done.5, f32[16,8,128]{2,1,0:T(8,128)S(1)} %copy-done.4, f32[32,56,128]{2,1,0:T(8,128)S(1)} %all-to-all-done.1.recv_ref, s32[96,128]{1,0:T(8,128)S(1)} %bitcast.20, bf16[512,1536]{1,0:T(8,128)(2,1)S(1)} %copy-done.3, ...), custom_call_target="tpu_custom_call" | custom-call | flops 6000000000 | bytes 4194304 | tf_op jit(solution)/shard_map/collect/pallas_call | solution.py:774
  (14 shorter events, 0.0 us)
Async XLA Ops:
  42.3 1.9 %copy-start.6 = (f32[32,64,128]{2,1,0:T(8,128)}, f32[32,64,128]{2,1,0:T(8,128)S(1)}, u32[]{:S(2)}) copy-start(f32[32,64,128]{2,1,0:T(8,128)S(1)} %all_to_all.10.recv_ref.own_ref) | copy-start | bytes 3145732
  42.3 43.9 %collective-permute-start = (f32[32,64,128]{2,1,0:T(8,128)S(1)}, f32[32,64,128]{2,1,0:T(8,128)S(1)}, u32[]{:S(2)}, u32[]{:S(2)}) collective-permute-start(f32[32,64,128]{2,1,0:T(8,128)S(1)} %all_to_all.10.recv_ref.own_ref), channel_id=1, source_target_pairs={{0,1},{1,0},{2,3},{3,2},{4,5},{5,4},{6,7},{7,6},{8,9},{9,8},{10,11... | collective-permute-start | bytes 3145736 | tf_op jit(solution)/shard_map/ppermute | solution.py:798
  42.3 43.9 %collective-permute-start.1 = (f32[32,64,128]{2,1,0:T(8,128)S(1)}, f32[32,64,128]{2,1,0:T(8,128)S(1)}, u32[]{:S(2)}, u32[]{:S(2)}) collective-permute-start(f32[32,64,128]{2,1,0:T(8,128)S(1)} %all_to_all.10.recv_ref.own_ref), channel_id=1, source_target_pairs={{0,2},{1,3},{2,0},{3,1},{4,6},{5,7},{6,4},{7,5},{8,10},{9,11},{10,... | collective-permute-start | bytes 3145736 | tf_op jit(solution)/shard_map/ppermute | solution.py:798
  43.3 46.7 %collective-permute-start.2 = (f32[32,64,128]{2,1,0:T(8,128)S(1)}, f32[32,64,128]{2,1,0:T(8,128)}, u32[]{:S(2)}, u32[]{:S(2)}) collective-permute-start(f32[32,64,128]{2,1,0:T(8,128)S(1)} %all_to_all.10.recv_ref.own_ref), channel_id=1, source_target_pairs={{0,3},{1,2},{2,1},{3,0},{4,7},{5,6},{6,5},{7,4},{8,11},{9,10},{10,... | collective-permute-start | bytes 3145736 | tf_op jit(solution)/shard_map/ppermute | solution.py:798
  86.1 12.2 %copy-start.9 = (f32[64,64]{1,0:T(8,128)S(1)}, f32[64,64]{1,0:T(8,128)}, u32[]{:S(2)}) copy-start(f32[64,64]{1,0:T(8,128)} %param.19) | copy-start | bytes 49156
  86.1 12.2 %copy-start.10 = (s32[64]{0:T(128)S(1)}, s32[64]{0:T(128)}, u32[]{:S(2)}) copy-start(s32[64]{0:T(128)} %param.18) | copy-start | bytes 772
  86.1 3.9 %copy-start.7 = (f32[32,64,128]{2,1,0:T(8,128)}, f32[32,64,128]{2,1,0:T(8,128)S(1)}, u32[]{:S(2)}) copy-start(f32[32,64,128]{2,1,0:T(8,128)S(1)} %collective-permute-done.one_ref) | copy-start | bytes 3145732
  86.2 3.9 %copy-start.8 = (f32[32,64,128]{2,1,0:T(8,128)}, f32[32,64,128]{2,1,0:T(8,128)S(1)}, u32[]{:S(2)}) copy-start(f32[32,64,128]{2,1,0:T(8,128)S(1)} %collective-permute-done.1.two_ref) | copy-start | bytes 3145732
  93.9 21.8 %all-to-all-start.1 = ((f32[32,56,128]{2,1,0:T(8,128)}), f32[32,56,128]{2,1,0:T(8,128)S(1)}, u32[]{:S(2)}, u32[]{:S(2)}) async-start(f32[32,56,128]{2,1,0:T(8,128)} %get-tuple-element.17), calls=%async_computation.1 | async-start | bytes 1835008 | tf_op jit(solution)/shard_map/all_to_all | solution.py:801
  99.0 16.6 %copy-start.1 = (s32[12288]{0:T(1024)S(1)}, s32[12288]{0:T(1024)}, u32[]{:S(2)}) copy-start(s32[12288]{0:T(1024)} %param.17) | copy-start | bytes 147460
  99.0 16.6 %copy-start.3 = (bf16[512,1536]{1,0:T(8,128)(2,1)S(1)}, bf16[512,1536]{1,0:T(8,128)(2,1)}, u32[]{:S(2)}) copy-start(bf16[512,1536]{1,0:T(8,128)(2,1)} %constant.21.clone.table_ref) | copy-start | bytes 4718596
  99.0 16.6 %copy-start.4 = (f32[16,8,128]{2,1,0:T(8,128)S(1)}, f32[16,8,128]{2,1,0:T(8,128)}, u32[]{:S(2)}) copy-start(f32[16,8,128]{2,1,0:T(8,128)} %get-tuple-element.15.key_ref) | copy-start | bytes 196612
  99.0 16.6 %copy-start.5 = (s32[2,16]{1,0:T(2,128)S(1)}, s32[2,16]{1,0:T(2,128)}, u32[]{:S(2)}) copy-start(s32[2,16]{1,0:T(2,128)} %get-tuple-element.14.span_ref) | copy-start | bytes 388
  115.6 0.9 copy-start
  116.5 0.7 copy-start.2

commit v6 on v5

--- a/solution.py
+++ b/solution.py
@@ -30,11 +30,11 @@
 CHUNKS = 16
 NQ = 4
 NCH = 3
-PAIR = 4
+PAIR = 8
 PLACE_UNROLL = 4
 PICK_UNROLL = 6
 GRAM_STEPS = 2
-FETCH_UNROLL = 4
+FETCH_UNROLL = 16
 F32 = jnp.float32
 BF16 = jnp.bfloat16
 NN = (((1,), (0,)), ((), ()))
@@ -209,13 +209,19 @@
     return (square + z * z) * (KIN_MAX / 3.0 / 16384.0)
 
 
-def spread_kernel(slot_ref, tile_ref, coef_ref, proj_ref, stick_ref, table_hbm, out_ref, key_ref, kinetic_ref,
-                  span_ref, parts, acc, becp, table_ref, table_sem):
+def spread_kernel(slot_ref, tile_ref, coef_ref, proj_hbm, stick_ref, table_hbm, out_ref, key_ref, kinetic_ref,
+                  span_ref, parts, acc, becp, table_ref, proj_buf, table_sem, proj_sems):
     step = pl.program_id(0)
     table_copy = pltpu.make_async_copy(table_hbm, table_ref, table_sem)
 
+    def proj_copy(at):
+        here = pl.ds(pl.multiple_of(at * KC, KC), KC)
+        return pltpu.make_async_copy(proj_hbm.at[:, :, here], proj_buf.at[at], proj_sems.at[at])
+
     @pl.when(step == 0)
     def _():
+        for at in range(COEFS // KC):
+            proj_copy(at).start()
         table_copy.start()
         slot = slot_ref[...].astype(F32)
         z = jnp.floor((slot + 0.5) * (1.0 / STICKS))
@@ -290,8 +296,9 @@
 
     c_re = coef_ref[0]
     c_im = coef_ref[1]
-    p_re = proj_ref[0]
-    p_im = proj_ref[1]
+    proj_copy(step).wait()
+    p_re = proj_buf[step, 0]
+    p_im = proj_buf[step, 1]
     real = p_re * c_re + p_im * c_im
     imag = p_re * c_im - p_im * c_re
     both = jnp.concatenate([real, imag], axis=0)
@@ -329,7 +336,7 @@
             pl.BlockSpec((128, 128), lambda i: (0, 0)),
             pl.BlockSpec((2, 128, 128), lambda i: (0, 0, 0)),
             pl.BlockSpec((2, 1, KC), lambda i: (0, 0, i)),
-            pl.BlockSpec((2, PROJ, KC), lambda i: (0, 0, i)),
+            pl.BlockSpec(memory_space=pl.ANY),
             pl.BlockSpec((PW * TILES, 128), lambda i: (0, 0)),
             pl.BlockSpec(memory_space=pl.ANY),
         ],
@@ -350,7 +357,9 @@
             pltpu.VMEM((SLOT_ROWS + WINDOW, 512), F32),
             pltpu.VMEM((128, 128), F32),
             pltpu.VMEM((512, 1536), BF16),
+            pltpu.VMEM((COEFS // KC, 2, PROJ, KC), F32),
             pltpu.SemaphoreType.DMA,
+            pltpu.SemaphoreType.DMA((COEFS // KC,)),
         ],
         compiler_params=pltpu.CompilerParams(vmem_limit_bytes=60 << 20),
         cost_estimate=pl.CostEstimate(flops=6 * 10 ** 9, bytes_accessed=12 << 20, transcendentals=0),
@@ -373,13 +382,9 @@
 
 
 def write_bounds(columns, bounds):
-    firsts, lasts = [], []
-    for column in columns:
-        chunk = jnp.floor(fold(jnp.floor(column * (1.0 / GY)))[0] * 0.125)
-        firsts.append(jnp.min(chunk, axis=1, keepdims=True))
-        lasts.append(jnp.max(chunk, axis=1, keepdims=True))
-    first = jnp.broadcast_to(jnp.concatenate(firsts, axis=0), (GROUPS, 128))
-    last = jnp.broadcast_to(jnp.concatenate(lasts, axis=0), (GROUPS, 128))
+    chunk = jnp.floor(fold(jnp.floor(jnp.concatenate(columns, axis=0) * (1.0 / GY)))[0] * 0.125)
+    first = jnp.broadcast_to(jnp.min(chunk, axis=1, keepdims=True), (GROUPS, 128))
+    last = jnp.broadcast_to(jnp.max(chunk, axis=1, keepdims=True), (GROUPS, 128))
     lane = iota((GROUPS, 128), 1)
     start = jnp.sum(jnp.where(last < lane, 1.0, 0.0), axis=0, keepdims=True)
     end = jnp.sum(jnp.where(first <= lane, 1.0, 0.0), axis=0, keepdims=True)
@@ -393,10 +398,14 @@
     bounds[...] = jnp.concatenate(lines, axis=0).astype(jnp.int32)
 
 
-def field_kernel(recv_ref, field_hbm, y_in_ref, y_out_ref, x_in_ref, x_out_ref, out_ref,
-                 wide, hot, keys, signs, grid, done, sticks, field_ref, bounds, range_ref, field_sem, range_sem):
-    field_copy = pltpu.make_async_copy(field_hbm, field_ref, field_sem)
-    field_copy.start()
+def field_kernel(recv_ref, field_hbm, y_in_hbm, y_out_hbm, x_in_hbm, x_out_hbm, out_ref,
+                 wide, hot, keys, signs, grid, done, sticks, field_ref, y_in_ref, y_out_ref, x_in_ref, x_out_ref,
+                 bounds, range_ref, sems, range_sem):
+    copies = [pltpu.make_async_copy(source, target, sems.at[at]) for at, (source, target) in enumerate((
+        (field_hbm, field_ref), (y_in_hbm, y_in_ref), (y_out_hbm, y_out_ref),
+        (x_in_hbm, x_in_ref), (x_out_hbm, x_out_ref)))]
+    for copy in copies:
+        copy.start()
     cells = []
     for g in range(4):
         mixed = swap_chunks([recv_ref[g * 8 + i, TILES * ROWS:TILES * ROWS + 8, :] for i in range(8)])
@@ -511,7 +520,8 @@
             plane(pair * PAIR + at)
         return carry
 
-    field_copy.wait()
+    for copy in copies:
+        copy.wait()
     lax.fori_loop(0, PLANES // PAIR, planes, 0)
 
     def pick(q, first, chunks):
@@ -559,7 +569,7 @@
     vmem = pl.BlockSpec(memory_space=pltpu.VMEM)
     return pl.pallas_call(
         field_kernel,
-        in_specs=[vmem, pl.BlockSpec(memory_space=pl.ANY)] + [vmem] * 4,
+        in_specs=[vmem] + [pl.BlockSpec(memory_space=pl.ANY)] * 5,
         out_specs=vmem,
         out_shape=jax.ShapeDtypeStruct((PW, 48, 128), F32),
         scratch_shapes=[
@@ -571,12 +581,16 @@
             pltpu.VMEM((ROWS, GX + 16 * (NCH - 1), 512), BF16),
             pltpu.VMEM((GROUPS, ROWS, 512), F32),
             pltpu.VMEM((PLANES, GX, GY), F32),
+            pltpu.VMEM((768, 256), BF16),
+            pltpu.VMEM((768, 256), BF16),
+            pltpu.VMEM((256, 768), BF16),
+            pltpu.VMEM((256, 768), BF16),
             pltpu.VMEM((8, 128), jnp.int32),
             pltpu.SMEM((8, 128), jnp.int32),
-            pltpu.SemaphoreType.DMA,
+            pltpu.SemaphoreType.DMA((5,)),
             pltpu.SemaphoreType.DMA,
         ],
-        compiler_params=pltpu.CompilerParams(vmem_limit_bytes=60 << 20),
+        compiler_params=pltpu.CompilerParams(vmem_limit_bytes=48 << 20),
         cost_estimate=pl.CostEstimate(flops=35 * 10 ** 9, bytes_accessed=8 << 20, transcendentals=0),
         name="apply_field",
     )(recv, field, *plane_tables())
@@ -640,7 +654,7 @@
         out_specs=[pl.BlockSpec((PW, 56, 128), lambda i: (0, 0, 0)), pl.BlockSpec((4, 8, 128), lambda i: (0, 0, 0))],
         out_shape=[jax.ShapeDtypeStruct((PW, 56, 128), F32), jax.ShapeDtypeStruct((4, 8, 128), F32)],
         scratch_shapes=[pltpu.VMEM((8, PLANES, 128), F32), pltpu.VMEM((16, 8, 128), F32)],
-        compiler_params=pltpu.CompilerParams(vmem_limit_bytes=60 << 20),
+        compiler_params=pltpu.CompilerParams(vmem_limit_bytes=16 << 20),
         cost_estimate=pl.CostEstimate(flops=10 ** 7, bytes_accessed=6 << 20, transcendentals=0),
         name="gram_part",
     )(recv, *others, worked)
@@ -686,7 +700,7 @@
         out_specs=[pl.BlockSpec((2, 1, KC), lambda i: (0, 0, i)), pl.BlockSpec((8, 128), lambda i: (0, 0))],
         out_shape=[jax.ShapeDtypeStruct((2, 1, COEFS), F32), jax.ShapeDtypeStruct((8, 128), F32)],
         scratch_shapes=[pltpu.VMEM((2, PROJ, 128), F32)],
-        compiler_params=pltpu.CompilerParams(vmem_limit_bytes=60 << 20),
+        compiler_params=pltpu.CompilerParams(vmem_limit_bytes=16 << 20),
         cost_estimate=pl.CostEstimate(flops=10 ** 7, bytes_accessed=10 << 20, transcendentals=0),
         name="base_part",
     )(kinetic, coef, proj, matrix, becp)

time: 126 us -> 121 us (0.960)
  Pallas kernels: 72.5 us -> 63.9 us
  waiting for transfers between devices: 14 us -> 16.9 us
  local copies, waits for them, and re-layouts: 1.69 us -> 3.52 us
    pallas_call x1, Pallas kernels: 42 us -> 38.9 us  [apply_field(): pl.pallas_call(field_kernel, in_specs=[vmem] + [pl.BlockSpec(memory_space...]
    pallas_call x1, Pallas kernels: 6.37 us -> 3.43 us  [base_part(): pl.pallas_call(base_kernel, grid=(COEFS // KC,), in_specs=[pl.BlockSpec((...]
    ppermute x3, waiting for transfers between devices: 3.86 us -> 6.8 us  [local(): lax.ppermute(recv, 'band', [(b, b ^ m) for b in range(4)])]
    pallas_call x1, Pallas kernels: 3.83 us -> 1.85 us  [gram_part(): pl.pallas_call(gram_kernel, grid=(GRAM_STEPS,), in_specs=[pl.BlockSpec((s...]
    unnamed x23 -> x29, local copies, waits for them, and re-layouts: 1.69 us -> 3.52 us
  transfers between devices with their start and end apart: 4 -> 4, of which waited for: 2 -> 2; matrix products, arithmetic and copies ran while one was open for 1% -> 0% of each run, Pallas kernels for 39% -> 35%
where the time goes in v6:
time: 121 us
  Pallas kernels  63.9 us (53%)
  blocking collectives  29.1 us (24%)
  waiting for transfers between devices  16.9 us (14%)
  starting transfers between devices  6.66 us (6%)
  local copies, waits for them, and re-layouts  3.52 us (3%)
    pallas_call x1, Pallas kernels, apply_field(): pl.pallas_call(field_kernel, in_specs=[vmem] + [pl.BlockSpec(memory_space...  38.9 us
    all_to_all x1, blocking collectives, local(): recv = lax.all_to_all(sent, 'pw', split_axis=0, concat_axis=0, tiled=True)  29.1 us
    pallas_call x1, Pallas kernels, spread_sticks(): pl.pallas_call(spread_kernel, grid=(COEFS // KC,), in_specs=[pl.BlockSpec...  11.9 us
    all_to_all x1, waiting for transfers between devices, local(): lax.all_to_all(payload, 'pw', split_axis=0, concat_axis=0, tiled=True)  10.1 us
    pallas_call x1, Pallas kernels, collect(): pl.pallas_call(collect_kernel, in_specs=[pl.BlockSpec(memory_space=pltpu....  7.79 us
    ppermute x3, waiting for transfers between devices, local(): lax.ppermute(recv, 'band', [(b, b ^ m) for b in range(4)])  6.8 us
    all_to_all x1, starting transfers between devices, local(): lax.all_to_all(payload, 'pw', split_axis=0, concat_axis=0, tiled=True)  4.8 us
    unnamed x29, local copies, waits for them, and re-layouts  3.52 us
  transfers between devices with their start and end apart: 4, of which 2 were waited for; matrix products, arithmetic and copies ran while one was open for 0% of the time, Pallas kernels for 35%

profile of v6, /device:TPU:0, one launch (start us, length us, event | category | flops | bytes accessed | tf_op | source)
XLA Modules:
  0.0 121.0 jit_solution(9072527717373548167)
XLA Ops:
  0.6 0.0 copy-start.6
  0.6 0.0 copy-start.7
  0.7 0.0 copy-start.8
  0.7 0.0 copy-start.9
  0.7 11.9 %spread_sticks.1 = (f32[32,64,128]{2,1,0:T(8,128)}, f32[16,8,128]{2,1,0:T(8,128)}, f32[128,128]{1,0:T(8,128)}, s32[2,16]{1,0:T(2,128)}) custom-call(s32[128,128]{1,0:T(8,128)} %bitcast.23, f32[2,128,128]{2,1,0:T(8,128)} %bitcast.18, f32[2,1,16384]{2,1,0:T(1,128)} %coef_ref.3, f32[2,64,16384]{2,1,0:T(8,128)} %proj_ref.1, s32[96,128]{1,0:T(8,128)} %bitcast.21, ...), custom_call_target="tpu_custom_call" | custom-call | flops 6000000000 | bytes 12582912 | tf_op jit(solution)/shard_map/spread_sticks/pallas_call | solution.py:332
  12.6 0.0 copy-start.3
  12.6 29.1 %all_to_all.10.recv_ref.own_ref = f32[32,64,128]{2,1,0:T(8,128)S(1)} all-to-all(f32[32,64,128]{2,1,0:T(8,128)} %get-tuple-element.16), channel_id=1, replica_groups=mesh['pw'=32,'band'=4] {'pw'}, dimensions={0} | all-to-all | bytes 2097152 | tf_op jit(solution)/shard_map/all_to_all | solution.py:811
  41.8 0.0 collective-permute-start
  41.8 1.0 collective-permute-start.1
  42.8 0.8 collective-permute-start.2
  43.6 38.9 %apply_field.1.worked_ref = f32[32,48,128]{2,1,0:T(8,128)S(1)} custom-call(f32[32,64,128]{2,1,0:T(8,128)S(1)} %all_to_all.10.recv_ref.own_ref, f32[8,256,256]{2,1,0:T(8,128)S(1)} %copy-done.3, bf16[768,256]{1,0:T(8,128)(2,1)S(1)} %copy-done.6, bf16[768,256]{1,0:T(8,128)(2,1)S(1)} %copy-done.7, bf16[256,768]{1,0:T(8,128)(2,1)S(1)} %copy-done.8, ...), custom_call_target="tpu_custom_call" | custom-call | flops 35000000512 | bytes 8388608 | tf_op jit(solution)/shard_map/apply_field/pallas_call | solution.py:570
  82.6 0.0 copy-start.12
  82.6 0.0 copy-start.13
  82.6 0.0 collective-permute-done.1.two_ref
  82.6 6.8 %collective-permute-done.2.three_ref = f32[32,64,128]{2,1,0:T(8,128)S(1)} collective-permute-done((f32[32,64,128]{2,1,0:T(8,128)S(1)}, f32[32,64,128]{2,1,0:T(8,128)S(1)}, u32[]{:S(2)}, u32[]{:S(2)}) %collective-permute-start.2) | collective-permute-done | bytes 1048608 | tf_op jit(solution)/shard_map/ppermute | solution.py:812
  89.4 1.9 %gram_part.1 = (f32[32,56,128]{2,1,0:T(8,128)}, f32[4,8,128]{2,1,0:T(8,128)S(1)}) custom-call(f32[32,64,128]{2,1,0:T(8,128)S(1)} %all_to_all.10.recv_ref.own_ref, f32[32,64,128]{2,1,0:T(8,128)S(1)} %collective-permute-done.one_ref, f32[32,64,128]{2,1,0:T(8,128)S(1)} %collective-permute-done.1.two_ref, f32[32,64,128]{2,1,0:T(8,128)S(1)} %collective-permute-done.2.three_ref, ...), custom_call_target="tpu_custom_call" | custom-call | flops 10000000 | bytes 6291456 | tf_op jit(solution)/shard_map/gram_part/pallas_call | solution.py:648
  91.3 4.8 %all-to-all-start.1 = ((f32[32,56,128]{2,1,0:T(8,128)}), f32[32,56,128]{2,1,0:T(8,128)S(1)}, u32[]{:S(2)}, u32[]{:S(2)}) async-start(f32[32,56,128]{2,1,0:T(8,128)} %get-tuple-element.17), calls=%async_computation.1 | async-start | bytes 1835008 | tf_op jit(solution)/shard_map/all_to_all | solution.py:815
  96.1 0.1 copy.16
  96.2 0.1 fusion.1.matrix_ref
  96.3 0.0 copy-start
  96.3 3.4 %copy-done = f32[2,64,16384]{2,1,0:T(8,128)S(1)} copy-done((f32[2,64,16384]{2,1,0:T(8,128)S(1)}, f32[2,64,16384]{2,1,0:T(8,128)}, u32[]{:S(2)}) %copy-start) | copy-done | bytes 8388632
  99.7 3.4 %base_part.1 = (f32[2,1,16384]{2,1,0:T(1,128)S(1)}, f32[8,128]{1,0:T(8,128)S(1)}) custom-call(f32[1,16384]{1,0:T(1,128)S(1)} %bitcast.19, f32[2,1,16384]{2,1,0:T(1,128)S(1)} %copy-done.1, f32[2,64,16384]{2,1,0:T(8,128)S(1)} %copy-done, f32[64,64]{1,0:T(8,128)S(1)} %fusion.1.matrix_ref, f32[4,8,128]{2,1,0:T(8,128)S(1)} %get-tuple-element.19.becp_ref), custom_call_target="tpu_custom_call" | custom-call | flops 10000000 | bytes 10485760 | tf_op jit(solution)/shard_map/base_part/pallas_call | solution.py:690
  103.1 10.1 %all-to-all-done.1.recv_ref = f32[32,56,128]{2,1,0:T(8,128)S(1)} async-done(((f32[32,56,128]{2,1,0:T(8,128)}), f32[32,56,128]{2,1,0:T(8,128)S(1)}, u32[]{:S(2)}, u32[]{:S(2)}) %all-to-all-start.1) | async-done | bytes 917536 | tf_op jit(solution)/shard_map/all_to_all | solution.py:815
  113.2 7.8 %collect.1 = (f32[2,128,128]{2,1,0:T(8,128)}, f32[2,1,4]{2,1,0:T(1,128)}, f32[2,1,4]{2,1,0:T(1,128)}) custom-call(s32[2,16]{1,0:T(2,128)S(1)} %copy-done.11, f32[16,8,128]{2,1,0:T(8,128)S(1)} %copy-done.10, f32[32,56,128]{2,1,0:T(8,128)S(1)} %all-to-all-done.1.recv_ref, s32[96,128]{1,0:T(8,128)S(1)} %bitcast.22, bf16[512,1536]{1,0:T(8,128)(2,1)S(1)} %copy-done.5, ...), custom_call_target="tpu_custom_call" | custom-call | flops 6000000000 | bytes 4194304 | tf_op jit(solution)/shard_map/collect/pallas_call | solution.py:788
  (20 shorter events, 0.0 us)
Async XLA Ops:
  0.6 43.0 %copy-start.6 = (bf16[768,256]{1,0:T(8,128)(2,1)S(1)}, bf16[768,256]{1,0:T(8,128)(2,1)}, u32[]{:S(2)}) copy-start(bf16[768,256]{1,0:T(8,128)(2,1)} %constant.17.clone.y_in_hbm) | copy-start | bytes 1179652
  0.6 43.0 %copy-start.7 = (bf16[768,256]{1,0:T(8,128)(2,1)S(1)}, bf16[768,256]{1,0:T(8,128)(2,1)}, u32[]{:S(2)}) copy-start(bf16[768,256]{1,0:T(8,128)(2,1)} %constant.18.clone.y_out_hbm) | copy-start | bytes 1179652
  0.7 43.0 %copy-start.8 = (bf16[256,768]{1,0:T(8,128)(2,1)S(1)}, bf16[256,768]{1,0:T(8,128)(2,1)}, u32[]{:S(2)}) copy-start(bf16[256,768]{1,0:T(8,128)(2,1)} %constant.19.clone.x_in_hbm) | copy-start | bytes 1179652
  0.7 43.0 %copy-start.9 = (bf16[256,768]{1,0:T(8,128)(2,1)S(1)}, bf16[256,768]{1,0:T(8,128)(2,1)}, u32[]{:S(2)}) copy-start(bf16[256,768]{1,0:T(8,128)(2,1)} %constant.20.clone.x_out_hbm) | copy-start | bytes 1179652
  12.6 31.0 %copy-start.3 = (f32[8,256,256]{2,1,0:T(8,128)S(1)}, f32[8,256,256]{2,1,0:T(8,128)}, u32[]{:S(2)}) copy-start(f32[8,256,256]{2,1,0:T(8,128)} %field_hbm.1) | copy-start | bytes 6291460
  41.8 40.8 %collective-permute-start = (f32[32,64,128]{2,1,0:T(8,128)S(1)}, f32[32,64,128]{2,1,0:T(8,128)S(1)}, u32[]{:S(2)}, u32[]{:S(2)}) collective-permute-start(f32[32,64,128]{2,1,0:T(8,128)S(1)} %all_to_all.10.recv_ref.own_ref), channel_id=1, source_target_pairs={{0,1},{1,0},{2,3},{3,2},{4,5},{5,4},{6,7},{7,6},{8,9},{9,8},{10,11... | collective-permute-start | bytes 3145736 | tf_op jit(solution)/shard_map/ppermute | solution.py:812
  41.8 40.8 %collective-permute-start.1 = (f32[32,64,128]{2,1,0:T(8,128)S(1)}, f32[32,64,128]{2,1,0:T(8,128)S(1)}, u32[]{:S(2)}, u32[]{:S(2)}) collective-permute-start(f32[32,64,128]{2,1,0:T(8,128)S(1)} %all_to_all.10.recv_ref.own_ref), channel_id=1, source_target_pairs={{0,2},{1,3},{2,0},{3,1},{4,6},{5,7},{6,4},{7,5},{8,10},{9,11},{10,... | collective-permute-start | bytes 3145736 | tf_op jit(solution)/shard_map/ppermute | solution.py:812
  42.8 46.6 %collective-permute-start.2 = (f32[32,64,128]{2,1,0:T(8,128)S(1)}, f32[32,64,128]{2,1,0:T(8,128)S(1)}, u32[]{:S(2)}, u32[]{:S(2)}) collective-permute-start(f32[32,64,128]{2,1,0:T(8,128)S(1)} %all_to_all.10.recv_ref.own_ref), channel_id=1, source_target_pairs={{0,3},{1,2},{2,1},{3,0},{4,7},{5,6},{6,5},{7,4},{8,11},{9,10},{10,... | collective-permute-start | bytes 3145736 | tf_op jit(solution)/shard_map/ppermute | solution.py:812
  82.6 13.5 %copy-start.12 = (f32[64,64]{1,0:T(8,128)S(1)}, f32[64,64]{1,0:T(8,128)}, u32[]{:S(2)}) copy-start(f32[64,64]{1,0:T(8,128)} %param.19) | copy-start | bytes 49156
  82.6 13.6 %copy-start.13 = (s32[64]{0:T(128)S(1)}, s32[64]{0:T(128)}, u32[]{:S(2)}) copy-start(s32[64]{0:T(128)} %param.18) | copy-start | bytes 772
  82.6 13.7 %copy-start.2 = (f32[128,128]{1,0:T(8,128)S(1)}, f32[128,128]{1,0:T(8,128)}, u32[]{:S(2)}) copy-start(f32[128,128]{1,0:T(8,128)} %get-tuple-element.18) | copy-start | bytes 196612
  91.3 5.0 %copy-start.1 = (f32[2,1,16384]{2,1,0:T(1,128)S(1)}, f32[2,1,16384]{2,1,0:T(1,128)}, u32[]{:S(2)}) copy-start(f32[2,1,16384]{2,1,0:T(1,128)} %coef_ref.3) | copy-start | bytes 393220
  91.3 21.9 %all-to-all-start.1 = ((f32[32,56,128]{2,1,0:T(8,128)}), f32[32,56,128]{2,1,0:T(8,128)S(1)}, u32[]{:S(2)}, u32[]{:S(2)}) async-start(f32[32,56,128]{2,1,0:T(8,128)} %get-tuple-element.17), calls=%async_computation.1 | async-start | bytes 1835008 | tf_op jit(solution)/shard_map/all_to_all | solution.py:815
  96.3 3.4 %copy-start = (f32[2,64,16384]{2,1,0:T(8,128)S(1)}, f32[2,64,16384]{2,1,0:T(8,128)}, u32[]{:S(2)}) copy-start(f32[2,64,16384]{2,1,0:T(8,128)} %proj_ref.1) | copy-start | bytes 25165828
  99.7 13.5 %copy-start.4 = (s32[12288]{0:T(1024)S(1)}, s32[12288]{0:T(1024)}, u32[]{:S(2)}) copy-start(s32[12288]{0:T(1024)} %param.17) | copy-start | bytes 147460
  99.7 13.5 %copy-start.5 = (bf16[512,1536]{1,0:T(8,128)(2,1)S(1)}, bf16[512,1536]{1,0:T(8,128)(2,1)}, u32[]{:S(2)}) copy-start(bf16[512,1536]{1,0:T(8,128)(2,1)} %constant.21.clone.table_ref) | copy-start | bytes 4718596
  99.7 13.5 %copy-start.10 = (f32[16,8,128]{2,1,0:T(8,128)S(1)}, f32[16,8,128]{2,1,0:T(8,128)}, u32[]{:S(2)}) copy-start(f32[16,8,128]{2,1,0:T(8,128)} %get-tuple-element.15.key_ref) | copy-start | bytes 196612
  99.7 13.5 %copy-start.11 = (s32[2,16]{1,0:T(2,128)S(1)}, s32[2,16]{1,0:T(2,128)}, u32[]{:S(2)}) copy-start(s32[2,16]{1,0:T(2,128)} %get-tuple-element.14.span_ref) | copy-start | bytes 388

commit v7 on v6

--- a/solution.py
+++ b/solution.py
@@ -23,7 +23,7 @@
 ROWS = 2 * PLANES
 KC = 4096
 STEP_BLOCKS = KC // 1024
-WINDOW = 256
+WINDOW = 320
 SLOT_ROWS = 768
 TILES = STICKS // 128
 GROUPS = 24
@@ -255,7 +255,7 @@
             last = jnp.max(key_parts(keys[half + 7][at:at + 1])[0]).astype(jnp.int32)
             first = (first >> 4) << 4
             span_ref[0, block] = first
-            span_ref[1, block] = ((last - first) >> 8) + 1
+            span_ref[1, block] = lax.div(last - first, WINDOW) + 1
         acc[...] = jnp.zeros_like(acc)
         becp[...] = jnp.zeros_like(becp)
 
@@ -596,19 +596,8 @@
     )(recv, field, *plane_tables())
 
 
-def gram_kernel(own_ref, one_ref, two_ref, three_ref, worked_ref, out_ref, becp_ref, total, small):
-    step = pl.program_id(0)
-
-    @pl.when(step == 0)
-    def _():
-        total[...] = jnp.zeros_like(total)
-        small[...] = jnp.zeros_like(small)
-        becp_ref[...] = jnp.zeros_like(becp_ref)
-
-    span = PW // GRAM_STEPS
-    here = pl.ds(pl.multiple_of(step * span, span), span)
+def add_pairs(span, own_ref, refs, worked_ref, total, small, becp_ref):
     worked = worked_ref[...].reshape(span * TILES, 2, PLANES, 128)
-    out_ref[here, :TILES * ROWS, :] = worked_ref[...]
     w_re = worked[:, 0]
     w_im = worked[:, 1]
     upper = lax.broadcasted_iota(jnp.int32, (span * 8, 128), 0) % 8 < 4
@@ -620,7 +609,7 @@
 
     turned = jnp.where(upper, halves(mine), -halves(mine))
     weight = jnp.where(upper, halves(weight), weight)
-    for a, ref in enumerate((own_ref, one_ref, two_ref, three_ref)):
+    for a, ref in refs.items():
         lines = ref[:, :TILES * ROWS, :].reshape(span * TILES, 2, PLANES, 128)
         a_re = lines[:, 0]
         a_im = lines[:, 1]
@@ -633,6 +622,31 @@
         for at, value in ((a, real * weight), (4 + a, imag * weight), (8 + a, real), (12 + a, imag)):
             small[at] += jnp.sum(value.reshape(span, 8, 128), axis=0)
 
+
+def first_kernel(own_ref, one_ref, two_ref, worked_ref, total, small, becp_ref):
+    @pl.when(pl.program_id(0) == 0)
+    def _():
+        total[...] = jnp.zeros_like(total)
+        small[...] = jnp.zeros_like(small)
+        becp_ref[...] = jnp.zeros_like(becp_ref)
+
+    add_pairs(PW // GRAM_STEPS, own_ref, {0: own_ref, 1: one_ref, 2: two_ref}, worked_ref, total, small, becp_ref)
+
+
+def last_kernel(total_ref, small_ref, sums_ref, own_ref, three_ref, worked_ref, out_ref, becp_ref, total, small):
+    step = pl.program_id(0)
+
+    @pl.when(step == 0)
+    def _():
+        total[...] = total_ref[...]
+        small[...] = small_ref[...]
+        becp_ref[...] = sums_ref[...]
+
+    span = PW // GRAM_STEPS
+    here = pl.ds(pl.multiple_of(step * span, span), span)
+    out_ref[here, :TILES * ROWS, :] = worked_ref[...]
+    add_pairs(span, own_ref, {3: three_ref}, worked_ref, total, small, becp_ref)
+
     @pl.when(step == pl.num_programs(0) - 1)
     def _():
         scale = 1.0 / (GX * GY * GZ)
@@ -643,21 +657,40 @@
         out_ref[:, TILES * ROWS:, :] = jnp.broadcast_to(line[None], (PW, 8, 128))
 
 
-def gram_part(recv, others, worked):
+SUM_SHAPES = ((8, PLANES, 128), (16, 8, 128), (4, 8, 128))
+
+
+def gram_first(sticks, worked):
     span = PW // GRAM_STEPS
     return pl.pallas_call(
-        gram_kernel,
+        first_kernel,
         grid=(GRAM_STEPS,),
-        in_specs=[pl.BlockSpec((span, 64, 128), lambda i: (i, 0, 0))] * 4 + [
+        in_specs=[pl.BlockSpec((span, 64, 128), lambda i: (i, 0, 0))] * 3 + [
             pl.BlockSpec((span, 48, 128), lambda i: (i, 0, 0)),
         ],
+        out_specs=[pl.BlockSpec(shape, lambda i: (0, 0, 0)) for shape in SUM_SHAPES],
+        out_shape=[jax.ShapeDtypeStruct(shape, F32) for shape in SUM_SHAPES],
+        compiler_params=pltpu.CompilerParams(vmem_limit_bytes=16 << 20),
+        cost_estimate=pl.CostEstimate(flops=10 ** 7, bytes_accessed=5 << 20, transcendentals=0),
+        name="gram_first",
+    )(*sticks, worked)
+
+
+def gram_last(sums, recv, three, worked):
+    span = PW // GRAM_STEPS
+    return pl.pallas_call(
+        last_kernel,
+        grid=(GRAM_STEPS,),
+        in_specs=[pl.BlockSpec(shape, lambda i: (0, 0, 0)) for shape in SUM_SHAPES]
+        + [pl.BlockSpec((span, 64, 128), lambda i: (i, 0, 0))] * 2
+        + [pl.BlockSpec((span, 48, 128), lambda i: (i, 0, 0))],
         out_specs=[pl.BlockSpec((PW, 56, 128), lambda i: (0, 0, 0)), pl.BlockSpec((4, 8, 128), lambda i: (0, 0, 0))],
         out_shape=[jax.ShapeDtypeStruct((PW, 56, 128), F32), jax.ShapeDtypeStruct((4, 8, 128), F32)],
         scratch_shapes=[pltpu.VMEM((8, PLANES, 128), F32), pltpu.VMEM((16, 8, 128), F32)],
         compiler_params=pltpu.CompilerParams(vmem_limit_bytes=16 << 20),
-        cost_estimate=pl.CostEstimate(flops=10 ** 7, bytes_accessed=6 << 20, transcendentals=0),
-        name="gram_part",
-    )(recv, *others, worked)
+        cost_estimate=pl.CostEstimate(flops=10 ** 7, bytes_accessed=4 << 20, transcendentals=0),
+        name="gram_last",
+    )(*sums, recv, three, worked)
 
 
 def base_kernel(kinetic_ref, coef_ref, proj_ref, matrix_ref, becp_ref, out_ref, far_ref, weight):
@@ -809,9 +842,12 @@
     stick = stick_column.reshape(PW * TILES, 128)
     sent, key, kinetic, span = spread_sticks(grid_slot.reshape(128, 128), wave_coef, projector, stick)
     recv = lax.all_to_all(sent, "pw", split_axis=0, concat_axis=0, tiled=True)
-    others = [lax.ppermute(recv, "band", [(b, b ^ m) for b in range(4)]) for m in (1, 2, 3)]
+    one = lax.ppermute(recv, "band", [(b, b ^ 1) for b in range(4)])
+    two = lax.ppermute(recv, "band", [(b, b ^ 2) for b in range(4)])
     worked = apply_field(recv, potential)
-    payload, becp = gram_part(recv, others, worked)
+    late, _ = lax.optimization_barrier((two, worked))
+    three = lax.ppermute(late, "band", [(b, b ^ 1) for b in range(4)])
+    payload, becp = gram_last(gram_first((recv, one, two), worked), recv, three, worked)
     returned = lax.all_to_all(payload, "pw", split_axis=0, concat_axis=0, tiled=True)
 
     same_atom = proj_atom[:, None] == proj_atom[None, :]

time: 121 us -> 120 us (level)
  waiting for transfers between devices: 16.9 us -> 11.7 us
  Pallas kernels: 63.9 us -> 67.4 us
    ppermute x3, waiting for transfers between devices: 6.8 us -> 1.41 us  [the longest x1 1.4 us: local(): three = lax.ppermute(late, 'band', [(b, b ^ 1) for b in range(4)])]
  transfers between devices with their start and end apart: 4 -> 4, of which waited for: 2 -> 2; matrix products, arithmetic and copies ran while one was open for 0% -> 0% of each run, Pallas kernels for 35% -> 37%
where the time goes in v7:
time: 120 us; the launch traced here: 119 us
  Pallas kernels  67.4 us (56%)
  blocking collectives  29.2 us (24%)
  waiting for transfers between devices  11.7 us (10%)
  starting transfers between devices  6.84 us (6%)
  local copies, waits for them, and re-layouts  3.51 us (3%)
    pallas_call x1, Pallas kernels, apply_field(): pl.pallas_call(field_kernel, in_specs=[vmem] + [pl.BlockSpec(memory_space...  40.1 us
    all_to_all x1, blocking collectives, local(): recv = lax.all_to_all(sent, 'pw', split_axis=0, concat_axis=0, tiled=True)  29.2 us
    pallas_call x1, Pallas kernels, spread_sticks(): pl.pallas_call(spread_kernel, grid=(COEFS // KC,), in_specs=[pl.BlockSpec...  12.6 us
    all_to_all x1, waiting for transfers between devices, local(): lax.all_to_all(payload, 'pw', split_axis=0, concat_axis=0, tiled=True)  10.3 us
    pallas_call x1, Pallas kernels, collect(): pl.pallas_call(collect_kernel, in_specs=[pl.BlockSpec(memory_space=pltpu....  8.89 us
    all_to_all x1, starting transfers between devices, local(): lax.all_to_all(payload, 'pw', split_axis=0, concat_axis=0, tiled=True)  5.25 us
    unnamed x29, local copies, waits for them, and re-layouts  3.51 us
    pallas_call x1, Pallas kernels, base_part(): pl.pallas_call(base_kernel, grid=(COEFS // KC,), in_specs=[pl.BlockSpec((...  3.43 us
  transfers between devices with their start and end apart: 4, of which 2 were waited for; matrix products, arithmetic and copies ran while one was open for 0% of the time, Pallas kernels for 37%

profile of v7, /device:TPU:0, one launch (start us, length us, event | category | flops | bytes accessed | tf_op | source)
XLA Modules:
  0.0 119.4 jit_solution(16737824921667843139)
XLA Ops:
  0.6 0.0 copy-start.6
  0.6 0.0 copy-start.7
  0.7 0.0 copy-start.8
  0.7 0.0 copy-start.9
  0.7 12.6 %spread_sticks.1 = (f32[32,64,128]{2,1,0:T(8,128)}, f32[16,8,128]{2,1,0:T(8,128)}, f32[128,128]{1,0:T(8,128)}, s32[2,16]{1,0:T(2,128)}) custom-call(s32[128,128]{1,0:T(8,128)} %bitcast.23, f32[2,128,128]{2,1,0:T(8,128)} %bitcast.18, f32[2,1,16384]{2,1,0:T(1,128)} %coef_ref.3, f32[2,64,16384]{2,1,0:T(8,128)} %proj_ref.1, s32[96,128]{1,0:T(8,128)} %bitcast.21, ...), custom_call_target="tpu_custom_call" | custom-call | flops 6000000000 | bytes 12582912 | tf_op jit(solution)/shard_map/spread_sticks/pallas_call | solution.py:332
  13.3 0.0 copy-start.3
  13.3 29.2 %all_to_all.10.recv_ref.own_ref = f32[32,64,128]{2,1,0:T(8,128)S(1)} all-to-all(f32[32,64,128]{2,1,0:T(8,128)} %get-tuple-element.20), channel_id=1, replica_groups=mesh['pw'=32,'band'=4] {'pw'}, dimensions={0} | all-to-all | bytes 2097152 | tf_op jit(solution)/shard_map/all_to_all | solution.py:844
  42.4 1.0 collective-permute-start.1
  43.4 0.0 collective-permute-start
  43.5 40.1 %apply_field.1.worked_ref = f32[32,48,128]{2,1,0:T(8,128)S(1)} custom-call(f32[32,64,128]{2,1,0:T(8,128)S(1)} %all_to_all.10.recv_ref.own_ref, f32[8,256,256]{2,1,0:T(8,128)S(1)} %copy-done.3, bf16[768,256]{1,0:T(8,128)(2,1)S(1)} %copy-done.6, bf16[768,256]{1,0:T(8,128)(2,1)S(1)} %copy-done.7, bf16[256,768]{1,0:T(8,128)(2,1)S(1)} %copy-done.8, ...), custom_call_target="tpu_custom_call" | custom-call | flops 35000000512 | bytes 8388608 | tf_op jit(solution)/shard_map/apply_field/pallas_call | solution.py:570
  83.6 0.0 collective-permute-done.1.two_ref
  83.6 0.6 collective-permute-start.2
  84.2 0.0 collective-permute-done.one_ref
  84.2 0.9 gram_first.1
  85.1 1.4 %collective-permute-done.2.three_ref = f32[32,64,128]{2,1,0:T(8,128)S(1)} collective-permute-done((f32[32,64,128]{2,1,0:T(8,128)S(1)}, f32[32,64,128]{2,1,0:T(8,128)S(1)}, u32[]{:S(2)}, u32[]{:S(2)}) %collective-permute-start.2) | collective-permute-done | bytes 1048608 | tf_op jit(solution)/shard_map/ppermute | solution.py:849
  86.5 1.5 %gram_last.1 = (f32[32,56,128]{2,1,0:T(8,128)}, f32[4,8,128]{2,1,0:T(8,128)S(1)}) custom-call(f32[8,8,128]{2,1,0:T(8,128)S(1)} %get-tuple-element.21.total_ref, f32[16,8,128]{2,1,0:T(8,128)S(1)} %get-tuple-element.22.small_ref, f32[4,8,128]{2,1,0:T(8,128)S(1)} %get-tuple-element.23.sums_ref, f32[32,64,128]{2,1,0:T(8,128)S(1)} %all_to_all.10.recv_ref.own_ref, ...), custom_call_target="tpu_custom_call" | custom-call | flops 10000000 | bytes 4194304 | tf_op jit(solution)/shard_map/gram_last/pallas_call | solution.py:681
  88.0 5.3 %all-to-all-start.1 = ((f32[32,56,128]{2,1,0:T(8,128)}), f32[32,56,128]{2,1,0:T(8,128)S(1)}, u32[]{:S(2)}, u32[]{:S(2)}) async-start(f32[32,56,128]{2,1,0:T(8,128)} %get-tuple-element.25), calls=%async_computation.1 | async-start | bytes 1835008 | tf_op jit(solution)/shard_map/all_to_all | solution.py:851
  93.2 0.1 copy.16
  93.3 0.1 fusion.1.matrix_ref
  93.4 0.0 copy-start
  93.4 3.4 %copy-done = f32[2,64,16384]{2,1,0:T(8,128)S(1)} copy-done((f32[2,64,16384]{2,1,0:T(8,128)S(1)}, f32[2,64,16384]{2,1,0:T(8,128)}, u32[]{:S(2)}) %copy-start) | copy-done | bytes 8388632
  96.8 3.4 %base_part.1 = (f32[2,1,16384]{2,1,0:T(1,128)S(1)}, f32[8,128]{1,0:T(8,128)S(1)}) custom-call(f32[1,16384]{1,0:T(1,128)S(1)} %bitcast.19, f32[2,1,16384]{2,1,0:T(1,128)S(1)} %copy-done.1, f32[2,64,16384]{2,1,0:T(8,128)S(1)} %copy-done, f32[64,64]{1,0:T(8,128)S(1)} %fusion.1.matrix_ref, f32[4,8,128]{2,1,0:T(8,128)S(1)} %get-tuple-element.27.becp_ref), custom_call_target="tpu_custom_call" | custom-call | flops 10000000 | bytes 10485760 | tf_op jit(solution)/shard_map/base_part/pallas_call | solution.py:723
  100.3 10.3 %all-to-all-done.1.recv_ref = f32[32,56,128]{2,1,0:T(8,128)S(1)} async-done(((f32[32,56,128]{2,1,0:T(8,128)}), f32[32,56,128]{2,1,0:T(8,128)S(1)}, u32[]{:S(2)}, u32[]{:S(2)}) %all-to-all-start.1) | async-done | bytes 917536 | tf_op jit(solution)/shard_map/all_to_all | solution.py:851
  110.5 8.9 %collect.1 = (f32[2,128,128]{2,1,0:T(8,128)}, f32[2,1,4]{2,1,0:T(1,128)}, f32[2,1,4]{2,1,0:T(1,128)}) custom-call(s32[2,16]{1,0:T(2,128)S(1)} %copy-done.11, f32[16,8,128]{2,1,0:T(8,128)S(1)} %copy-done.10, f32[32,56,128]{2,1,0:T(8,128)S(1)} %all-to-all-done.1.recv_ref, s32[96,128]{1,0:T(8,128)S(1)} %bitcast.22, bf16[512,1536]{1,0:T(8,128)(2,1)S(1)} %copy-done.5, ...), custom_call_target="tpu_custom_call" | custom-call | flops 6000000000 | bytes 4194304 | tf_op jit(solution)/shard_map/collect/pallas_call | solution.py:821
  (21 shorter events, 0.0 us)
Async XLA Ops:
  0.6 42.8 %copy-start.6 = (bf16[768,256]{1,0:T(8,128)(2,1)S(1)}, bf16[768,256]{1,0:T(8,128)(2,1)}, u32[]{:S(2)}) copy-start(bf16[768,256]{1,0:T(8,128)(2,1)} %constant.17.clone.y_in_hbm) | copy-start | bytes 1179652
  0.6 42.8 %copy-start.7 = (bf16[768,256]{1,0:T(8,128)(2,1)S(1)}, bf16[768,256]{1,0:T(8,128)(2,1)}, u32[]{:S(2)}) copy-start(bf16[768,256]{1,0:T(8,128)(2,1)} %constant.18.clone.y_out_hbm) | copy-start | bytes 1179652
  0.7 42.8 %copy-start.8 = (bf16[256,768]{1,0:T(8,128)(2,1)S(1)}, bf16[256,768]{1,0:T(8,128)(2,1)}, u32[]{:S(2)}) copy-start(bf16[256,768]{1,0:T(8,128)(2,1)} %constant.19.clone.x_in_hbm) | copy-start | bytes 1179652
  0.7 42.8 %copy-start.9 = (bf16[256,768]{1,0:T(8,128)(2,1)S(1)}, bf16[256,768]{1,0:T(8,128)(2,1)}, u32[]{:S(2)}) copy-start(bf16[256,768]{1,0:T(8,128)(2,1)} %constant.20.clone.x_out_hbm) | copy-start | bytes 1179652
  13.3 30.2 %copy-start.3 = (f32[8,256,256]{2,1,0:T(8,128)S(1)}, f32[8,256,256]{2,1,0:T(8,128)}, u32[]{:S(2)}) copy-start(f32[8,256,256]{2,1,0:T(8,128)} %field_hbm.1) | copy-start | bytes 6291460
  42.4 41.2 %collective-permute-start.1 = (f32[32,64,128]{2,1,0:T(8,128)S(1)}, f32[32,64,128]{2,1,0:T(8,128)S(1)}, u32[]{:S(2)}, u32[]{:S(2)}) collective-permute-start(f32[32,64,128]{2,1,0:T(8,128)S(1)} %all_to_all.10.recv_ref.own_ref), channel_id=1, source_target_pairs={{0,2},{1,3},{2,0},{3,1},{4,6},{5,7},{6,4},{7,5},{8,10},{9,11},{10,... | collective-permute-start | bytes 3145736 | tf_op jit(solution)/shard_map/ppermute | solution.py:846
  43.4 40.7 %collective-permute-start = (f32[32,64,128]{2,1,0:T(8,128)S(1)}, f32[32,64,128]{2,1,0:T(8,128)S(1)}, u32[]{:S(2)}, u32[]{:S(2)}) collective-permute-start(f32[32,64,128]{2,1,0:T(8,128)S(1)} %all_to_all.10.recv_ref.own_ref), channel_id=1, source_target_pairs={{0,1},{1,0},{2,3},{3,2},{4,5},{5,4},{6,7},{7,6},{8,9},{9,8},{10,11... | collective-permute-start | bytes 3145736 | tf_op jit(solution)/shard_map/ppermute | solution.py:845
  83.6 2.9 %collective-permute-start.2 = (f32[32,64,128]{2,1,0:T(8,128)S(1)}, f32[32,64,128]{2,1,0:T(8,128)S(1)}, u32[]{:S(2)}, u32[]{:S(2)}) collective-permute-start(f32[32,64,128]{2,1,0:T(8,128)S(1)} %collective-permute-done.1.two_ref), channel_id=1, source_target_pairs={{0,1},{1,0},{2,3},{3,2},{4,5},{5,4},{6,7},{7,6},{8,9},{9,8},{10,11... | collective-permute-start | bytes 3145736 | tf_op jit(solution)/shard_map/ppermute | solution.py:849
  86.5 6.8 %copy-start.12 = (f32[64,64]{1,0:T(8,128)S(1)}, f32[64,64]{1,0:T(8,128)}, u32[]{:S(2)}) copy-start(f32[64,64]{1,0:T(8,128)} %param.19) | copy-start | bytes 49156
  86.5 6.8 %copy-start.13 = (s32[64]{0:T(128)S(1)}, s32[64]{0:T(128)}, u32[]{:S(2)}) copy-start(s32[64]{0:T(128)} %param.18) | copy-start | bytes 772
  86.5 6.9 %copy-start.1 = (f32[2,1,16384]{2,1,0:T(1,128)S(1)}, f32[2,1,16384]{2,1,0:T(1,128)}, u32[]{:S(2)}) copy-start(f32[2,1,16384]{2,1,0:T(1,128)} %coef_ref.3) | copy-start | bytes 393220
  86.5 6.9 %copy-start.2 = (f32[128,128]{1,0:T(8,128)S(1)}, f32[128,128]{1,0:T(8,128)}, u32[]{:S(2)}) copy-start(f32[128,128]{1,0:T(8,128)} %get-tuple-element.26) | copy-start | bytes 196612
  88.0 22.6 %all-to-all-start.1 = ((f32[32,56,128]{2,1,0:T(8,128)}), f32[32,56,128]{2,1,0:T(8,128)S(1)}, u32[]{:S(2)}, u32[]{:S(2)}) async-start(f32[32,56,128]{2,1,0:T(8,128)} %get-tuple-element.25), calls=%async_computation.1 | async-start | bytes 1835008 | tf_op jit(solution)/shard_map/all_to_all | solution.py:851
  93.4 3.4 %copy-start = (f32[2,64,16384]{2,1,0:T(8,128)S(1)}, f32[2,64,16384]{2,1,0:T(8,128)}, u32[]{:S(2)}) copy-start(f32[2,64,16384]{2,1,0:T(8,128)} %proj_ref.1) | copy-start | bytes 25165828
  96.8 13.7 %copy-start.4 = (s32[12288]{0:T(1024)S(1)}, s32[12288]{0:T(1024)}, u32[]{:S(2)}) copy-start(s32[12288]{0:T(1024)} %param.17) | copy-start | bytes 147460
  96.8 13.7 %copy-start.5 = (bf16[512,1536]{1,0:T(8,128)(2,1)S(1)}, bf16[512,1536]{1,0:T(8,128)(2,1)}, u32[]{:S(2)}) copy-start(bf16[512,1536]{1,0:T(8,128)(2,1)} %constant.21.clone.table_ref) | copy-start | bytes 4718596
  96.8 13.7 %copy-start.10 = (f32[16,8,128]{2,1,0:T(8,128)S(1)}, f32[16,8,128]{2,1,0:T(8,128)}, u32[]{:S(2)}) copy-start(f32[16,8,128]{2,1,0:T(8,128)} %get-tuple-element.19.key_ref) | copy-start | bytes 196612
  96.8 13.7 %copy-start.11 = (s32[2,16]{1,0:T(2,128)S(1)}, s32[2,16]{1,0:T(2,128)}, u32[]{:S(2)}) copy-start(s32[2,16]{1,0:T(2,128)} %get-tuple-element.18.span_ref) | copy-start | bytes 388

commit v8 on v7

--- a/solution.py
+++ b/solution.py
@@ -24,6 +24,7 @@
 KC = 4096
 STEP_BLOCKS = KC // 1024
 WINDOW = 320
+WINDOWS = (208, 256, 272, 288, 304, 320, 320, 320, 320, 320, 320, 304, 288, 272, 256, 208)
 SLOT_ROWS = 768
 TILES = STICKS // 128
 GROUPS = 24
@@ -34,7 +35,6 @@
 PLACE_UNROLL = 4
 PICK_UNROLL = 6
 GRAM_STEPS = 2
-FETCH_UNROLL = 16
 F32 = jnp.float32
 BF16 = jnp.bfloat16
 NN = (((1,), (0,)), ((), ()))
@@ -210,7 +210,7 @@
 
 
 def spread_kernel(slot_ref, tile_ref, coef_ref, proj_hbm, stick_ref, table_hbm, out_ref, key_ref, kinetic_ref,
-                  span_ref, parts, acc, becp, table_ref, proj_buf, table_sem, proj_sems):
+                  span_ref, order_ref, parts, acc, becp, table_ref, proj_buf, table_sem, proj_sems):
     step = pl.program_id(0)
     table_copy = pltpu.make_async_copy(table_hbm, table_ref, table_sem)
 
@@ -256,6 +256,8 @@
             first = (first >> 4) << 4
             span_ref[0, block] = first
             span_ref[1, block] = lax.div(last - first, WINDOW) + 1
+            span_ref[2, block] = WINDOWS[block]
+            span_ref[3, block] = jnp.maximum(lax.div(last - first - WINDOWS[block] + WINDOW, WINDOW), 0)
         acc[...] = jnp.zeros_like(acc)
         becp[...] = jnp.zeros_like(becp)
 
@@ -310,6 +312,7 @@
     @pl.when(step == pl.num_programs(0) - 1)
     def _():
         order, ordered = rank_of(owned_row(stick_ref))
+        order_ref[...] = order.astype(BF16)
         sticks = jnp.concatenate(
             [jnp.concatenate([acc[t * 256:(t + 1) * 256, part * 128:(part + 1) * 128] for t in range(TILES)], axis=1)
              for part in range(4)], axis=0).astype(BF16)
@@ -345,12 +348,14 @@
             pl.BlockSpec((16, 8, 128), lambda i: (0, 0, 0)),
             pl.BlockSpec((128, 128), lambda i: (0, 0)),
             pl.BlockSpec(memory_space=pltpu.SMEM),
+            pl.BlockSpec((STICKS, STICKS), lambda i: (0, 0)),
         ],
         out_shape=[
             jax.ShapeDtypeStruct((PW, 64, 128), F32),
             jax.ShapeDtypeStruct((16, 8, 128), F32),
             jax.ShapeDtypeStruct((128, 128), F32),
-            jax.ShapeDtypeStruct((2, 16), jnp.int32),
+            jax.ShapeDtypeStruct((4, 16), jnp.int32),
+            jax.ShapeDtypeStruct((STICKS, STICKS), BF16),
         ],
         scratch_shapes=[
             pltpu.VMEM((6, 16, 8, 128), F32),
@@ -739,7 +744,7 @@
     )(kinetic, coef, proj, matrix, becp)
 
 
-def collect_kernel(span_ref, key_ref, recv_ref, stick_ref, table_ref, base_ref, far_ref, out_ref,
+def collect_kernel(span_ref, key_ref, recv_ref, order_ref, table_ref, base_ref, far_ref, out_ref,
                    energy_ref, overlap_ref, values, found_re, found_im):
     total = jnp.sum(recv_ref[:, TILES * ROWS:, :], axis=0) + far_ref[...]
     band = lax.axis_index("band")
@@ -751,8 +756,7 @@
         energy_ref[ri] = total[:1, ri * 4:ri * 4 + 4]
         overlap_ref[ri] = total[:1, 8 + ri * 4:12 + ri * 4]
 
-    order, _ = rank_of(owned_row(stick_ref))
-    order = order.astype(BF16)
+    order = order_ref[...]
     lines = jnp.concatenate(
         [recv_ref[:, t * ROWS:(t + 1) * ROWS, :].reshape(512, 128) for t in range(TILES)], axis=1)
     high, low = split(lines)
@@ -766,16 +770,14 @@
     values[:, SLOT_ROWS:, :] = jnp.zeros((2, WINDOW, 256), BF16)
 
     lane_of = iota((128, 1024), 0).astype(BF16)
-    row_of = iota((WINDOW, 1024), 0)
-
-    def fetch(block, first):
+    def fetch(block, first, wide):
         row, lane = key_parts(block_row(key_ref, block))
         hit = jnp.where(lane_of == lane.astype(BF16), jnp.ones((), BF16), jnp.zeros((), BF16))
-        here = pl.ds(pl.multiple_of(first, 16), WINDOW)
+        here = pl.ds(pl.multiple_of(first, 16), wide)
         got = mm(jnp.concatenate([values[0, here, :], values[1, here, :]], axis=0), jnp.concatenate([hit, hit], axis=0))
-        mine = row_of == row - first.astype(F32)
-        return (jnp.sum(jnp.where(mine, got[:WINDOW], 0.0), axis=0, keepdims=True),
-                jnp.sum(jnp.where(mine, got[WINDOW:], 0.0), axis=0, keepdims=True))
+        mine = iota((wide, 1024), 0) == row - first.astype(F32)
+        return (jnp.sum(jnp.where(mine, got[:wide], 0.0), axis=0, keepdims=True),
+                jnp.sum(jnp.where(mine, got[wide:], 0.0), axis=0, keepdims=True))
 
     def put(block, pair, old):
         at = pl.ds(block // 2, 1)
@@ -785,22 +787,18 @@
                 piece = line[:, v * 128:(v + 1) * 128]
                 ref[half + v, at, :] = ref[half + v, at, :] + piece if old else piece
 
-    def one(step, carry):
-        for at in range(FETCH_UNROLL):
-            block = step * FETCH_UNROLL + at
-            put(block, fetch(block, span_ref[0, block]), False)
-        return carry
-
-    lax.fori_loop(0, 16 // FETCH_UNROLL, one, 0)
-
-    @pl.when(sum(span_ref[1, block] for block in range(16)) > 16)
+    for block in range(16):
+        put(block, fetch(block, span_ref[0, block], WINDOWS[block]), False)
+
+    @pl.when(sum(span_ref[3, block] for block in range(16)) > 0)
     def _():
         def rest(block, carry):
             def more(p, inner):
-                put(block, fetch(block, span_ref[0, block] + p * WINDOW), True)
+                first = span_ref[0, block] + span_ref[2, block] + p * WINDOW
+                put(block, fetch(block, first, WINDOW), True)
                 return inner
 
-            return lax.fori_loop(1, span_ref[1, block], more, carry)
+            return lax.fori_loop(0, span_ref[3, block], more, carry)
 
         lax.fori_loop(0, 16, rest, 0)
 
@@ -816,7 +814,7 @@
         out_ref[1, here, :] = base_ref[1, here, :] + imag[v] * scale
 
 
-def collect(span, key, recv, stick, base, far):
+def collect(span, key, recv, order, base, far):
     vmem = pl.BlockSpec(memory_space=pltpu.VMEM)
     return pl.pallas_call(
         collect_kernel,
@@ -835,12 +833,12 @@
         compiler_params=pltpu.CompilerParams(vmem_limit_bytes=32 << 20),
         cost_estimate=pl.CostEstimate(flops=6 * 10 ** 9, bytes_accessed=4 << 20, transcendentals=0),
         name="collect",
-    )(span, key, recv, stick, jnp.asarray(collect_table()), base, far)
+    )(span, key, recv, order, jnp.asarray(collect_table()), base, far)
 
 
 def local(wave_coef, projector, potential, grid_slot, stick_column, proj_atom, coupling):
     stick = stick_column.reshape(PW * TILES, 128)
-    sent, key, kinetic, span = spread_sticks(grid_slot.reshape(128, 128), wave_coef, projector, stick)
+    sent, key, kinetic, span, order = spread_sticks(grid_slot.reshape(128, 128), wave_coef, projector, stick)
     recv = lax.all_to_all(sent, "pw", split_axis=0, concat_axis=0, tiled=True)
     one = lax.ppermute(recv, "band", [(b, b ^ 1) for b in range(4)])
     two = lax.ppermute(recv, "band", [(b, b ^ 2) for b in range(4)])
@@ -853,7 +851,7 @@
     same_atom = proj_atom[:, None] == proj_atom[None, :]
     matrix = jnp.where(same_atom, 0.5 * (coupling + coupling.T), 0.0)
     base, far = base_part(kinetic.reshape(1, COEFS), wave_coef, projector, matrix, becp)
-    applied, energy, overlap = collect(span, key, returned, stick, base.reshape(2, 128, 128), far)
+    applied, energy, overlap = collect(span, key, returned, order, base.reshape(2, 128, 128), far)
     return applied.reshape(2, 1, COEFS), energy.transpose(0, 2, 1), overlap.transpose(0, 2, 1)
 
 

time: 120 us -> 121 us (level)
  transfers between devices with their start and end apart: 4 -> 4, of which waited for: 2 -> 2; matrix products, arithmetic and copies ran while one was open for 0% -> 0% of each run, Pallas kernels for 37% -> 38%
where the time goes in v8:
time: 121 us; the launch traced here: 120 us
  Pallas kernels  67.6 us (56%)
  blocking collectives  29.1 us (24%)
  waiting for transfers between devices  11.7 us (10%)
  starting transfers between devices  6.87 us (6%)
  local copies, waits for them, and re-layouts  3.51 us (3%)
    pallas_call x1, Pallas kernels, apply_field(): pl.pallas_call(field_kernel, in_specs=[vmem] + [pl.BlockSpec(memory_space...  40.8 us
    all_to_all x1, blocking collectives, local(): recv = lax.all_to_all(sent, 'pw', split_axis=0, concat_axis=0, tiled=True)  29.1 us
    pallas_call x1, Pallas kernels, spread_sticks(): pl.pallas_call(spread_kernel, grid=(COEFS // KC,), in_specs=[pl.BlockSpec...  12.7 us
    all_to_all x1, waiting for transfers between devices, local(): lax.all_to_all(payload, 'pw', split_axis=0, concat_axis=0, tiled=True)  10.3 us
    pallas_call x1, Pallas kernels, collect(): pl.pallas_call(collect_kernel, in_specs=[pl.BlockSpec(memory_space=pltpu....  8.33 us
    all_to_all x1, starting transfers between devices, local(): lax.all_to_all(payload, 'pw', split_axis=0, concat_axis=0, tiled=True)  5.26 us
    unnamed x29, local copies, waits for them, and re-layouts  3.51 us
    pallas_call x1, Pallas kernels, base_part(): pl.pallas_call(base_kernel, grid=(COEFS // KC,), in_specs=[pl.BlockSpec((...  3.43 us
  transfers between devices with their start and end apart: 4, of which 2 were waited for; matrix products, arithmetic and copies ran while one was open for 0% of the time, Pallas kernels for 38%

profile of v8, /device:TPU:0, one launch (start us, length us, event | category | flops | bytes accessed | tf_op | source)
XLA Modules:
  0.0 119.7 jit_solution(5464474592600196923)
XLA Ops:
  0.6 0.0 copy-start.5
  0.6 0.0 copy-start.6
  0.7 0.0 copy-start.7
  0.7 0.0 copy-start.8
  0.7 12.7 %spread_sticks.1 = (f32[32,64,128]{2,1,0:T(8,128)}, f32[16,8,128]{2,1,0:T(8,128)}, f32[128,128]{1,0:T(8,128)}, s32[4,16]{1,0:T(4,128)}, bf16[384,384]{1,0:T(8,128)(2,1)}) custom-call(s32[128,128]{1,0:T(8,128)} %bitcast.21, f32[2,128,128]{2,1,0:T(8,128)} %bitcast.18, f32[2,1,16384]{2,1,0:T(1,128)} %coef_ref.3, f32[2,64,16384]{2,1,0:T(8,128)} %proj_ref.1, ...), custom_call_target="tpu_custom_call" | custom-call | flops 6000000000 | bytes 12582912 | tf_op jit(solution)/shard_map/spread_sticks/pallas_call | solution.py:335
  13.4 0.0 copy-start.3
  13.4 29.1 %all_to_all.10.recv_ref.own_ref = f32[32,64,128]{2,1,0:T(8,128)S(1)} all-to-all(f32[32,64,128]{2,1,0:T(8,128)} %get-tuple-element.21), channel_id=1, replica_groups=mesh['pw'=32,'band'=4] {'pw'}, dimensions={0} | all-to-all | bytes 2097152 | tf_op jit(solution)/shard_map/all_to_all | solution.py:842
  42.5 1.0 collective-permute-start.1
  43.5 0.0 collective-permute-start
  43.6 40.8 %apply_field.1.worked_ref = f32[32,48,128]{2,1,0:T(8,128)S(1)} custom-call(f32[32,64,128]{2,1,0:T(8,128)S(1)} %all_to_all.10.recv_ref.own_ref, f32[8,256,256]{2,1,0:T(8,128)S(1)} %copy-done.3, bf16[768,256]{1,0:T(8,128)(2,1)S(1)} %copy-done.5, bf16[768,256]{1,0:T(8,128)(2,1)S(1)} %copy-done.6, bf16[256,768]{1,0:T(8,128)(2,1)S(1)} %copy-done.7, ...), custom_call_target="tpu_custom_call" | custom-call | flops 35000000512 | bytes 8388608 | tf_op jit(solution)/shard_map/apply_field/pallas_call | solution.py:575
  84.4 0.0 collective-permute-done.1.two_ref
  84.4 0.6 collective-permute-start.2
  85.0 0.0 collective-permute-done.one_ref
  85.0 0.9 gram_first.1
  85.8 1.4 %collective-permute-done.2.three_ref = f32[32,64,128]{2,1,0:T(8,128)S(1)} collective-permute-done((f32[32,64,128]{2,1,0:T(8,128)S(1)}, f32[32,64,128]{2,1,0:T(8,128)S(1)}, u32[]{:S(2)}, u32[]{:S(2)}) %collective-permute-start.2) | collective-permute-done | bytes 1048608 | tf_op jit(solution)/shard_map/ppermute | solution.py:847
  87.2 1.5 %gram_last.1 = (f32[32,56,128]{2,1,0:T(8,128)}, f32[4,8,128]{2,1,0:T(8,128)S(1)}) custom-call(f32[8,8,128]{2,1,0:T(8,128)S(1)} %get-tuple-element.22.total_ref, f32[16,8,128]{2,1,0:T(8,128)S(1)} %get-tuple-element.23.small_ref, f32[4,8,128]{2,1,0:T(8,128)S(1)} %get-tuple-element.24.sums_ref, f32[32,64,128]{2,1,0:T(8,128)S(1)} %all_to_all.10.recv_ref.own_ref, ...), custom_call_target="tpu_custom_call" | custom-call | flops 10000000 | bytes 4194304 | tf_op jit(solution)/shard_map/gram_last/pallas_call | solution.py:686
  88.7 5.3 %all-to-all-start.1 = ((f32[32,56,128]{2,1,0:T(8,128)}), f32[32,56,128]{2,1,0:T(8,128)S(1)}, u32[]{:S(2)}, u32[]{:S(2)}) async-start(f32[32,56,128]{2,1,0:T(8,128)} %get-tuple-element.26), calls=%async_computation.1 | async-start | bytes 1835008 | tf_op jit(solution)/shard_map/all_to_all | solution.py:849
  94.0 0.1 copy.16
  94.1 0.1 fusion.1.matrix_ref
  94.2 0.0 copy-start
  94.2 3.4 %copy-done = f32[2,64,16384]{2,1,0:T(8,128)S(1)} copy-done((f32[2,64,16384]{2,1,0:T(8,128)S(1)}, f32[2,64,16384]{2,1,0:T(8,128)}, u32[]{:S(2)}) %copy-start) | copy-done | bytes 8388632
  97.6 3.4 %base_part.1 = (f32[2,1,16384]{2,1,0:T(1,128)S(1)}, f32[8,128]{1,0:T(8,128)S(1)}) custom-call(f32[1,16384]{1,0:T(1,128)S(1)} %bitcast.19, f32[2,1,16384]{2,1,0:T(1,128)S(1)} %copy-done.1, f32[2,64,16384]{2,1,0:T(8,128)S(1)} %copy-done, f32[64,64]{1,0:T(8,128)S(1)} %fusion.1.matrix_ref, f32[4,8,128]{2,1,0:T(8,128)S(1)} %get-tuple-element.29.becp_ref), custom_call_target="tpu_custom_call" | custom-call | flops 10000000 | bytes 10485760 | tf_op jit(solution)/shard_map/base_part/pallas_call | solution.py:728
  101.0 10.3 %all-to-all-done.1.recv_ref = f32[32,56,128]{2,1,0:T(8,128)S(1)} async-done(((f32[32,56,128]{2,1,0:T(8,128)}), f32[32,56,128]{2,1,0:T(8,128)S(1)}, u32[]{:S(2)}, u32[]{:S(2)}) %all-to-all-start.1) | async-done | bytes 917536 | tf_op jit(solution)/shard_map/all_to_all | solution.py:849
  111.3 8.3 %collect.1 = (f32[2,128,128]{2,1,0:T(8,128)}, f32[2,1,4]{2,1,0:T(1,128)}, f32[2,1,4]{2,1,0:T(1,128)}) custom-call(s32[4,16]{1,0:T(4,128)S(1)} %copy-done.11, f32[16,8,128]{2,1,0:T(8,128)S(1)} %copy-done.10, f32[32,56,128]{2,1,0:T(8,128)S(1)} %all-to-all-done.1.recv_ref, bf16[384,384]{1,0:T(8,128)(2,1)S(1)} %copy-done.9, bf16[512,1536]{1,0:T(8,128)(2,1)S(1)} %copy-done.4, ...), custom_call_target="tpu_custom_call" | custom-call | flops 6000000000 | bytes 4194304 | tf_op jit(solution)/shard_map/collect/pallas_call | solution.py:819
  (21 shorter events, 0.0 us)
Async XLA Ops:
  0.6 42.9 %copy-start.5 = (bf16[768,256]{1,0:T(8,128)(2,1)S(1)}, bf16[768,256]{1,0:T(8,128)(2,1)}, u32[]{:S(2)}) copy-start(bf16[768,256]{1,0:T(8,128)(2,1)} %constant.17.clone.y_in_hbm) | copy-start | bytes 1179652
  0.6 42.9 %copy-start.6 = (bf16[768,256]{1,0:T(8,128)(2,1)S(1)}, bf16[768,256]{1,0:T(8,128)(2,1)}, u32[]{:S(2)}) copy-start(bf16[768,256]{1,0:T(8,128)(2,1)} %constant.18.clone.y_out_hbm) | copy-start | bytes 1179652
  0.7 42.9 %copy-start.7 = (bf16[256,768]{1,0:T(8,128)(2,1)S(1)}, bf16[256,768]{1,0:T(8,128)(2,1)}, u32[]{:S(2)}) copy-start(bf16[256,768]{1,0:T(8,128)(2,1)} %constant.19.clone.x_in_hbm) | copy-start | bytes 1179652
  0.7 42.9 %copy-start.8 = (bf16[256,768]{1,0:T(8,128)(2,1)S(1)}, bf16[256,768]{1,0:T(8,128)(2,1)}, u32[]{:S(2)}) copy-start(bf16[256,768]{1,0:T(8,128)(2,1)} %constant.20.clone.x_out_hbm) | copy-start | bytes 1179652
  13.4 30.2 %copy-start.3 = (f32[8,256,256]{2,1,0:T(8,128)S(1)}, f32[8,256,256]{2,1,0:T(8,128)}, u32[]{:S(2)}) copy-start(f32[8,256,256]{2,1,0:T(8,128)} %field_hbm.1) | copy-start | bytes 6291460
  42.5 41.9 %collective-permute-start.1 = (f32[32,64,128]{2,1,0:T(8,128)S(1)}, f32[32,64,128]{2,1,0:T(8,128)S(1)}, u32[]{:S(2)}, u32[]{:S(2)}) collective-permute-start(f32[32,64,128]{2,1,0:T(8,128)S(1)} %all_to_all.10.recv_ref.own_ref), channel_id=1, source_target_pairs={{0,2},{1,3},{2,0},{3,1},{4,6},{5,7},{6,4},{7,5},{8,10},{9,11},{10,... | collective-permute-start | bytes 3145736 | tf_op jit(solution)/shard_map/ppermute | solution.py:844
  43.5 41.4 %collective-permute-start = (f32[32,64,128]{2,1,0:T(8,128)S(1)}, f32[32,64,128]{2,1,0:T(8,128)S(1)}, u32[]{:S(2)}, u32[]{:S(2)}) collective-permute-start(f32[32,64,128]{2,1,0:T(8,128)S(1)} %all_to_all.10.recv_ref.own_ref), channel_id=1, source_target_pairs={{0,1},{1,0},{2,3},{3,2},{4,5},{5,4},{6,7},{7,6},{8,9},{9,8},{10,11... | collective-permute-start | bytes 3145736 | tf_op jit(solution)/shard_map/ppermute | solution.py:843
  84.4 2.9 %collective-permute-start.2 = (f32[32,64,128]{2,1,0:T(8,128)S(1)}, f32[32,64,128]{2,1,0:T(8,128)S(1)}, u32[]{:S(2)}, u32[]{:S(2)}) collective-permute-start(f32[32,64,128]{2,1,0:T(8,128)S(1)} %collective-permute-done.1.two_ref), channel_id=1, source_target_pairs={{0,1},{1,0},{2,3},{3,2},{4,5},{5,4},{6,7},{7,6},{8,9},{9,8},{10,11... | collective-permute-start | bytes 3145736 | tf_op jit(solution)/shard_map/ppermute | solution.py:847
  87.2 6.8 %copy-start.12 = (f32[64,64]{1,0:T(8,128)S(1)}, f32[64,64]{1,0:T(8,128)}, u32[]{:S(2)}) copy-start(f32[64,64]{1,0:T(8,128)} %param.19) | copy-start | bytes 49156
  87.2 6.9 %copy-start.13 = (s32[64]{0:T(128)S(1)}, s32[64]{0:T(128)}, u32[]{:S(2)}) copy-start(s32[64]{0:T(128)} %param.18) | copy-start | bytes 772
  87.2 6.9 %copy-start.1 = (f32[2,1,16384]{2,1,0:T(1,128)S(1)}, f32[2,1,16384]{2,1,0:T(1,128)}, u32[]{:S(2)}) copy-start(f32[2,1,16384]{2,1,0:T(1,128)} %coef_ref.3) | copy-start | bytes 393220
  87.2 6.9 %copy-start.2 = (f32[128,128]{1,0:T(8,128)S(1)}, f32[128,128]{1,0:T(8,128)}, u32[]{:S(2)}) copy-start(f32[128,128]{1,0:T(8,128)} %get-tuple-element.28) | copy-start | bytes 196612
  88.7 22.6 %all-to-all-start.1 = ((f32[32,56,128]{2,1,0:T(8,128)}), f32[32,56,128]{2,1,0:T(8,128)S(1)}, u32[]{:S(2)}, u32[]{:S(2)}) async-start(f32[32,56,128]{2,1,0:T(8,128)} %get-tuple-element.26), calls=%async_computation.1 | async-start | bytes 1835008 | tf_op jit(solution)/shard_map/all_to_all | solution.py:849
  94.2 3.4 %copy-start = (f32[2,64,16384]{2,1,0:T(8,128)S(1)}, f32[2,64,16384]{2,1,0:T(8,128)}, u32[]{:S(2)}) copy-start(f32[2,64,16384]{2,1,0:T(8,128)} %proj_ref.1) | copy-start | bytes 25165828
  97.6 13.7 %copy-start.4 = (bf16[512,1536]{1,0:T(8,128)(2,1)S(1)}, bf16[512,1536]{1,0:T(8,128)(2,1)}, u32[]{:S(2)}) copy-start(bf16[512,1536]{1,0:T(8,128)(2,1)} %constant.21.clone.table_ref) | copy-start | bytes 4718596
  97.6 13.7 %copy-start.9 = (bf16[384,384]{1,0:T(8,128)(2,1)S(1)}, bf16[384,384]{1,0:T(8,128)(2,1)}, u32[]{:S(2)}) copy-start(bf16[384,384]{1,0:T(8,128)(2,1)} %get-tuple-element.27.order_ref) | copy-start | bytes 884740
  97.6 13.7 %copy-start.10 = (f32[16,8,128]{2,1,0:T(8,128)S(1)}, f32[16,8,128]{2,1,0:T(8,128)}, u32[]{:S(2)}) copy-start(f32[16,8,128]{2,1,0:T(8,128)} %get-tuple-element.20.key_ref) | copy-start | bytes 196612
  97.6 13.7 %copy-start.11 = (s32[4,16]{1,0:T(4,128)S(1)}, s32[4,16]{1,0:T(4,128)}, u32[]{:S(2)}) copy-start(s32[4,16]{1,0:T(4,128)} %get-tuple-element.19.span_ref) | copy-start | bytes 772
